TPU v7x, 1024 devices: a whole 8x8x8 slice. The times are simulated.
1024 devices in a mesh: rep: 16 (over z, x_lo), fsdp: 64 (over y, x_hi, core).
Axes of the slice: x: 8 (x_hi: 4, x_lo: 2; x = x_hi * 2 + x_lo), y: 8, z: 8, core: 2. Of those that a mesh axis runs over, the one named last changes fastest.
Arguments:
- tokens_in: bfloat16 [16, 8192, 8192], P('rep', 'fsdp'), may hold values from -16 to 16
- norm_gain: bfloat16 [16, 8192], P('rep', 'fsdp'), may hold values from 0.099609375 to 1.8984375
- value_weight: bfloat16 [16, 8192, 128], P('rep', 'fsdp'), may hold values from -0.0625 to 0.0625
- value_cotangent: bfloat16 [16, 8192, 128], P('rep', 'fsdp'), may hold values from -6 to 6
- step_count: int32 [], replicated, may hold values from 1 to 8
- m_weight: float32 [16, 8192, 128], P('rep', 'fsdp'), may hold values from -0.15625 to 0.15625
- v_weight: float32 [16, 8192, 128], P('rep', 'fsdp'), may hold values from 3.6621095e-05 to 0.00036621094
- m_gain: float32 [16, 8192], P('rep', 'fsdp'), may hold values from -0.01953125 to 0.01953125
- v_gain: float32 [16, 8192], P('rep', 'fsdp'), may hold values from 5.722046e-07 to 5.722046e-06
- frag_local: float32 [16, 8192, 1024], P('rep', 'fsdp'), may hold values from -6 to 6
- frag_global: float32 [8192, 1024], P('fsdp'), may hold values from -6 to 6
- frag_moment: float32 [8192, 1024], P('fsdp'), may hold values from -4 to 4
Outputs:
- values: bfloat16 [16, 8192, 128], P('rep', 'fsdp')
- weight_step: float32 [16, 8192, 128], P('rep', 'fsdp')
- gain_step: float32 [16, 8192], P('rep', 'fsdp')
- new_global: float32 [8192, 1024], P('fsdp')
- new_moment: float32 [8192, 1024], P('fsdp')
All inputs are finite; a program needn't handle non-finite values.
Results may differ from a plain program's by a relative error of at most 0.015.
Values may be sent and summed in bfloat16 or wider, within the bound.
No kernel may reach another device: no remote copies, remote signals or barrier semaphores. Data moves between devices by JAX's collectives and lax.ppermute only.
A program may use at most 32 MiB of HBM per device.

v0:
```python
import jax
import jax.numpy as jnp
from jax import lax
from jax.sharding import PartitionSpec as P


def normalize(tokens):
    floats = tokens.astype(jnp.float32)
    inverse_rms = lax.rsqrt(jnp.mean(floats * floats, axis=-1, keepdims=True) + 1e-05)
    return (floats * inverse_rms).astype(jnp.bfloat16)


def adam_direction(gradient, first_moment, second_moment, steps):
    first_new = 0.9 * first_moment + 0.1 * gradient
    second_new = 0.95 * second_moment + 0.05 * gradient * gradient
    first_fix = 1.0 - jnp.power(jnp.float32(0.9), steps)
    second_fix = 1.0 - jnp.power(jnp.float32(0.95), steps)
    return first_new / first_fix / (jnp.sqrt(second_new / second_fix) + 1e-08)


def outer_update(global_params, moment, local_mean):
    delta = global_params - local_mean
    moment_new = 0.9 * moment + delta
    return (global_params - 0.7 * (delta + 0.9 * moment_new), moment_new)


def local(
    tokens_in,
    norm_gain,
    value_weight,
    value_cotangent,
    step_count,
    m_weight,
    v_weight,
    m_gain,
    v_gain,
    frag_local,
    frag_global,
    frag_moment,
):
    tokens = tokens_in[0]
    gain_rows = norm_gain[0]
    weight_rows = value_weight[0]
    cotangent = value_cotangent[0]
    full_weight, full_gain = (
        lax.all_gather(weight_rows, "fsdp", axis=0, tiled=True),
        lax.all_gather(gain_rows, "fsdp", axis=0, tiled=True),
    )
    normed = normalize(tokens)
    hidden = (normed.astype(jnp.float32) * full_gain.astype(jnp.float32)).astype(jnp.bfloat16)
    values = jnp.dot(hidden, full_weight, preferred_element_type=jnp.float32).astype(jnp.bfloat16)
    token_total = tokens.shape[0] * lax.axis_size("fsdp")
    input_grad = lax.dot_general(
        cotangent, full_weight, (((1,), (1,)), ((), ())), preferred_element_type=jnp.float32
    )
    weight_term = lax.dot_general(
        hidden, cotangent, (((0,), (0,)), ((), ())), preferred_element_type=jnp.float32
    )
    gain_term = jnp.sum(input_grad * normed.astype(jnp.float32), axis=0)
    weight_sum, gain_sum = (
        lax.psum_scatter(weight_term, "fsdp", scatter_dimension=0, tiled=True),
        lax.psum_scatter(gain_term, "fsdp", scatter_dimension=0, tiled=True),
    )
    steps = step_count.astype(jnp.float32)
    weight_step = adam_direction(weight_sum / token_total, m_weight[0], v_weight[0], steps)
    gain_step = adam_direction(gain_sum / token_total, m_gain[0], v_gain[0], steps)
    own_local = frag_local[0]
    replicas = lax.axis_size("rep")
    local_sum = lax.psum(own_local.astype(jnp.bfloat16), "rep").astype(jnp.float32)
    new_global, new_moment = outer_update(frag_global, frag_moment, local_sum / replicas)
    return (values[None], weight_step[None], gain_step[None], new_global, new_moment)


def solution(mesh):
    in_specs = (
        P("rep", "fsdp", None),
        P("rep", "fsdp"),
        P("rep", "fsdp", None),
        P("rep", "fsdp", None),
        P(),
        P("rep", "fsdp", None),
        P("rep", "fsdp", None),
        P("rep", "fsdp"),
        P("rep", "fsdp"),
        P("rep", "fsdp", None),
        P("fsdp", None),
        P("fsdp", None),
    )
    out_specs = (
        P("rep", "fsdp", None),
        P("rep", "fsdp", None),
        P("rep", "fsdp"),
        P("fsdp", None),
        P("fsdp", None),
    )
    return jax.shard_map(local, mesh=mesh, in_specs=in_specs, out_specs=out_specs, check_vma=False)
```

profile of v0, /device:TPU:2, one launch (start us, length us, event | category | flops | bytes accessed | tf_op | source)
XLA Modules:
  0.0 469.3 jit_solution(17865359689719408479)
XLA Ops:
  8.0 0.0 copy-start
  8.0 0.0 copy-start.1
  8.0 0.0 all-reduce.3.cloned.1.call-start
  8.1 1.9 convert_bitcast_fusion.1
  10.0 0.0 all-reduce.3.cloned.1.call-update
  10.0 0.0 all-gather.4.cloned.1.call-start
  10.1 0.5 all-gather.4.cloned.1.call-update
  10.6 0.0 reduce-scatter.2.cloned.1.call-start
  10.6 82.5 %all-gather = bf16[1,8192]{1,0:T(2,128)(2,1)S(1)} all-gather(bf16[1,128]{1,0:T(2,128)(2,1)} %param.13), channel_id=2, replica_groups=mesh['rep'=16,'fsdp'=64] {'fsdp'}, dimensions={1}, use_global_device_ids=true | all-gather | bytes 16640 | tf_op jit(solution)/shard_map/all_gather | solution.py:47
  93.1 2.1 fusion.3
  95.2 0.0 copy-done
  95.3 0.0 copy-done.1
  95.3 2.8 fusion.7
  98.0 0.0 copy-start.2
  98.0 0.0 copy-start.3
  98.0 0.0 reduce-scatter.2.cloned.1.call-update
  98.1 0.0 copy-start.6
  98.1 0.0 copy-start.7
  98.9 1.3 dynamic-slice
  100.8 74.8 %all-reduce.3.cloned.1.call-done = bf16[128,1024]{1,0:T(8,128)(2,1)} async-done(((bf16[128,1024]{1,0:T(8,128)(2,1)}), bf16[128,1024]{1,0:T(8,128)(2,1)}) %all-reduce.3.cloned.1.call-update) | async-done | bytes 262160 | tf_op jit(solution)/shard_map/psum | solution.py:69
  175.6 0.0 copy-done.2
  175.6 0.0 copy-done.3
  175.6 2.1 multiply_subtract_fusion
  177.7 0.0 copy-start.4
  177.7 0.0 copy-start.5
  177.7 0.0 all-gather.4.cloned.1.call-done
  177.7 2.4 fusion.17
  180.1 276.6 %all-reduce = f32[8192]{0:T(1024)S(1)} all-reduce(f32[8192]{0:T(1024)S(1)} %fusion.17), channel_id=5, replica_groups=mesh['rep'=16,'fsdp'=64] {'fsdp'}, use_global_device_ids=true, to_apply=%region_3.0.clone | all-reduce | flops 8192 | bytes 65536
  456.7 0.0 copy-done.6
  456.7 0.0 copy-done.7
  456.7 0.6 fusion.41
  457.3 3.0 fusion.25
  460.3 0.0 reduce-scatter.2.cloned.1.call-done
  460.3 0.0 copy-done.4
  460.3 0.0 copy-done.5
  460.3 1.5 fusion.36
  (2 shorter events, 0.0 us)
Async XLA Ops:
  8.0 87.2 %copy-start = (bf16[1,128,128]{2,1,0:T(8,128)(2,1)S(1)}, bf16[1,128,128]{2,1,0:T(8,128)(2,1)}, u32[]{:S(2)}) copy-start(bf16[1,128,128]{2,1,0:T(8,128)(2,1)} %param.15) | copy-start | bytes 98308
  8.0 87.2 %copy-start.1 = (bf16[1,128,8192]{2,1,0:T(8,128)(2,1)S(1)}, bf16[1,128,8192]{2,1,0:T(8,128)(2,1)}, u32[]{:S(2)}) copy-start(bf16[1,128,8192]{2,1,0:T(8,128)(2,1)} %param.12) | copy-start | bytes 6291460
  8.0 167.6 %all-reduce.3.cloned.1.call-start = ((), (), s32[]{:S(2)}) async-start(), calls=%async_computation.2 | async-start | bytes 524288 | tf_op jit(solution)/shard_map/psum | solution.py:69
  10.0 167.7 %all-gather.4.cloned.1.call-start = ((), (), s32[]{:S(2)}) async-start(), calls=%async_computation.3 | async-start | bytes 2129920 | tf_op jit(solution)/shard_map/all_gather | solution.py:46
  10.6 449.7 %reduce-scatter.2.cloned.1.call-start = ((), (), s32[]{:S(2)}) async-start(), calls=%async_computation.1 | async-start | bytes 4259840 | tf_op jit(solution)/shard_map/reduce_scatter | solution.py:61
  98.0 77.6 %copy-start.2 = (f32[128,1024]{1,0:T(8,128)S(1)}, f32[128,1024]{1,0:T(8,128)}, u32[]{:S(2)}) copy-start(f32[128,1024]{1,0:T(8,128)} %param.22) | copy-start | bytes 1572868
  98.0 77.6 %copy-start.3 = (f32[128,1024]{1,0:T(8,128)S(1)}, f32[128,1024]{1,0:T(8,128)}, u32[]{:S(2)}) copy-start(f32[128,1024]{1,0:T(8,128)} %param.23) | copy-start | bytes 1572868
  98.1 358.6 %copy-start.6 = (f32[1,128]{1,0:T(1,128)S(1)}, f32[1,128]{1,0:T(1,128)}, u32[]{:S(2)}) copy-start(f32[1,128]{1,0:T(1,128)} %param.20) | copy-start | bytes 1540
  98.1 358.6 %copy-start.7 = (f32[1,128]{1,0:T(1,128)S(1)}, f32[1,128]{1,0:T(1,128)}, u32[]{:S(2)}) copy-start(f32[1,128]{1,0:T(1,128)} %param.19) | copy-start | bytes 1540
  177.7 282.6 %copy-start.4 = (f32[1,128,128]{2,1,0:T(8,128)S(1)}, f32[1,128,128]{2,1,0:T(8,128)}, u32[]{:S(2)}) copy-start(f32[1,128,128]{2,1,0:T(8,128)} %param.18) | copy-start | bytes 196612
  177.7 282.6 %copy-start.5 = (f32[1,128,128]{2,1,0:T(8,128)S(1)}, f32[1,128,128]{2,1,0:T(8,128)}, u32[]{:S(2)}) copy-start(f32[1,128,128]{2,1,0:T(8,128)} %param.17) | copy-start | bytes 196612
Sparse Core Ops, SparseCore 0:
  13.3 162.2 all-reduce.2
Sparse Core Ops, SparseCore 1:
  15.0 100.1 all-gather.3
  120.9 161.3 reduce-scatter.1
where the time goes:
time: 470 us; the launch traced here: 469 us
  blocking collectives  359 us (76%)
  waiting for transfers between devices  75.3 us (16%)
  between operations  17 us (4%)
  other arithmetic  8.27 us (2%)
  matrix products  8.19 us (2%)
    unnamed x1, blocking collectives  277 us
    all_gather x1, blocking collectives, local(): lax.all_gather(gain_rows, 'fsdp', axis=0, tiled=True)  82.5 us
    psum x1, waiting for transfers between devices, local(): lax.psum(own_local.astype(jnp.bfloat16), 'rep').astype(jnp.float32)  74.8 us
  transfers between devices with their start and end apart: 3, of which 1 were waited for; matrix products, arithmetic and copies ran while one was open for 3% of the time, Pallas kernels for 0%

commit v1 on v0

v1 whole, which is shorter than its diff:
```python
import jax
import jax.numpy as jnp
from jax import lax
from jax.sharding import Mesh
from jax.sharding import PartitionSpec as P

CORES = 2
SWAP = [(0, 1), (1, 0)]


def adam_direction(gradient, first_moment, second_moment, steps):
    first_new = 0.9 * first_moment + 0.1 * gradient
    second_new = 0.95 * second_moment + 0.05 * gradient * gradient
    first_fix = 1.0 - jnp.power(jnp.float32(0.9), steps)
    second_fix = 1.0 - jnp.power(jnp.float32(0.95), steps)
    return first_new / first_fix / (jnp.sqrt(second_new / second_fix) + 1e-08)


def outer_update(global_params, moment, local_mean):
    delta = global_params - local_mean
    moment_new = 0.9 * moment + delta
    return (global_params - 0.7 * (delta + 0.9 * moment_new), moment_new)


def exchange(blocks, axis):
    return lax.all_to_all(blocks, axis, 0, 0, tiled=True)


def spread(block, axis):
    return exchange(jnp.broadcast_to(block[None], (lax.axis_size(axis),) + block.shape), axis)


def local(
    tokens_in,
    norm_gain,
    value_weight,
    value_cotangent,
    step_count,
    m_weight,
    v_weight,
    m_gain,
    v_gain,
    frag_local,
    frag_global,
    frag_moment,
):
    tokens = tokens_in[0]
    gain = norm_gain[0].astype(jnp.float32)
    weight = value_weight[0].astype(jnp.float32)
    cotangent = value_cotangent[0].astype(jnp.float32)
    rows, width = tokens.shape
    head = weight.shape[1]
    chips = lax.axis_size("chip")
    token_total = rows * chips * CORES
    first_core = lax.axis_index("core") == 0

    scaled_weight = (weight * gain[:, None]).astype(jnp.bfloat16)
    own_weight = spread(scaled_weight, "chip")
    other_weight = lax.ppermute(own_weight, "core", SWAP)

    floats = tokens.astype(jnp.float32)
    inverse_rms = lax.rsqrt(jnp.mean(floats * floats, axis=-1, keepdims=True) + 1e-05)
    scaled_cotangent = (cotangent * inverse_rms).astype(jnp.bfloat16)
    parts = tokens.reshape(rows, chips, CORES, -1)
    own_tokens = jnp.where(first_core, parts[:, :, 0], parts[:, :, 1]).reshape(rows, -1)
    other_tokens = jnp.where(first_core, parts[:, :, 1], parts[:, :, 0]).reshape(rows, -1)

    def gradient_term(some_tokens):
        return lax.dot_general(
            some_tokens, scaled_cotangent, (((0,), (0,)), ((), ())), preferred_element_type=jnp.float32
        )

    arrived = lax.ppermute(gradient_term(other_tokens).astype(jnp.bfloat16), "core", SWAP)
    chip_term = (gradient_term(own_tokens) + arrived.astype(jnp.float32)).astype(jnp.bfloat16)
    terms = exchange(chip_term.reshape(chips, -1, head), "chip")
    gradient = jnp.sum(terms.astype(jnp.float32), axis=0) / token_total

    replicas = lax.axis_size("rep")
    frag = frag_local[0].astype(jnp.bfloat16)
    frag_terms = exchange(frag.reshape(replicas, -1, frag.shape[1]), "rep")
    frag_sum = jnp.sum(frag_terms.astype(jnp.float32), axis=0).astype(jnp.bfloat16)
    local_sum = spread(frag_sum, "rep").reshape(frag.shape).astype(jnp.float32)
    new_global, new_moment = outer_update(frag_global, frag_moment, local_sum / replicas)

    def product(some_tokens, some_weight):
        return jnp.dot(some_tokens, some_weight.reshape(-1, head), preferred_element_type=jnp.float32)

    summed = product(own_tokens, own_weight) + product(other_tokens, other_weight)
    values = (summed * inverse_rms).astype(jnp.bfloat16)

    steps = step_count.astype(jnp.float32)
    weight_step = adam_direction(gradient * gain[:, None], m_weight[0], v_weight[0], steps)
    gain_step = adam_direction(jnp.sum(weight * gradient, axis=1), m_gain[0], v_gain[0], steps)
    return (values[None], weight_step[None], gain_step[None], new_global, new_moment)


def solution(mesh):
    split = Mesh(mesh.devices.reshape(mesh.shape["rep"], -1, CORES), ("rep", "chip", "core"))
    fsdp = ("chip", "core")
    in_specs = (
        P("rep", fsdp, None),
        P("rep", fsdp),
        P("rep", fsdp, None),
        P("rep", fsdp, None),
        P(),
        P("rep", fsdp, None),
        P("rep", fsdp, None),
        P("rep", fsdp),
        P("rep", fsdp),
        P("rep", fsdp, None),
        P(fsdp, None),
        P(fsdp, None),
    )
    out_specs = (
        P("rep", fsdp, None),
        P("rep", fsdp, None),
        P("rep", fsdp),
        P(fsdp, None),
        P(fsdp, None),
    )
    return jax.shard_map(local, mesh=split, in_specs=in_specs, out_specs=out_specs, check_vma=False)
```

time: 470 us -> 132 us (0.28)
  blocking collectives: 359 us -> 28.4 us
  starting transfers between devices: 0.12 us -> 26.1 us
  waiting for transfers between devices: 75.3 us -> 57.3 us
  between operations: 17 us -> 1.53 us
    unnamed x1 -> x0, blocking collectives: 277 us -> none
    all_gather x1 -> x0, blocking collectives: 82.5 us -> none  [local(): lax.all_gather(gain_rows, 'fsdp', axis=0, tiled=True)]
    psum x1 -> x0, waiting for transfers between devices: 74.8 us -> none  [local(): lax.psum(own_local.astype(jnp.bfloat16), 'rep').astype(jnp.float32)]
    all_to_all x0 -> x3, waiting for transfers between devices: none -> 54.6 us  [exchange(): return lax.all_to_all(blocks, axis, 0, 0, tiled=True)]
    all_to_all x0 -> x1, blocking collectives: none -> 28.4 us  [exchange(): return lax.all_to_all(blocks, axis, 0, 0, tiled=True)]
    all_to_all x0 -> x3, starting transfers between devices: none -> 22.3 us  [exchange(): return lax.all_to_all(blocks, axis, 0, 0, tiled=True)]
  transfers between devices with their start and end apart: 3 -> 5, of which waited for: 1 -> 4; matrix products, arithmetic and copies ran while one was open for 3% -> 9% of each run, Pallas kernels for 0% -> 0%
where the time goes in v1:
time: 132 us; the launch traced here: 131 us
  waiting for transfers between devices  57.3 us (43%)
  blocking collectives  28.4 us (22%)
  starting transfers between devices  26.1 us (20%)
  other arithmetic  8.66 us (7%)
  matrix products  4.74 us (4%)
  local copies, waits for them, and re-layouts  4.48 us (3%)
  between operations  1.53 us (1%)
    all_to_all x3, waiting for transfers between devices, exchange(): return lax.all_to_all(blocks, axis, 0, 0, tiled=True)  54.6 us
    all_to_all x1, blocking collectives, exchange(): return lax.all_to_all(blocks, axis, 0, 0, tiled=True)  28.4 us
    all_to_all x3, starting transfers between devices, exchange(): return lax.all_to_all(blocks, axis, 0, 0, tiled=True)  22.3 us
    dot_general x2, matrix products, product(): jnp.dot(some_tokens, some_weight.reshape(-1, head), preferred_element_typ...  2.8 us
  transfers between devices with their start and end apart: 5, of which 4 were waited for; matrix products, arithmetic and copies ran while one was open for 9% of the time, Pallas kernels for 0%

profile of v1, /device:TPU:2, one launch (start us, length us, event | category | flops | bytes accessed | tf_op | source)
XLA Modules:
  0.0 131.2 jit_solution(7897063375707283973)
XLA Ops:
  0.6 0.0 copy-start.7
  0.6 0.0 copy-start.2
  0.7 0.0 copy-start
  0.7 1.2 convert_bitcast_fusion
  1.9 28.4 %all_to_all.20 = bf16[16,8,1024]{2,1,0:T(8,128)(2,1)S(1)} all-to-all(bf16[16,8,1024]{2,1,0:T(8,128)(2,1)S(1)} %convert_bitcast_fusion), channel_id=1, replica_groups=mesh['rep'=16,'chip'=32,'core'=2] {'rep'}, dimensions={0} | all-to-all | bytes 524288 | tf_op jit(solution)/shard_map/all_to_all | solution.py:26
  30.3 0.7 broadcast_in_dim.11
  31.1 4.5 %all-to-all-start.3 = ((bf16[16,8,1024]{2,1,0:T(8,128)(2,1)}), bf16[16,8,1024]{2,1,0:T(8,128)(2,1)S(1)}, u32[]{:S(2)}, u32[]{:S(2)}) async-start(bf16[16,8,1024]{2,1,0:T(8,128)(2,1)} %broadcast_in_dim.11), calls=%async_computation.3 | async-start | bytes 524288 | tf_op jit(solution)/shard_map/all_to_all | solution.py:26
  35.6 0.0 copy-done.7
  35.6 0.0 copy-done.2
  35.6 0.1 fusion.16
  35.7 0.0 copy-done
  35.7 0.5 multiply_reduce_fusion
  36.2 9.7 %all-to-all-done.3 = bf16[16,8,1024]{2,1,0:T(8,128)(2,1)S(1)} async-done(((bf16[16,8,1024]{2,1,0:T(8,128)(2,1)}), bf16[16,8,1024]{2,1,0:T(8,128)(2,1)S(1)}, u32[]{:S(2)}, u32[]{:S(2)}) %all-to-all-start.3) | async-done | bytes 262176 | tf_op jit(solution)/shard_map/all_to_all | solution.py:26
  45.9 1.2 broadcast_in_dim.9
  47.1 12.0 %all-to-all-start = ((bf16[32,128,128]{2,1,0:T(8,128)(2,1)}), bf16[32,128,128]{2,1,0:T(8,128)(2,1)S(1)}, u32[]{:S(2)}, u32[]{:S(2)}) async-start(bf16[32,128,128]{2,1,0:T(8,128)(2,1)} %broadcast_in_dim.9), calls=%async_computation | async-start | bytes 2097152 | tf_op jit(solution)/shard_map/all_to_all | solution.py:26
  59.1 2.5 %copy.21 = bf16[1,128,8192]{1,2,0:T(8,128)(2,1)} copy(bf16[1,128,8192]{2,1,0:T(8,128)(2,1)S(1)} %copy-done) | data formatting | bytes 4194304 | tf_op args[0]
  61.6 0.0 copy-start.1
  61.6 1.7 %broadcast_select_fusion = (bf16[128,32,1,128]{0,3,2,1:T(8,128)(2,1)S(1)}, bf16[128,32,1,128]{0,3,2,1:T(8,128)(2,1)S(1)}) fusion(pred[]{:T(512)S(6)} %eq.3, bf16[128,32,2,128]{0,3,2,1:T(8,128)(2,1)} %bitcast.71), kind=kLoop, calls=%fused_computation.12 | loop fusion | flops 1048576 | bytes 4194305 | tf_op jit(solution)/shard_map/jit(_where)/select_n | solution.py:66
  63.3 0.0 copy-done.1
  63.3 0.5 convolution_convert_fusion
  63.8 1.9 %collective-permute-start.1 = (bf16[4096,128]{1,0:T(8,128)(2,1)S(1)}, bf16[4096,128]{1,0:T(8,128)(2,1)S(1)}, u32[]{:S(2)}, u32[]{:S(2)}) collective-permute-start(bf16[4096,128]{1,0:T(8,128)(2,1)S(1)} %convolution_convert_fusion), channel_id=1, source_target_pairs={{0,1},{1,0},{2,3},{3,2},{4,5},{5,4},{6,7},{7,6},{8,9},{9,8},{10,11... | collective-permute-start | bytes 3145736 | tf_op jit(solution)/shard_map/ppermute | solution.py:73
  65.7 2.6 %collective-permute-done.1 = bf16[4096,128]{1,0:T(8,128)(2,1)S(1)} collective-permute-done((bf16[4096,128]{1,0:T(8,128)(2,1)S(1)}, bf16[4096,128]{1,0:T(8,128)(2,1)S(1)}, u32[]{:S(2)}, u32[]{:S(2)}) %collective-permute-start.1) | collective-permute-done | bytes 1048608 | tf_op jit(solution)/shard_map/ppermute | solution.py:73
  68.3 1.5 %add_convert_fusion = bf16[4096,128]{1,0:T(8,128)(2,1)} fusion(bf16[4096,128]{1,0:T(8,128)(2,1)S(1)} %collective-permute-done.1, bf16[128,4096]{0,1:T(8,128)(2,1)S(1)} %bitcast.70, bf16[1,128,128]{2,1,0:T(8,128)(2,1)S(1)} %copy-done.1, f32[128]{0:T(128)S(1)} %add_rsqrt_fusion), kind=kOutput, calls=%fused_computation.3 | convolution fusion | flops 135839744 | bytes 3179008 | tf_op jit(solution)/shard_map/dot_general | solution.py:69
  69.8 21.1 %all-to-all-done = bf16[32,128,128]{2,1,0:T(8,128)(2,1)S(1)} async-done(((bf16[32,128,128]{2,1,0:T(8,128)(2,1)}), bf16[32,128,128]{2,1,0:T(8,128)(2,1)S(1)}, u32[]{:S(2)}, u32[]{:S(2)}) %all-to-all-start) | async-done | bytes 1048608 | tf_op jit(solution)/shard_map/all_to_all | solution.py:26
  90.9 5.8 %all-to-all-start.1 = ((bf16[32,128,128]{2,1,0:T(8,128)(2,1)}), bf16[32,128,128]{2,1,0:T(8,128)(2,1)}, u32[]{:S(2)}, u32[]{:S(2)}) async-start(bf16[32,128,128]{2,1,0:T(8,128)(2,1)} %bitcast.72), calls=%async_computation.1 | async-start | bytes 2097152 | tf_op jit(solution)/shard_map/all_to_all | solution.py:26
  97.5 1.9 %collective-permute-start = (bf16[32,128,128]{2,1,0:T(8,128)(2,1)S(1)}, bf16[32,128,128]{2,1,0:T(8,128)(2,1)}, u32[]{:S(2)}, u32[]{:S(2)}) collective-permute-start(bf16[32,128,128]{2,1,0:T(8,128)(2,1)S(1)} %all-to-all-done), channel_id=1, source_target_pairs={{0,1},{1,0},{2,3},{3,2},{4,5},{5,4},{6,7},{7,6},{8,9},{9,8},{10,11... | collective-permute-start | bytes 3145736 | tf_op jit(solution)/shard_map/ppermute | solution.py:59
  99.4 2.3 %multiply_subtract_fusion = (f32[128,1024]{1,0:T(8,128)}, f32[128,1024]{1,0:T(8,128)}) fusion(f32[128,1024]{1,0:T(8,128)} %param.22, bf16[16,8,1024]{2,1,0:T(8,128)(2,1)S(1)} %all-to-all-done.3, f32[128,1024]{1,0:T(8,128)} %param.23), kind=kLoop, calls=%fused_computation.15 | loop fusion | flops 1179648 | bytes 2359296 | tf_op jit(solution)/shard_map/sub | solution.py:22
  101.8 0.0 copy-start.5
  101.8 0.0 copy-start.6
  101.8 0.0 copy-start.3
  101.8 0.0 copy-start.4
  101.8 0.5 convolution_bitcast_fusion.1
  102.3 23.8 %all-to-all-done.1 = bf16[32,128,128]{2,1,0:T(8,128)(2,1)} async-done(((bf16[32,128,128]{2,1,0:T(8,128)(2,1)}), bf16[32,128,128]{2,1,0:T(8,128)(2,1)}, u32[]{:S(2)}, u32[]{:S(2)}) %all-to-all-start.1) | async-done | bytes 1048608 | tf_op jit(solution)/shard_map/all_to_all | solution.py:26
  126.1 1.4 %convert_reduce_fusion = f32[128,128]{1,0:T(8,128)S(1)} fusion(bf16[32,128,128]{2,1,0:T(8,128)(2,1)} %all-to-all-done.1), kind=kLoop, calls=%fused_computation.2 | loop fusion | flops 1032192 | bytes 1114112 | tf_op jit(solution)/shard_map/reduce_sum | solution.py:76
  127.5 0.1 fusion.8
  127.6 0.0 copy-done.5
  127.6 0.0 copy-done.6
  127.6 0.5 fusion.24
  128.1 0.0 copy-done.3
  128.1 0.0 copy-done.4
  128.1 0.7 fusion.14
  128.9 0.0 collective-permute-done
  128.9 2.3 %fusion.3 = bf16[1,128,128]{2,1,0:T(8,128)(2,1)} fusion(f32[128,128]{1,0:T(8,128)S(1)} %convolution_bitcast_fusion.1, bf16[32,128,128]{2,1,0:T(8,128)(2,1)} %collective-permute-done, bf16[128,32,1,128]{0,3,2,1:T(8,128)(2,1)S(1)} %get-tuple-element.7, f32[128]{0:T(128)S(1)} %add_rsqrt_fusion), kind=kOutput, calls=%fused_computation.9 | convolution fusion | flops 134266880 | bytes 2195968 | tf_op jit(solution)/shard_map/dot_general | solution.py:86
  (4 shorter events, 0.1 us)
Async XLA Ops:
  0.6 34.9 %copy-start.7 = (bf16[1,128]{1,0:T(2,128)(2,1)S(1)}, bf16[1,128]{1,0:T(2,128)(2,1)}, u32[]{:S(2)}) copy-start(bf16[1,128]{1,0:T(2,128)(2,1)} %param.13) | copy-start | bytes 772
  0.6 34.9 %copy-start.2 = (bf16[1,128,128]{2,1,0:T(8,128)(2,1)S(1)}, bf16[1,128,128]{2,1,0:T(8,128)(2,1)}, u32[]{:S(2)}) copy-start(bf16[1,128,128]{2,1,0:T(8,128)(2,1)} %param.14) | copy-start | bytes 98308
  0.7 35.0 %copy-start = (bf16[1,128,8192]{2,1,0:T(8,128)(2,1)S(1)}, bf16[1,128,8192]{2,1,0:T(8,128)(2,1)}, u32[]{:S(2)}) copy-start(bf16[1,128,8192]{2,1,0:T(8,128)(2,1)} %param.12) | copy-start | bytes 6291460
  31.1 14.8 %all-to-all-start.3 = ((bf16[16,8,1024]{2,1,0:T(8,128)(2,1)}), bf16[16,8,1024]{2,1,0:T(8,128)(2,1)S(1)}, u32[]{:S(2)}, u32[]{:S(2)}) async-start(bf16[16,8,1024]{2,1,0:T(8,128)(2,1)} %broadcast_in_dim.11), calls=%async_computation.3 | async-start | bytes 524288 | tf_op jit(solution)/shard_map/all_to_all | solution.py:26
  47.1 43.8 %all-to-all-start = ((bf16[32,128,128]{2,1,0:T(8,128)(2,1)}), bf16[32,128,128]{2,1,0:T(8,128)(2,1)S(1)}, u32[]{:S(2)}, u32[]{:S(2)}) async-start(bf16[32,128,128]{2,1,0:T(8,128)(2,1)} %broadcast_in_dim.9), calls=%async_computation | async-start | bytes 2097152 | tf_op jit(solution)/shard_map/all_to_all | solution.py:26
  61.6 1.7 %copy-start.1 = (bf16[1,128,128]{2,1,0:T(8,128)(2,1)S(1)}, bf16[1,128,128]{2,1,0:T(8,128)(2,1)}, u32[]{:S(2)}) copy-start(bf16[1,128,128]{2,1,0:T(8,128)(2,1)} %param.15) | copy-start | bytes 98308
  63.8 4.6 %collective-permute-start.1 = (bf16[4096,128]{1,0:T(8,128)(2,1)S(1)}, bf16[4096,128]{1,0:T(8,128)(2,1)S(1)}, u32[]{:S(2)}, u32[]{:S(2)}) collective-permute-start(bf16[4096,128]{1,0:T(8,128)(2,1)S(1)} %convolution_convert_fusion), channel_id=1, source_target_pairs={{0,1},{1,0},{2,3},{3,2},{4,5},{5,4},{6,7},{7,6},{8,9},{9,8},{10,11... | collective-permute-start | bytes 3145736 | tf_op jit(solution)/shard_map/ppermute | solution.py:73
  90.9 35.2 %all-to-all-start.1 = ((bf16[32,128,128]{2,1,0:T(8,128)(2,1)}), bf16[32,128,128]{2,1,0:T(8,128)(2,1)}, u32[]{:S(2)}, u32[]{:S(2)}) async-start(bf16[32,128,128]{2,1,0:T(8,128)(2,1)} %bitcast.72), calls=%async_computation.1 | async-start | bytes 2097152 | tf_op jit(solution)/shard_map/all_to_all | solution.py:26
  97.5 31.4 %collective-permute-start = (bf16[32,128,128]{2,1,0:T(8,128)(2,1)S(1)}, bf16[32,128,128]{2,1,0:T(8,128)(2,1)}, u32[]{:S(2)}, u32[]{:S(2)}) collective-permute-start(bf16[32,128,128]{2,1,0:T(8,128)(2,1)S(1)} %all-to-all-done), channel_id=1, source_target_pairs={{0,1},{1,0},{2,3},{3,2},{4,5},{5,4},{6,7},{7,6},{8,9},{9,8},{10,11... | collective-permute-start | bytes 3145736 | tf_op jit(solution)/shard_map/ppermute | solution.py:59
  101.8 25.8 %copy-start.5 = (f32[1,128]{1,0:T(1,128)S(1)}, f32[1,128]{1,0:T(1,128)}, u32[]{:S(2)}) copy-start(f32[1,128]{1,0:T(1,128)} %param.20) | copy-start | bytes 1540
  101.8 25.8 %copy-start.6 = (f32[1,128]{1,0:T(1,128)S(1)}, f32[1,128]{1,0:T(1,128)}, u32[]{:S(2)}) copy-start(f32[1,128]{1,0:T(1,128)} %param.19) | copy-start | bytes 1540
  101.8 26.4 %copy-start.3 = (f32[1,128,128]{2,1,0:T(8,128)S(1)}, f32[1,128,128]{2,1,0:T(8,128)}, u32[]{:S(2)}) copy-start(f32[1,128,128]{2,1,0:T(8,128)} %param.18) | copy-start | bytes 196612
  101.8 26.4 %copy-start.4 = (f32[1,128,128]{2,1,0:T(8,128)S(1)}, f32[1,128,128]{2,1,0:T(8,128)}, u32[]{:S(2)}) copy-start(f32[1,128,128]{2,1,0:T(8,128)} %param.17) | copy-start | bytes 196612

commit v2 on v0

v2 whole, which is shorter than its diff:
```python
import functools

import jax
import jax.numpy as jnp
from jax import lax
from jax.experimental import pallas as pl
from jax.experimental.pallas import tpu as pltpu
from jax.sharding import PartitionSpec as P

EIGHT = 8
FOUR = 4
LANES = 128


def chip_of(core, four, eight):
    if core:
        return eight * FOUR + four
    return (eight // FOUR * FOUR + four) * FOUR + eight % FOUR


def device_of(core, four, eight):
    return chip_of(core, four, eight) * 2 + core


EIGHT_GROUPS = [[device_of(core, four, eight) for eight in range(EIGHT)] for core in range(2) for four in range(FOUR)]
SWAP_CORES = [(device, device ^ 1) for device in range(2 * FOUR * EIGHT)]


def four_pairs(step):
    return [
        (device_of(core, four, eight), device_of(core, four ^ step, eight))
        for core in range(2)
        for four in range(FOUR)
        for eight in range(EIGHT)
    ]


def exchange(blocks, axis, groups=None):
    return lax.all_to_all(blocks, axis, 0, 0, axis_index_groups=groups, tiled=True)


def spread(block, count, axis, groups=None):
    return exchange(jnp.broadcast_to(block[None], (count,) + block.shape), axis, groups)


def call(kernel, *out_shapes):
    return pl.pallas_call(
        kernel,
        out_shape=out_shapes,
        compiler_params=pltpu.CompilerParams(vmem_limit_bytes=32 * 1024 * 1024),
    )


def lanes_of(block):
    return slice(block * LANES, (block + 1) * LANES)


def split_kernel(tokens_ref, cotangent_ref, keep_ref, send_ref, inverse_ref):
    device = lax.axis_index("fsdp")
    core = lax.rem(device, 2)
    chip = lax.div(device, 2)
    row, column = lax.div(chip, FOUR), lax.rem(chip, FOUR)
    fours = (lax.rem(row, FOUR), column)
    rows, width = tokens_ref.shape
    total = jnp.zeros((rows, LANES), jnp.float32)
    for block in range(width // LANES):
        floats = tokens_ref[:, lanes_of(block)].astype(jnp.float32)
        total += floats * floats
    inverse = lax.rsqrt(jnp.sum(total, axis=1, keepdims=True) / width + 1e-05)
    inverse_ref[...] = jnp.broadcast_to(inverse, (rows, LANES))
    send_ref[:, lanes_of(FOUR * EIGHT)] = (cotangent_ref[...].astype(jnp.float32) * inverse).astype(jnp.bfloat16)
    for step in range(FOUR):
        for eight in range(EIGHT):
            chips = [chip_of(kind, fours[kind] ^ step, eight) for kind in range(2)]
            for target, kind in ((keep_ref, core), (send_ref, 1 - core)):
                source = jnp.where(kind == 0, chips[0], chips[1]) * 2 + kind
                start = pl.multiple_of(source * LANES, LANES)
                target[:, lanes_of(step * EIGHT + eight)] = tokens_ref[:, pl.ds(start, LANES)]


def gradient_kernel(keep_ref, arrived_ref, send_ref, own_ref, *out_refs):
    last = lanes_of(FOUR * EIGHT)
    columns = EIGHT * LANES
    cotangents = jnp.concatenate([send_ref[:, last], arrived_ref[:, last]], axis=0)
    for step, out_ref in enumerate((own_ref,) + out_refs):
        part = slice(step * columns, (step + 1) * columns)
        both = jnp.concatenate([keep_ref[:, part], arrived_ref[:, part]], axis=0)
        term = lax.dot_general(cotangents, both, (((0,), (0,)), ((), ())), preferred_element_type=jnp.float32)
        out_ref[...] = term.astype(out_ref.dtype)


def add_kernel(own_ref, first_ref, second_ref, third_ref, out_ref):
    for block in range(EIGHT):
        part = lanes_of(block)
        total = own_ref[:, part]
        for ref in (first_ref, second_ref, third_ref):
            total += ref[:, part].astype(jnp.float32)
        out_ref[block] = total.astype(out_ref.dtype)


def values_kernel(keep_ref, arrived_ref, *refs):
    *weight_refs, own_ref, other_ref = refs
    columns = EIGHT * LANES
    total = jnp.zeros((2 * own_ref.shape[0], own_ref.shape[1]), jnp.float32)
    for step, weight_ref in enumerate(weight_refs):
        part = slice(step * columns, (step + 1) * columns)
        both = jnp.concatenate([keep_ref[:, part], arrived_ref[:, part]], axis=0)
        total += jnp.dot(both, weight_ref[...], preferred_element_type=jnp.float32)
    own_ref[...] = total[: own_ref.shape[0]]
    other_ref[...] = total[own_ref.shape[0] :]


def adam_direction(gradient, first_moment, second_moment, first_fix, second_fix):
    first_new = 0.9 * first_moment + 0.1 * gradient
    second_new = 0.95 * second_moment + 0.05 * gradient * gradient
    return first_new / first_fix / (jnp.sqrt(second_new / second_fix) + 1e-08)


def adam_kernel(
    token_total,
    terms_ref,
    weight_ref,
    gain_ref,
    fixes_ref,
    m_weight_ref,
    v_weight_ref,
    m_gain_ref,
    v_gain_ref,
    weight_step_ref,
    gain_step_ref,
):
    total = terms_ref[0].astype(jnp.float32)
    for block in range(1, EIGHT):
        total += terms_ref[block].astype(jnp.float32)
    gradient = total / token_total
    fixes = fixes_ref[0:1, :], fixes_ref[1:2, :]
    weight_gradient = (gradient * gain_ref[...].astype(jnp.float32)).T
    weight_step_ref[...] = adam_direction(weight_gradient, m_weight_ref[...], v_weight_ref[...], *fixes)
    gain_gradient = jnp.sum(gradient * weight_ref[...].astype(jnp.float32).T, axis=0, keepdims=True)
    gain_step_ref[...] = adam_direction(gain_gradient, m_gain_ref[...], v_gain_ref[...], *fixes)


def outer_update(global_params, moment, local_mean):
    delta = global_params - local_mean
    moment_new = 0.9 * moment + delta
    return (global_params - 0.7 * (delta + 0.9 * moment_new), moment_new)


def local(
    tokens_in,
    norm_gain,
    value_weight,
    value_cotangent,
    step_count,
    m_weight,
    v_weight,
    m_gain,
    v_gain,
    frag_local,
    frag_global,
    frag_moment,
):
    tokens = tokens_in[0]
    rows, width = tokens.shape
    head = value_weight.shape[2]
    half = width // 2
    columns = EIGHT * LANES
    token_total = rows * lax.axis_size("fsdp")

    gains = norm_gain[0].astype(jnp.float32)[:, None]
    scaled_weight = (value_weight[0].astype(jnp.float32) * gains).astype(jnp.bfloat16)
    weights = [spread(scaled_weight, EIGHT, "fsdp", EIGHT_GROUPS).reshape(columns, head)]
    weights += [lax.ppermute(weights[0], "fsdp", four_pairs(step)) for step in range(1, FOUR)]

    keep, send, inverse_rms = call(
        split_kernel,
        jax.ShapeDtypeStruct((rows, half), jnp.bfloat16),
        jax.ShapeDtypeStruct((rows, half + LANES), jnp.bfloat16),
        jax.ShapeDtypeStruct((rows, LANES), jnp.float32),
    )(tokens, value_cotangent[0])
    arrived = lax.ppermute(send, "fsdp", SWAP_CORES)

    own_term, *terms = call(
        gradient_kernel,
        jax.ShapeDtypeStruct((head, columns), jnp.float32),
        *[jax.ShapeDtypeStruct((head, columns), jnp.bfloat16)] * (FOUR - 1),
    )(keep, arrived, send)
    terms = [lax.ppermute(term, "fsdp", four_pairs(step)) for step, term in enumerate(terms, 1)]
    (summed,) = call(add_kernel, jax.ShapeDtypeStruct((EIGHT, head, LANES), jnp.bfloat16))(own_term, *terms)
    scattered = exchange(summed, "fsdp", EIGHT_GROUPS)
    steps = step_count.astype(jnp.float32)
    fixes = 1.0 - jnp.power(jnp.array([[0.9], [0.95]], jnp.float32), steps)
    weight_step, gain_step = call(
        functools.partial(adam_kernel, token_total),
        jax.ShapeDtypeStruct(m_weight.shape[1:], jnp.float32),
        jax.ShapeDtypeStruct(m_gain.shape, jnp.float32),
    )(
        scattered,
        value_weight[0],
        norm_gain,
        jnp.broadcast_to(fixes, (2, LANES)),
        m_weight[0],
        v_weight[0],
        m_gain,
        v_gain,
    )

    replicas = lax.axis_size("rep")
    frag = frag_local[0].astype(jnp.bfloat16)
    frag_terms = exchange(frag.reshape(replicas, -1, frag.shape[1]), "rep")
    frag_sum = jnp.sum(frag_terms.astype(jnp.float32), axis=0).astype(jnp.bfloat16)
    local_sum = spread(frag_sum, replicas, "rep").reshape(frag.shape).astype(jnp.float32)
    new_global, new_moment = outer_update(frag_global, frag_moment, local_sum / replicas)

    partial = jax.ShapeDtypeStruct((rows, head), jnp.float32)
    own_part, other_part = call(values_kernel, partial, partial)(keep, arrived, *weights)
    arrived_part = lax.ppermute(other_part, "fsdp", SWAP_CORES)
    values = ((own_part + arrived_part) * inverse_rms).astype(jnp.bfloat16)

    return (values[None], weight_step[None], gain_step, new_global, new_moment)


def solution(mesh):
    in_specs = (
        P("rep", "fsdp", None),
        P("rep", "fsdp"),
        P("rep", "fsdp", None),
        P("rep", "fsdp", None),
        P(),
        P("rep", "fsdp", None),
        P("rep", "fsdp", None),
        P("rep", "fsdp"),
        P("rep", "fsdp"),
        P("rep", "fsdp", None),
        P("fsdp", None),
        P("fsdp", None),
    )
    out_specs = (
        P("rep", "fsdp", None),
        P("rep", "fsdp", None),
        P("rep", "fsdp"),
        P("fsdp", None),
        P("fsdp", None),
    )
    return jax.shard_map(local, mesh=mesh, in_specs=in_specs, out_specs=out_specs, check_vma=False)
```

time: 470 us -> 114 us (0.24)
  the two profiles are of different devices: /device:TPU:2 before, /device:TPU:18 now
where the time goes in v2:
time: 114 us; the launch traced here: 113 us
  starting transfers between devices  62.2 us (55%)
  waiting for transfers between devices  32.6 us (29%)
  other arithmetic  6 us (5%)
  Pallas kernels  5.71 us (5%)
  local copies, waits for them, and re-layouts  4.75 us (4%)
  between operations  1.56 us (1%)
    all_to_all x4, starting transfers between devices, exchange(): lax.all_to_all(blocks, axis, 0, 0, axis_index_groups=groups, tiled=True)  39.5 us
    all_to_all x4, waiting for transfers between devices, exchange(): lax.all_to_all(blocks, axis, 0, 0, axis_index_groups=groups, tiled=True)  26.2 us
    ppermute x3, starting transfers between devices, local(): lax.ppermute(weights[0], 'fsdp', four_pairs(step))  9.56 us
    ppermute x3, starting transfers between devices, local(): lax.ppermute(term, 'fsdp', four_pairs(step))  9.2 us
    ppermute x3, waiting for transfers between devices, local(): lax.ppermute(term, 'fsdp', four_pairs(step))  6.36 us
    unnamed x28, local copies, waits for them, and re-layouts  3.2 us
  transfers between devices with their start and end apart: 12, of which 4 were waited for; matrix products, arithmetic and copies ran while one was open for 5% of the time, Pallas kernels for 4%

profile of v2, /device:TPU:18, one launch (start us, length us, event | category | flops | bytes accessed | tf_op | source)
XLA Modules:
  0.0 112.8 jit_solution(8159819823125455477)
XLA Ops:
  0.6 0.7 bitcast_convert_fusion
  1.3 0.8 fusion
  2.1 0.7 broadcast_in_dim.29
  2.9 10.7 %all-to-all-start = ((bf16[8,128,128]{2,1,0:T(8,128)(2,1)}), bf16[8,128,128]{2,1,0:T(8,128)(2,1)S(1)}, u32[]{:S(2)}, u32[]{:S(2)}) async-start(bf16[8,128,128]{2,1,0:T(8,128)(2,1)} %broadcast_in_dim.29), calls=%async_computation | async-start | bytes 524288 | tf_op jit(solution)/shard_map/all_to_all | solution.py:39
  13.6 1.6 %copy-done = bf16[1,128,8192]{2,1,0:T(8,128)(2,1)S(1)} copy-done((bf16[1,128,8192]{2,1,0:T(8,128)(2,1)S(1)}, bf16[1,128,8192]{2,1,0:T(8,128)(2,1)}, u32[]{:S(2)}) %copy-start) | copy-done | bytes 2097176
  15.1 0.8 copy-done.6
  15.9 1.0 shard_map.164
  16.9 1.9 %collective-permute-start = (bf16[128,4224]{1,0:T(8,128)(2,1)S(1)}, bf16[128,4224]{1,0:T(8,128)(2,1)S(1)}, u32[]{:S(2)}, u32[]{:S(2)}) collective-permute-start(bf16[128,4224]{1,0:T(8,128)(2,1)S(1)} %get-tuple-element.17.send_ref), channel_id=1, source_target_pairs={{0,1},{1,0},{2,3},{3,2},{4,5},{5,4},{6,7},{7,6},{8,9},{9,8},{10,11... | collective-permute-start | bytes 3244040 | tf_op jit(solution)/shard_map/ppermute | solution.py:181
  18.8 0.7 convert_bitcast_fusion
  19.6 8.1 %all-to-all-done = bf16[8,128,128]{2,1,0:T(8,128)(2,1)S(1)} async-done(((bf16[8,128,128]{2,1,0:T(8,128)(2,1)}), bf16[8,128,128]{2,1,0:T(8,128)(2,1)S(1)}, u32[]{:S(2)}, u32[]{:S(2)}) %all-to-all-start) | async-done | bytes 262176 | tf_op jit(solution)/shard_map/all_to_all | solution.py:39
  27.6 18.3 %all-to-all-start.2 = ((bf16[16,8,1024]{2,1,0:T(8,128)(2,1)}), bf16[16,8,1024]{2,1,0:T(8,128)(2,1)}, u32[]{:S(2)}, u32[]{:S(2)}) async-start(bf16[16,8,1024]{2,1,0:T(8,128)(2,1)} %convert_bitcast_fusion), calls=%async_computation.2 | async-start | bytes 524288 | tf_op jit(solution)/shard_map/all_to_all | solution.py:39
  45.9 3.1 %collective-permute-start.1 = (bf16[1024,128]{1,0:T(8,128)(2,1)S(1)}, bf16[1024,128]{1,0:T(8,128)(2,1)}, u32[]{:S(2)}, u32[]{:S(2)}) collective-permute-start(bf16[1024,128]{1,0:T(8,128)(2,1)S(1)} %bitcast.26), channel_id=1, source_target_pairs={{0,8},{2,10},{4,12},{6,14},{32,40},{34,42},{36,44},{38,46},{8,0},{... | collective-permute-start | bytes 786440 | tf_op jit(solution)/shard_map/ppermute | solution.py:173
  49.0 6.4 %all-to-all-done.2 = bf16[16,8,1024]{2,1,0:T(8,128)(2,1)} async-done(((bf16[16,8,1024]{2,1,0:T(8,128)(2,1)}), bf16[16,8,1024]{2,1,0:T(8,128)(2,1)}, u32[]{:S(2)}, u32[]{:S(2)}) %all-to-all-start.2) | async-done | bytes 262176 | tf_op jit(solution)/shard_map/all_to_all | solution.py:39
  55.4 1.0 reduce_sum.12
  56.4 0.7 broadcast_in_dim.34
  57.1 4.8 %all-to-all-start.3 = ((bf16[16,8,1024]{2,1,0:T(8,128)(2,1)}), bf16[16,8,1024]{2,1,0:T(8,128)(2,1)}, u32[]{:S(2)}, u32[]{:S(2)}) async-start(bf16[16,8,1024]{2,1,0:T(8,128)(2,1)} %broadcast_in_dim.34), calls=%async_computation.3 | async-start | bytes 524288 | tf_op jit(solution)/shard_map/all_to_all | solution.py:39
  62.0 3.0 %collective-permute-start.2 = (bf16[1024,128]{1,0:T(8,128)(2,1)S(1)}, bf16[1024,128]{1,0:T(8,128)(2,1)}, u32[]{:S(2)}, u32[]{:S(2)}) collective-permute-start(bf16[1024,128]{1,0:T(8,128)(2,1)S(1)} %bitcast.27), channel_id=1, source_target_pairs={{0,16},{2,18},{4,20},{6,22},{32,48},{34,50},{36,52},{38,54},{8,24}... | collective-permute-start | bytes 786440 | tf_op jit(solution)/shard_map/ppermute | solution.py:173
  64.9 3.5 %collective-permute-start.3 = (bf16[1024,128]{1,0:T(8,128)(2,1)S(1)}, bf16[1024,128]{1,0:T(8,128)(2,1)}, u32[]{:S(2)}, u32[]{:S(2)}) collective-permute-start(bf16[1024,128]{1,0:T(8,128)(2,1)S(1)} %bitcast.28), channel_id=1, source_target_pairs={{0,24},{2,26},{4,28},{6,30},{32,56},{34,58},{36,60},{38,62},{8,16}... | collective-permute-start | bytes 786440 | tf_op jit(solution)/shard_map/ppermute | solution.py:173
  68.5 0.0 collective-permute-done.arrived_ref
  68.5 0.0 copy-start.13
  68.5 1.2 %shard_map.166 = (f32[128,1024]{1,0:T(8,128)S(1)}, bf16[128,1024]{1,0:T(8,128)(2,1)}, bf16[128,1024]{1,0:T(8,128)(2,1)}, bf16[128,1024]{1,0:T(8,128)(2,1)}) custom-call(bf16[128,4096]{1,0:T(8,128)(2,1)S(1)} %get-tuple-element.16.keep_ref, bf16[128,4224]{1,0:T(8,128)(2,1)S(1)} %collective-permute-done.arrived_ref, ...), custom_call_target="tpu_custom_call" | custom-call | tf_op jit(solution)/shard_map/pallas_call | solution.py:183
  69.7 0.8 copy-done.1
  70.5 3.6 %collective-permute-start.5 = (bf16[128,1024]{1,0:T(8,128)(2,1)}, bf16[128,1024]{1,0:T(8,128)(2,1)S(1)}, u32[]{:S(2)}, u32[]{:S(2)}) collective-permute-start(bf16[128,1024]{1,0:T(8,128)(2,1)} %get-tuple-element.22), channel_id=1, source_target_pairs={{0,8},{2,10},{4,12},{6,14},{32,40},{34,42},{36,44},{38,46},{8,0},{... | collective-permute-start | bytes 786440 | tf_op jit(solution)/shard_map/ppermute | solution.py:188
  74.1 2.1 %collective-permute-start.6 = (bf16[128,1024]{1,0:T(8,128)(2,1)}, bf16[128,1024]{1,0:T(8,128)(2,1)S(1)}, u32[]{:S(2)}, u32[]{:S(2)}) collective-permute-start(bf16[128,1024]{1,0:T(8,128)(2,1)} %get-tuple-element.23), channel_id=1, source_target_pairs={{0,16},{2,18},{4,20},{6,22},{32,48},{34,50},{36,52},{38,54},{8,24}... | collective-permute-start | bytes 786440 | tf_op jit(solution)/shard_map/ppermute | solution.py:188
  76.2 0.0 collective-permute-done.1.refs_1_
  76.2 3.5 %collective-permute-start.7 = (bf16[128,1024]{1,0:T(8,128)(2,1)}, bf16[128,1024]{1,0:T(8,128)(2,1)S(1)}, u32[]{:S(2)}, u32[]{:S(2)}) collective-permute-start(bf16[128,1024]{1,0:T(8,128)(2,1)} %get-tuple-element.24), channel_id=1, source_target_pairs={{0,24},{2,26},{4,28},{6,30},{32,56},{34,58},{36,60},{38,62},{8,16}... | collective-permute-start | bytes 786440 | tf_op jit(solution)/shard_map/ppermute | solution.py:188
  80.4 0.0 copy-start.2
  80.4 0.0 collective-permute-done.2.refs_2_
  80.5 0.0 collective-permute-done.3.refs_3_
  80.5 1.9 %shard_map.165 = (f32[128,128]{1,0:T(8,128)S(1)}, f32[128,128]{1,0:T(8,128)S(1)}) custom-call(bf16[128,4096]{1,0:T(8,128)(2,1)S(1)} %get-tuple-element.16.keep_ref, bf16[128,4224]{1,0:T(8,128)(2,1)S(1)} %collective-permute-done.arrived_ref, bf16[1024,128]{1,0:T(8,128)(2,1)S(1)} %bitcast.29, bf16[1024,128]{1,0:T(8,128)(2,1)} %collective-permute-done.1.refs_1_, ...), custom_call_target="tpu_custom_call" | custom-call | tf_op jit(solution)/shard_map/pallas_call | solution.py:216
  82.3 0.0 copy-start.11
  82.3 0.0 copy-start.12
  82.4 2.1 %collective-permute-start.4 = (f32[128,128]{1,0:T(8,128)S(1)}, f32[128,128]{1,0:T(8,128)S(1)}, u32[]{:S(2)}, u32[]{:S(2)}) collective-permute-start(f32[128,128]{1,0:T(8,128)S(1)} %get-tuple-element.19), channel_id=1, source_target_pairs={{0,1},{1,0},{2,3},{3,2},{4,5},{5,4},{6,7},{7,6},{8,9},{9,8},{10,11... | collective-permute-start | bytes 196616 | tf_op jit(solution)/shard_map/ppermute | solution.py:217
  84.4 0.0 collective-permute-done.5.first_ref
  84.4 6.3 %collective-permute-done.7.third_ref = bf16[128,1024]{1,0:T(8,128)(2,1)S(1)} collective-permute-done((bf16[128,1024]{1,0:T(8,128)(2,1)}, bf16[128,1024]{1,0:T(8,128)(2,1)S(1)}, u32[]{:S(2)}, u32[]{:S(2)}) %collective-permute-start.7) | collective-permute-done | bytes 262176 | tf_op jit(solution)/shard_map/ppermute | solution.py:188
  90.8 0.9 shard_map.167
  91.6 5.7 %all-to-all-start.1 = ((bf16[8,128,128]{2,1,0:T(8,128)(2,1)}), bf16[8,128,128]{2,1,0:T(8,128)(2,1)S(1)}, u32[]{:S(2)}, u32[]{:S(2)}) async-start(bf16[8,128,128]{2,1,0:T(8,128)(2,1)} %shard_map.167), calls=%async_computation.1 | async-start | bytes 524288 | tf_op jit(solution)/shard_map/all_to_all | solution.py:39
  97.4 0.0 copy-start.3
  97.4 0.0 copy-start.4
  97.4 0.0 copy-start.5
  97.4 0.0 copy-start.7
  97.4 0.0 copy-start.8
  97.4 0.0 copy-start.9
  97.4 2.1 %multiply_subtract_fusion = (f32[128,1024]{1,0:T(8,128)}, f32[128,1024]{1,0:T(8,128)}) fusion(f32[128,1024]{1,0:T(8,128)S(1)} %copy-done.11, bf16[16,8,1024]{2,1,0:T(8,128)(2,1)} %all-to-all-done.3, f32[128,1024]{1,0:T(8,128)S(1)} %copy-done.12), kind=kLoop, calls=%fused_computation.1 | loop fusion | flops 1179648 | bytes 2359296 | tf_op jit(solution)/shard_map/sub | solution.py:146
  99.6 0.6 fusion.1
  100.2 11.7 %all-to-all-done.1.terms_ref = bf16[8,128,128]{2,1,0:T(8,128)(2,1)S(1)} async-done(((bf16[8,128,128]{2,1,0:T(8,128)(2,1)}), bf16[8,128,128]{2,1,0:T(8,128)(2,1)S(1)}, u32[]{:S(2)}, u32[]{:S(2)}) %all-to-all-start.1) | async-done | bytes 262176 | tf_op jit(solution)/shard_map/all_to_all | solution.py:39
  111.9 0.1 broadcast_in_dim.32.fixes_ref
  112.0 0.8 shard_map.168
  (19 shorter events, 0.1 us)
Async XLA Ops:
  2.9 24.8 %all-to-all-start = ((bf16[8,128,128]{2,1,0:T(8,128)(2,1)}), bf16[8,128,128]{2,1,0:T(8,128)(2,1)S(1)}, u32[]{:S(2)}, u32[]{:S(2)}) async-start(bf16[8,128,128]{2,1,0:T(8,128)(2,1)} %broadcast_in_dim.29), calls=%async_computation | async-start | bytes 524288 | tf_op jit(solution)/shard_map/all_to_all | solution.py:39
  13.5 1.6 %copy-start = (bf16[1,128,8192]{2,1,0:T(8,128)(2,1)S(1)}, bf16[1,128,8192]{2,1,0:T(8,128)(2,1)}, u32[]{:S(2)}) copy-start(bf16[1,128,8192]{2,1,0:T(8,128)(2,1)} %param.13) | copy-start | bytes 6291460
  15.1 0.8 copy-start.6
  15.9 2.9 %copy-start.10 = (f32[1,128,1024]{2,1,0:T(8,128)S(1)}, f32[1,128,1024]{2,1,0:T(8,128)}, u32[]{:S(2)}) copy-start(f32[1,128,1024]{2,1,0:T(8,128)} %param.22) | copy-start | bytes 1572868
  16.9 51.6 %collective-permute-start = (bf16[128,4224]{1,0:T(8,128)(2,1)S(1)}, bf16[128,4224]{1,0:T(8,128)(2,1)S(1)}, u32[]{:S(2)}, u32[]{:S(2)}) collective-permute-start(bf16[128,4224]{1,0:T(8,128)(2,1)S(1)} %get-tuple-element.17.send_ref), channel_id=1, source_target_pairs={{0,1},{1,0},{2,3},{3,2},{4,5},{5,4},{6,7},{7,6},{8,9},{9,8},{10,11... | collective-permute-start | bytes 3244040 | tf_op jit(solution)/shard_map/ppermute | solution.py:181
  27.6 27.8 %all-to-all-start.2 = ((bf16[16,8,1024]{2,1,0:T(8,128)(2,1)}), bf16[16,8,1024]{2,1,0:T(8,128)(2,1)}, u32[]{:S(2)}, u32[]{:S(2)}) async-start(bf16[16,8,1024]{2,1,0:T(8,128)(2,1)} %convert_bitcast_fusion), calls=%async_computation.2 | async-start | bytes 524288 | tf_op jit(solution)/shard_map/all_to_all | solution.py:39
  45.9 30.3 %collective-permute-start.1 = (bf16[1024,128]{1,0:T(8,128)(2,1)S(1)}, bf16[1024,128]{1,0:T(8,128)(2,1)}, u32[]{:S(2)}, u32[]{:S(2)}) collective-permute-start(bf16[1024,128]{1,0:T(8,128)(2,1)S(1)} %bitcast.26), channel_id=1, source_target_pairs={{0,8},{2,10},{4,12},{6,14},{32,40},{34,42},{36,44},{38,46},{8,0},{... | collective-permute-start | bytes 786440 | tf_op jit(solution)/shard_map/ppermute | solution.py:173
  57.1 34.5 %all-to-all-start.3 = ((bf16[16,8,1024]{2,1,0:T(8,128)(2,1)}), bf16[16,8,1024]{2,1,0:T(8,128)(2,1)}, u32[]{:S(2)}, u32[]{:S(2)}) async-start(bf16[16,8,1024]{2,1,0:T(8,128)(2,1)} %broadcast_in_dim.34), calls=%async_computation.3 | async-start | bytes 524288 | tf_op jit(solution)/shard_map/all_to_all | solution.py:39
  62.0 18.5 %collective-permute-start.2 = (bf16[1024,128]{1,0:T(8,128)(2,1)S(1)}, bf16[1024,128]{1,0:T(8,128)(2,1)}, u32[]{:S(2)}, u32[]{:S(2)}) collective-permute-start(bf16[1024,128]{1,0:T(8,128)(2,1)S(1)} %bitcast.27), channel_id=1, source_target_pairs={{0,16},{2,18},{4,20},{6,22},{32,48},{34,50},{36,52},{38,54},{8,24}... | collective-permute-start | bytes 786440 | tf_op jit(solution)/shard_map/ppermute | solution.py:173
  64.9 15.5 %collective-permute-start.3 = (bf16[1024,128]{1,0:T(8,128)(2,1)S(1)}, bf16[1024,128]{1,0:T(8,128)(2,1)}, u32[]{:S(2)}, u32[]{:S(2)}) collective-permute-start(bf16[1024,128]{1,0:T(8,128)(2,1)S(1)} %bitcast.28), channel_id=1, source_target_pairs={{0,24},{2,26},{4,28},{6,30},{32,56},{34,58},{36,60},{38,62},{8,16}... | collective-permute-start | bytes 786440 | tf_op jit(solution)/shard_map/ppermute | solution.py:173
  68.5 11.9 %copy-start.13 = (f32[2,1]{0,1:T(1,128)S(1)}, f32[2,1]{0,1:T(1,128)}, u32[]{:S(2)}) copy-start(f32[2,1]{0,1:T(1,128)} %constant.14.clone) | copy-start | bytes 28
  69.7 0.8 copy-start.1
  70.5 13.9 %collective-permute-start.5 = (bf16[128,1024]{1,0:T(8,128)(2,1)}, bf16[128,1024]{1,0:T(8,128)(2,1)S(1)}, u32[]{:S(2)}, u32[]{:S(2)}) collective-permute-start(bf16[128,1024]{1,0:T(8,128)(2,1)} %get-tuple-element.22), channel_id=1, source_target_pairs={{0,8},{2,10},{4,12},{6,14},{32,40},{34,42},{36,44},{38,46},{8,0},{... | collective-permute-start | bytes 786440 | tf_op jit(solution)/shard_map/ppermute | solution.py:188
  74.1 10.3 %collective-permute-start.6 = (bf16[128,1024]{1,0:T(8,128)(2,1)}, bf16[128,1024]{1,0:T(8,128)(2,1)S(1)}, u32[]{:S(2)}, u32[]{:S(2)}) collective-permute-start(bf16[128,1024]{1,0:T(8,128)(2,1)} %get-tuple-element.23), channel_id=1, source_target_pairs={{0,16},{2,18},{4,20},{6,22},{32,48},{34,50},{36,52},{38,54},{8,24}... | collective-permute-start | bytes 786440 | tf_op jit(solution)/shard_map/ppermute | solution.py:188
  76.2 14.6 %collective-permute-start.7 = (bf16[128,1024]{1,0:T(8,128)(2,1)}, bf16[128,1024]{1,0:T(8,128)(2,1)S(1)}, u32[]{:S(2)}, u32[]{:S(2)}) collective-permute-start(bf16[128,1024]{1,0:T(8,128)(2,1)} %get-tuple-element.24), channel_id=1, source_target_pairs={{0,24},{2,26},{4,28},{6,30},{32,56},{34,58},{36,60},{38,62},{8,16}... | collective-permute-start | bytes 786440 | tf_op jit(solution)/shard_map/ppermute | solution.py:188
  80.4 10.4 %copy-start.2 = (f32[128,1024]{1,0:T(8,128)S(1)}, f32[128,1024]{1,0:T(8,128)}, u32[]{:S(2)}) copy-start(f32[128,1024]{1,0:T(8,128)} %copy-done.1) | copy-start | bytes 1572868
  82.3 15.0 %copy-start.11 = (f32[128,1024]{1,0:T(8,128)S(1)}, f32[128,1024]{1,0:T(8,128)}, u32[]{:S(2)}) copy-start(f32[128,1024]{1,0:T(8,128)} %param.23) | copy-start | bytes 1572868
  82.3 15.0 %copy-start.12 = (f32[128,1024]{1,0:T(8,128)S(1)}, f32[128,1024]{1,0:T(8,128)}, u32[]{:S(2)}) copy-start(f32[128,1024]{1,0:T(8,128)} %param.24) | copy-start | bytes 1572868
  82.4 17.2 %collective-permute-start.4 = (f32[128,128]{1,0:T(8,128)S(1)}, f32[128,128]{1,0:T(8,128)S(1)}, u32[]{:S(2)}, u32[]{:S(2)}) collective-permute-start(f32[128,128]{1,0:T(8,128)S(1)} %get-tuple-element.19), channel_id=1, source_target_pairs={{0,1},{1,0},{2,3},{3,2},{4,5},{5,4},{6,7},{7,6},{8,9},{9,8},{10,11... | collective-permute-start | bytes 196616 | tf_op jit(solution)/shard_map/ppermute | solution.py:217
  91.6 20.3 %all-to-all-start.1 = ((bf16[8,128,128]{2,1,0:T(8,128)(2,1)}), bf16[8,128,128]{2,1,0:T(8,128)(2,1)S(1)}, u32[]{:S(2)}, u32[]{:S(2)}) async-start(bf16[8,128,128]{2,1,0:T(8,128)(2,1)} %shard_map.167), calls=%async_computation.1 | async-start | bytes 524288 | tf_op jit(solution)/shard_map/all_to_all | solution.py:39
  97.4 14.6 %copy-start.3 = (bf16[1,128,128]{2,1,0:T(8,128)(2,1)S(1)}, bf16[1,128,128]{2,1,0:T(8,128)(2,1)}, u32[]{:S(2)}) copy-start(bf16[1,128,128]{2,1,0:T(8,128)(2,1)} %param.15) | copy-start | bytes 98308
  97.4 14.6 %copy-start.4 = (f32[1,128,128]{2,1,0:T(8,128)S(1)}, f32[1,128,128]{2,1,0:T(8,128)}, u32[]{:S(2)}) copy-start(f32[1,128,128]{2,1,0:T(8,128)} %param.18) | copy-start | bytes 196612
  97.4 14.6 %copy-start.5 = (f32[1,128,128]{2,1,0:T(8,128)S(1)}, f32[1,128,128]{2,1,0:T(8,128)}, u32[]{:S(2)}) copy-start(f32[1,128,128]{2,1,0:T(8,128)} %param.19) | copy-start | bytes 196612
  97.4 14.6 %copy-start.7 = (bf16[1,128]{1,0:T(2,128)(2,1)S(1)}, bf16[1,128]{1,0:T(2,128)(2,1)}, u32[]{:S(2)}) copy-start(bf16[1,128]{1,0:T(2,128)(2,1)} %gain_ref.1) | copy-start | bytes 772
  97.4 14.6 %copy-start.8 = (f32[1,128]{1,0:T(1,128)S(1)}, f32[1,128]{1,0:T(1,128)}, u32[]{:S(2)}) copy-start(f32[1,128]{1,0:T(1,128)} %m_gain_ref.1) | copy-start | bytes 1540
  97.4 14.6 %copy-start.9 = (f32[1,128]{1,0:T(1,128)S(1)}, f32[1,128]{1,0:T(1,128)}, u32[]{:S(2)}) copy-start(f32[1,128]{1,0:T(1,128)} %v_gain_ref.1) | copy-start | bytes 1540

commit v3 on v2

v3 whole, which is shorter than its diff:
```python
import functools

import jax
import jax.numpy as jnp
from jax import lax
from jax.experimental import pallas as pl
from jax.experimental.pallas import tpu as pltpu
from jax.sharding import PartitionSpec as P

EIGHT = 8
FOUR = 4
LANES = 128


def chip_of(core, four, eight):
    if core:
        return eight * FOUR + four
    return (eight // FOUR * FOUR + four) * FOUR + eight % FOUR


def device_of(core, four, eight):
    return chip_of(core, four, eight) * 2 + core


EIGHT_GROUPS = [[device_of(core, four, eight) for eight in range(EIGHT)] for core in range(2) for four in range(FOUR)]
SWAP_CORES = [(device, device ^ 1) for device in range(2 * FOUR * EIGHT)]


def four_pairs(step):
    return [
        (device_of(core, four, eight), device_of(core, four ^ step, eight))
        for core in range(2)
        for four in range(FOUR)
        for eight in range(EIGHT)
    ]


def exchange(blocks, axis, groups=None):
    return lax.all_to_all(blocks, axis, 0, 0, axis_index_groups=groups, tiled=True)


def spread(block, count, axis, groups=None):
    return exchange(jnp.broadcast_to(block[None], (count,) + block.shape), axis, groups)


def call(kernel, *out_shapes, mebibytes=16, **specs):
    return pl.pallas_call(
        kernel,
        out_shape=out_shapes,
        **specs,
        compiler_params=pltpu.CompilerParams(vmem_limit_bytes=mebibytes * 1024 * 1024),
    )


def lanes_of(block):
    return slice(block * LANES, (block + 1) * LANES)


def split_kernel(
    tokens_hbm,
    cotangent_hbm,
    weight_hbm,
    gain_ref,
    keep_ref,
    send_ref,
    scaled_ref,
    inverse_ref,
    spread_ref,
    tokens_ref,
    cotangent_ref,
    weight_ref,
    semaphores,
):
    rows, width = tokens_ref.shape
    pieces = 4
    piece = width // pieces
    copies = [
        pltpu.make_async_copy(weight_hbm, weight_ref, semaphores.at[pieces]),
        pltpu.make_async_copy(cotangent_hbm, cotangent_ref, semaphores.at[pieces + 1]),
    ]
    for index in range(pieces):
        part = slice(index * piece, (index + 1) * piece)
        copies.append(pltpu.make_async_copy(tokens_hbm.at[:, part], tokens_ref.at[:, part], semaphores.at[index]))
    for copy in copies:
        copy.start()

    copies[0].wait()
    gains = jnp.broadcast_to(gain_ref[...].astype(jnp.float32), (LANES, LANES)).T
    scaled_weight = (weight_ref[...].astype(jnp.float32) * gains).astype(jnp.bfloat16)
    for eight in range(EIGHT):
        spread_ref[eight] = scaled_weight

    total = jnp.zeros((rows, LANES), jnp.float32)
    for index in range(pieces):
        copies[2 + index].wait()
        for block in range(index * piece // LANES, (index + 1) * piece // LANES):
            floats = tokens_ref[:, lanes_of(block)].astype(jnp.float32)
            total += floats * floats
    inverse = lax.rsqrt(jnp.sum(total, axis=1, keepdims=True) / width + 1e-05)
    inverse_ref[...] = jnp.broadcast_to(inverse, (rows, LANES))
    copies[1].wait()
    scaled = (cotangent_ref[...].astype(jnp.float32) * inverse).astype(jnp.bfloat16)
    scaled_ref[...] = scaled
    send_ref[:, lanes_of(FOUR * EIGHT)] = scaled

    device = lax.axis_index("fsdp")
    core = lax.rem(device, 2)
    chip = lax.div(device, 2)
    row, column = lax.div(chip, FOUR), lax.rem(chip, FOUR)
    fours = (lax.rem(row, FOUR), column)
    for step in range(FOUR):
        for eight in range(EIGHT):
            chips = [chip_of(kind, fours[kind] ^ step, eight) for kind in range(2)]
            for target, kind in ((keep_ref, core), (send_ref, 1 - core)):
                source = jnp.where(kind == 0, chips[0], chips[1]) * 2 + kind
                start = pl.multiple_of(source * LANES, LANES)
                target[:, lanes_of(step * EIGHT + eight)] = tokens_ref[:, pl.ds(start, LANES)]


def gradient_term(keep_ref, arrived_ref, scaled_ref, step):
    part = slice(step * EIGHT * LANES, (step + 1) * EIGHT * LANES)
    cotangents = jnp.concatenate([scaled_ref[...], arrived_ref[:, lanes_of(FOUR * EIGHT)]], axis=0)
    both = jnp.concatenate([keep_ref[:, part], arrived_ref[:, part]], axis=0)
    return lax.dot_general(cotangents, both, (((0,), (0,)), ((), ())), preferred_element_type=jnp.float32)


def outgoing_kernel(keep_ref, arrived_ref, scaled_ref, weight_ref, again_ref, *out_refs):
    again_ref[...] = scaled_ref[...]
    for step, out_ref in enumerate(out_refs, 1):
        term = gradient_term(keep_ref, arrived_ref, scaled_ref, step)
        for eight in range(EIGHT):
            out_ref[0, eight] = weight_ref[eight]
            out_ref[1, eight] = term[:, lanes_of(eight)].astype(jnp.bfloat16)


def add_kernel(keep_ref, arrived_ref, scaled_ref, first_ref, second_ref, third_ref, out_ref):
    own = gradient_term(keep_ref, arrived_ref, scaled_ref, 0)
    for eight in range(EIGHT):
        total = own[:, lanes_of(eight)]
        for ref in (first_ref, second_ref, third_ref):
            total += ref[1, eight].astype(jnp.float32)
        out_ref[eight] = total.astype(out_ref.dtype)


def values_kernel(keep_ref, arrived_ref, weight_ref, first_ref, second_ref, third_ref, own_ref, other_ref):
    columns = EIGHT * LANES
    rows, head = own_ref.shape
    total = jnp.zeros((2 * rows, head), jnp.float32)
    weights = [weight_ref[...]] + [ref[0] for ref in (first_ref, second_ref, third_ref)]
    for step, weight in enumerate(weights):
        part = slice(step * columns, (step + 1) * columns)
        both = jnp.concatenate([keep_ref[:, part], arrived_ref[:, part]], axis=0)
        total += jnp.dot(both, weight.reshape(columns, head), preferred_element_type=jnp.float32)
    own_ref[...] = total[:rows]
    other_ref[...] = total[rows:]


def adam_direction(gradient, first_moment, second_moment, first_fix, second_fix):
    first_new = 0.9 * first_moment + 0.1 * gradient
    second_new = 0.95 * second_moment + 0.05 * gradient * gradient
    return first_new / first_fix / (jnp.sqrt(second_new / second_fix) + 1e-08)


def adam_kernel(
    token_total,
    terms_ref,
    weight_ref,
    gain_ref,
    fixes_ref,
    m_weight_ref,
    v_weight_ref,
    m_gain_ref,
    v_gain_ref,
    weight_step_ref,
    gain_step_ref,
):
    total = terms_ref[0].astype(jnp.float32)
    for block in range(1, EIGHT):
        total += terms_ref[block].astype(jnp.float32)
    gradient = total / token_total
    fixes = fixes_ref[0:1, :], fixes_ref[1:2, :]
    weight_gradient = (gradient * gain_ref[...].astype(jnp.float32)).T
    weight_step_ref[...] = adam_direction(weight_gradient, m_weight_ref[...], v_weight_ref[...], *fixes)
    gain_gradient = jnp.sum(gradient * weight_ref[...].astype(jnp.float32).T, axis=0, keepdims=True)
    gain_step_ref[...] = adam_direction(gain_gradient, m_gain_ref[...], v_gain_ref[...], *fixes)


def outer_update(global_params, moment, local_mean):
    delta = global_params - local_mean
    moment_new = 0.9 * moment + delta
    return (global_params - 0.7 * (delta + 0.9 * moment_new), moment_new)


def local(
    tokens_in,
    norm_gain,
    value_weight,
    value_cotangent,
    step_count,
    m_weight,
    v_weight,
    m_gain,
    v_gain,
    frag_local,
    frag_global,
    frag_moment,
):
    rows, width = tokens_in.shape[1:]
    head = value_weight.shape[2]
    half = width // 2
    token_total = rows * lax.axis_size("fsdp")
    replicas = lax.axis_size("rep")
    frag_shape = frag_local.shape[1:]

    hbm = pl.BlockSpec(memory_space=pltpu.HBM)
    keep, send, scaled, inverse_rms, spread_weight = call(
        split_kernel,
        jax.ShapeDtypeStruct((rows, half), jnp.bfloat16),
        jax.ShapeDtypeStruct((rows, half + LANES), jnp.bfloat16),
        jax.ShapeDtypeStruct((rows, head), jnp.bfloat16),
        jax.ShapeDtypeStruct((rows, LANES), jnp.float32),
        jax.ShapeDtypeStruct((EIGHT, LANES, head), jnp.bfloat16),
        mebibytes=60,
        in_specs=[hbm, hbm, hbm, pl.BlockSpec(memory_space=pltpu.VMEM)],
        scratch_shapes=[
            pltpu.VMEM((rows, width), jnp.bfloat16),
            pltpu.VMEM((rows, head), jnp.bfloat16),
            pltpu.VMEM((LANES, head), jnp.bfloat16),
            pltpu.SemaphoreType.DMA((6,)),
        ],
    )(tokens_in[0], value_cotangent[0], value_weight[0], norm_gain)
    arrived = lax.ppermute(send, "fsdp", SWAP_CORES)
    weight = exchange(spread_weight, "fsdp", EIGHT_GROUPS)

    scaled, *outgoing = call(
        outgoing_kernel,
        jax.ShapeDtypeStruct(scaled.shape, scaled.dtype),
        *[jax.ShapeDtypeStruct((2, EIGHT, head, LANES), jnp.bfloat16)] * (FOUR - 1),
    )(keep, arrived, scaled, weight)
    frag = frag_local[0].astype(jnp.bfloat16).reshape(replicas, -1, frag_shape[1])
    scaled, frag = lax.optimization_barrier((scaled, frag))
    incoming = [lax.ppermute(blocks, "fsdp", four_pairs(step)) for step, blocks in enumerate(outgoing, 1)]
    frag_terms = exchange(frag, "rep")
    frag_sum = jnp.sum(frag_terms.astype(jnp.float32), axis=0).astype(jnp.bfloat16)
    scaled, frag_sum = lax.optimization_barrier((scaled, frag_sum))
    local_sum = spread(frag_sum, replicas, "rep")

    (summed,) = call(add_kernel, jax.ShapeDtypeStruct((EIGHT, head, LANES), jnp.bfloat16))(
        keep, arrived, scaled, *incoming
    )
    summed, local_sum = lax.optimization_barrier((summed, local_sum))
    scattered = exchange(summed, "fsdp", EIGHT_GROUPS)
    local_mean = local_sum.reshape(frag_shape).astype(jnp.float32) / replicas
    new_global, new_moment = outer_update(frag_global, frag_moment, local_mean)

    partial = jax.ShapeDtypeStruct((rows, head), jnp.float32)
    own_part, other_part = call(values_kernel, partial, partial)(keep, arrived, weight, *incoming)
    arrived_part = lax.ppermute(other_part, "fsdp", SWAP_CORES)
    values = ((own_part + arrived_part) * inverse_rms).astype(jnp.bfloat16)

    steps = step_count.astype(jnp.float32)
    fixes = 1.0 - jnp.power(jnp.array([[0.9], [0.95]], jnp.float32), steps)
    weight_step, gain_step = call(
        functools.partial(adam_kernel, token_total),
        jax.ShapeDtypeStruct(m_weight.shape[1:], jnp.float32),
        jax.ShapeDtypeStruct(m_gain.shape, jnp.float32),
    )(
        scattered,
        value_weight[0],
        norm_gain,
        jnp.broadcast_to(fixes, (2, LANES)),
        m_weight[0],
        v_weight[0],
        m_gain,
        v_gain,
    )
    return (values[None], weight_step[None], gain_step, new_global, new_moment)


def solution(mesh):
    in_specs = (
        P("rep", "fsdp", None),
        P("rep", "fsdp"),
        P("rep", "fsdp", None),
        P("rep", "fsdp", None),
        P(),
        P("rep", "fsdp", None),
        P("rep", "fsdp", None),
        P("rep", "fsdp"),
        P("rep", "fsdp"),
        P("rep", "fsdp", None),
        P("fsdp", None),
        P("fsdp", None),
    )
    out_specs = (
        P("rep", "fsdp", None),
        P("rep", "fsdp", None),
        P("rep", "fsdp"),
        P("fsdp", None),
        P("fsdp", None),
    )
    return jax.shard_map(local, mesh=mesh, in_specs=in_specs, out_specs=out_specs, check_vma=False)
```

time: 114 us -> 110 us (0.965)
  starting transfers between devices: 62.2 us -> 52.8 us
  Pallas kernels: 5.71 us -> 10.9 us
  waiting for transfers between devices: 32.6 us -> 36.8 us
  local copies, waits for them, and re-layouts: 4.75 us -> 1.66 us
    ppermute x6 -> x3, starting transfers between devices: 18.8 us -> 9.21 us  [local(): lax.ppermute(blocks, 'fsdp', four_pairs(step))]
    ppermute x6 -> x3, waiting for transfers between devices: 6.36 us -> 11.6 us  [local(): lax.ppermute(blocks, 'fsdp', four_pairs(step))]
    pallas_call x1, Pallas kernels: 0.98 us -> 4.51 us  [local(): call(split_kernel, jax.ShapeDtypeStruct((rows, half), jnp.bfloat16), jax....]
    unnamed x28 -> x26, local copies, waits for them, and re-layouts: 3.2 us -> 0.85 us
    pallas_call x1, Pallas kernels: 0.85 us -> 2.04 us  [local(): call(add_kernel, jax.ShapeDtypeStruct((EIGHT, head, LANES), jnp.bfloat16))]
  transfers between devices with their start and end apart: 12 -> 9, of which waited for: 4 -> 5; matrix products, arithmetic and copies ran while one was open for 5% -> 6% of each run, Pallas kernels for 4% -> 4%
where the time goes in v3:
time: 110 us; the launch traced here: 109 us
  starting transfers between devices  52.8 us (48%)
  waiting for transfers between devices  36.8 us (33%)
  Pallas kernels  10.9 us (10%)
  other arithmetic  5.59 us (5%)
  local copies, waits for them, and re-layouts  1.66 us (2%)
  between operations  1.48 us (1%)
    all_to_all x4, starting transfers between devices, exchange(): lax.all_to_all(blocks, axis, 0, 0, axis_index_groups=groups, tiled=True)  39.6 us
    all_to_all x4, waiting for transfers between devices, exchange(): lax.all_to_all(blocks, axis, 0, 0, axis_index_groups=groups, tiled=True)  25.1 us
    ppermute x3, waiting for transfers between devices, local(): lax.ppermute(blocks, 'fsdp', four_pairs(step))  11.6 us
    ppermute x3, starting transfers between devices, local(): lax.ppermute(blocks, 'fsdp', four_pairs(step))  9.21 us
    pallas_call x1, Pallas kernels, local(): call(split_kernel, jax.ShapeDtypeStruct((rows, half), jnp.bfloat16), jax....  4.51 us
    pallas_call x1, Pallas kernels, local(): call(values_kernel, partial, partial)(keep, arrived, weight, *incoming)  2.37 us
    sub x1, other arithmetic, outer_update(): return (global_params - 0.7 * (delta + 0.9 * moment_new), moment_new)  2.33 us
  transfers between devices with their start and end apart: 9, of which 5 were waited for; matrix products, arithmetic and copies ran while one was open for 6% of the time, Pallas kernels for 4%

profile of v3, /device:TPU:18, one launch (start us, length us, event | category | flops | bytes accessed | tf_op | source)
XLA Modules:
  0.0 109.2 jit_solution(17098698433374831765)
XLA Ops:
  0.6 0.0 copy-start.10
  0.6 4.5 %shard_map.164 = (bf16[128,4096]{1,0:T(8,128)(2,1)}, bf16[128,4224]{1,0:T(8,128)(2,1)}, bf16[128,128]{1,0:T(8,128)(2,1)}, f32[128,128]{1,0:T(8,128)}, bf16[8,128,128]{2,1,0:T(8,128)(2,1)}) custom-call(bf16[128,8192]{1,0:T(8,128)(2,1)} %bitcast.23, bf16[128,128]{1,0:T(8,128)(2,1)} %bitcast.24, bf16[128,128]{1,0:T(8,128)(2,1)} %bitcast.19, bf16[1,128]{1,0:T(2,128)(2,1)} %gain_ref.3), custom_call_target="tpu_custom_call" | custom-call | tf_op jit(solution)/shard_map/pallas_call | solution.py:216
  5.2 0.0 copy-start
  5.2 0.0 copy-start.4
  5.2 2.1 %collective-permute-start = (bf16[128,4224]{1,0:T(8,128)(2,1)}, bf16[128,4224]{1,0:T(8,128)(2,1)S(1)}, u32[]{:S(2)}, u32[]{:S(2)}) collective-permute-start(bf16[128,4224]{1,0:T(8,128)(2,1)} %get-tuple-element.25), channel_id=1, source_target_pairs={{0,1},{1,0},{2,3},{3,2},{4,5},{5,4},{6,7},{7,6},{8,9},{9,8},{10,11... | collective-permute-start | bytes 3244040 | tf_op jit(solution)/shard_map/ppermute | solution.py:232
  7.2 10.7 %all-to-all-start = ((bf16[8,128,128]{2,1,0:T(8,128)(2,1)}), bf16[8,128,128]{2,1,0:T(8,128)(2,1)S(1)}, u32[]{:S(2)}, u32[]{:S(2)}) async-start(bf16[8,128,128]{2,1,0:T(8,128)(2,1)} %get-tuple-element.26), calls=%async_computation | async-start | bytes 524288 | tf_op jit(solution)/shard_map/all_to_all | solution.py:39
  17.9 0.0 copy-done.10
  17.9 0.7 convert_bitcast_fusion
  18.7 13.3 %all-to-all-done.weight_ref = bf16[8,128,128]{2,1,0:T(8,128)(2,1)S(1)} async-done(((bf16[8,128,128]{2,1,0:T(8,128)(2,1)}), bf16[8,128,128]{2,1,0:T(8,128)(2,1)S(1)}, u32[]{:S(2)}, u32[]{:S(2)}) %all-to-all-start) | async-done | bytes 262176 | tf_op jit(solution)/shard_map/all_to_all | solution.py:39
  32.0 0.0 collective-permute-done.arrived_ref
  32.0 0.0 copy-done
  32.0 0.0 copy-done.4
  32.0 1.2 %shard_map.165 = (bf16[128,128]{1,0:T(8,128)(2,1)S(1)}, bf16[2,8,128,128]{3,2,1,0:T(8,128)(2,1)}, bf16[2,8,128,128]{3,2,1,0:T(8,128)(2,1)S(1)}, bf16[2,8,128,128]{3,2,1,0:T(8,128)(2,1)S(1)}) custom-call(bf16[128,4096]{1,0:T(8,128)(2,1)S(1)} %copy-done, bf16[128,4224]{1,0:T(8,128)(2,1)S(1)} %collective-permute-done.arrived_ref, ...), custom_call_target="tpu_custom_call" | custom-call | tf_op jit(solution)/shard_map/pallas_call | solution.py:235
  33.2 0.8 copy-done.9
  34.0 18.2 %all-to-all-start.1 = ((bf16[16,8,1024]{2,1,0:T(8,128)(2,1)}), bf16[16,8,1024]{2,1,0:T(8,128)(2,1)}, u32[]{:S(2)}, u32[]{:S(2)}) async-start(bf16[16,8,1024]{2,1,0:T(8,128)(2,1)} %convert_bitcast_fusion), calls=%async_computation.1 | async-start | bytes 524288 | tf_op jit(solution)/shard_map/all_to_all | solution.py:39
  52.2 0.0 copy-done.8
  52.2 3.2 %collective-permute-start.1 = (bf16[2,8,128,128]{3,2,1,0:T(8,128)(2,1)}, bf16[2,8,128,128]{3,2,1,0:T(8,128)(2,1)S(1)}, u32[]{:S(2)}, u32[]{:S(2)}) collective-permute-start(bf16[2,8,128,128]{3,2,1,0:T(8,128)(2,1)} %get-tuple-element.28), channel_id=1, source_target_pairs={{0,8},{2,10},{4,12},{6,14},{32,40},{34,42},{36,44},{38,46},{8,0},{... | collective-permute-start | bytes 1572872 | tf_op jit(solution)/shard_map/ppermute | solution.py:242
  55.4 2.9 %collective-permute-start.2 = (bf16[2,8,128,128]{3,2,1,0:T(8,128)(2,1)}, bf16[2,8,128,128]{3,2,1,0:T(8,128)(2,1)S(1)}, u32[]{:S(2)}, u32[]{:S(2)}) collective-permute-start(bf16[2,8,128,128]{3,2,1,0:T(8,128)(2,1)} %copy-done.9), channel_id=1, source_target_pairs={{0,16},{2,18},{4,20},{6,22},{32,48},{34,50},{36,52},{38,54},{8,24}... | collective-permute-start | bytes 1572872 | tf_op jit(solution)/shard_map/ppermute | solution.py:242
  58.3 3.1 %collective-permute-start.3 = (bf16[2,8,128,128]{3,2,1,0:T(8,128)(2,1)}, bf16[2,8,128,128]{3,2,1,0:T(8,128)(2,1)}, u32[]{:S(2)}, u32[]{:S(2)}) collective-permute-start(bf16[2,8,128,128]{3,2,1,0:T(8,128)(2,1)} %copy-done.8), channel_id=1, source_target_pairs={{0,24},{2,26},{4,28},{6,30},{32,56},{34,58},{36,60},{38,62},{8,16}... | collective-permute-start | bytes 1572872 | tf_op jit(solution)/shard_map/ppermute | solution.py:242
  61.4 1.2 %all-to-all-done.1 = bf16[16,8,1024]{2,1,0:T(8,128)(2,1)} async-done(((bf16[16,8,1024]{2,1,0:T(8,128)(2,1)}), bf16[16,8,1024]{2,1,0:T(8,128)(2,1)}, u32[]{:S(2)}, u32[]{:S(2)}) %all-to-all-start.1) | async-done | bytes 262176 | tf_op jit(solution)/shard_map/all_to_all | solution.py:39
  62.6 1.0 reduce_sum.12
  63.6 0.7 broadcast_in_dim.20
  64.3 7.2 %all-to-all-start.2 = ((bf16[16,8,1024]{2,1,0:T(8,128)(2,1)}), bf16[16,8,1024]{2,1,0:T(8,128)(2,1)}, u32[]{:S(2)}, u32[]{:S(2)}) async-start(bf16[16,8,1024]{2,1,0:T(8,128)(2,1)} %broadcast_in_dim.20), calls=%async_computation.2 | async-start | bytes 524288 | tf_op jit(solution)/shard_map/all_to_all | solution.py:39
  72.2 0.0 copy-start.12
  72.2 0.0 collective-permute-done.1.first_ref
  72.2 4.3 %collective-permute-done.2.second_ref = bf16[2,8,128,128]{3,2,1,0:T(8,128)(2,1)S(1)} collective-permute-done((bf16[2,8,128,128]{3,2,1,0:T(8,128)(2,1)}, bf16[2,8,128,128]{3,2,1,0:T(8,128)(2,1)S(1)}, u32[]{:S(2)}, u32[]{:S(2)}) %collective-permute-start.2) | collective-permute-done | bytes 524320 | tf_op jit(solution)/shard_map/ppermute | solution.py:242
  76.6 7.3 %collective-permute-done.3.third_ref = bf16[2,8,128,128]{3,2,1,0:T(8,128)(2,1)} collective-permute-done((bf16[2,8,128,128]{3,2,1,0:T(8,128)(2,1)}, bf16[2,8,128,128]{3,2,1,0:T(8,128)(2,1)}, u32[]{:S(2)}, u32[]{:S(2)}) %collective-permute-start.3) | collective-permute-done | bytes 524320 | tf_op jit(solution)/shard_map/ppermute | solution.py:242
  83.9 2.4 %shard_map.166 = (f32[128,128]{1,0:T(8,128)S(1)}, f32[128,128]{1,0:T(8,128)}) custom-call(bf16[128,4096]{1,0:T(8,128)(2,1)S(1)} %copy-done, bf16[128,4224]{1,0:T(8,128)(2,1)S(1)} %collective-permute-done.arrived_ref, bf16[8,128,128]{2,1,0:T(8,128)(2,1)S(1)} %all-to-all-done.weight_ref, bf16[2,8,128,128]{3,2,1,0:T(8,128)(2,1)S(1)} %collective-permute-done.1.first_ref, ...), custom_call_target="tpu_custom_call" | custom-call | tf_op jit(solution)/shard_map/pallas_call | solution.py:257
  86.2 1.9 %collective-permute-start.4 = (f32[128,128]{1,0:T(8,128)}, f32[128,128]{1,0:T(8,128)}, u32[]{:S(2)}, u32[]{:S(2)}) collective-permute-start(f32[128,128]{1,0:T(8,128)} %get-tuple-element.32), channel_id=1, source_target_pairs={{0,1},{1,0},{2,3},{3,2},{4,5},{5,4},{6,7},{7,6},{8,9},{9,8},{10,11... | collective-permute-start | bytes 196616 | tf_op jit(solution)/shard_map/ppermute | solution.py:258
  88.1 0.0 copy-done.12
  88.2 2.0 %shard_map.167 = bf16[8,128,128]{2,1,0:T(8,128)(2,1)} custom-call(bf16[128,4096]{1,0:T(8,128)(2,1)S(1)} %copy-done, bf16[128,4224]{1,0:T(8,128)(2,1)S(1)} %collective-permute-done.arrived_ref, bf16[128,128]{1,0:T(8,128)(2,1)S(1)} %get-tuple-element.37.scaled_ref, bf16[2,8,128,128]{3,2,1,0:T(8,128)(2,1)S(1)} %collective-permute-done.1.first_ref, ...), custom_call_target="tpu_custom_call" | custom-call | tf_op jit(solution)/shard_map/pallas_call | solution.py:248
  90.2 0.0 all-to-all-done.2
  90.2 3.5 %all-to-all-start.3 = ((bf16[8,128,128]{2,1,0:T(8,128)(2,1)}), bf16[8,128,128]{2,1,0:T(8,128)(2,1)S(1)}, u32[]{:S(2)}, u32[]{:S(2)}) async-start(bf16[8,128,128]{2,1,0:T(8,128)(2,1)} %shard_map.167), calls=%async_computation.3 | async-start | bytes 524288 | tf_op jit(solution)/shard_map/all_to_all | solution.py:39
  93.8 0.0 collective-permute-done.4
  93.8 1.5 %fusion = bf16[1,128,128]{2,1,0:T(8,128)(2,1)} fusion(f32[128,128]{1,0:T(8,128)} %get-tuple-element.33, f32[128,128]{1,0:T(8,128)S(1)} %get-tuple-element.31, f32[128,128]{1,0:T(8,128)} %collective-permute-done.4), kind=kLoop, calls=%fused_computation.5 | loop fusion | flops 49152 | bytes 229376 | tf_op jit(solution)/shard_map/broadcast_in_dim | solution.py:277
  95.3 0.0 copy-done.11
  95.3 0.0 copy-start.5
  95.3 0.0 copy-start.6
  95.3 0.0 copy-start.7
  95.3 2.3 %multiply_subtract_fusion = (f32[128,1024]{1,0:T(8,128)}, f32[128,1024]{1,0:T(8,128)}) fusion(f32[128,1024]{1,0:T(8,128)S(1)} %copy-done.11, bf16[16,8,1024]{2,1,0:T(8,128)(2,1)} %all-to-all-done.2, f32[128,1024]{1,0:T(8,128)} %param.24), kind=kLoop, calls=%fused_computation.1 | loop fusion | flops 1179648 | bytes 2359296 | tf_op jit(solution)/shard_map/sub | solution.py:191
  97.7 10.6 %all-to-all-done.3.terms_ref = bf16[8,128,128]{2,1,0:T(8,128)(2,1)S(1)} async-done(((bf16[8,128,128]{2,1,0:T(8,128)(2,1)}), bf16[8,128,128]{2,1,0:T(8,128)(2,1)S(1)}, u32[]{:S(2)}, u32[]{:S(2)}) %all-to-all-start.3) | async-done | bytes 262176 | tf_op jit(solution)/shard_map/all_to_all | solution.py:39
  108.3 0.1 broadcast_in_dim.22.fixes_ref
  108.4 0.0 copy-done.1
  108.4 0.0 copy-done.2
  108.4 0.0 copy-done.3
  108.4 0.0 copy-done.6
  108.4 0.0 copy-done.7
  108.4 0.8 shard_map.168
  (8 shorter events, 0.0 us)
Async XLA Ops:
  0.6 17.3 %copy-start.10 = (f32[1,128,1024]{2,1,0:T(8,128)S(1)}, f32[1,128,1024]{2,1,0:T(8,128)}, u32[]{:S(2)}) copy-start(f32[1,128,1024]{2,1,0:T(8,128)} %param.22) | copy-start | bytes 1572868
  5.2 26.9 %copy-start = (bf16[128,4096]{1,0:T(8,128)(2,1)S(1)}, bf16[128,4096]{1,0:T(8,128)(2,1)}, u32[]{:S(2)}) copy-start(bf16[128,4096]{1,0:T(8,128)(2,1)} %get-tuple-element.24.keep_ref) | copy-start | bytes 3145732
  5.2 26.9 %copy-start.4 = (bf16[128,128]{1,0:T(8,128)(2,1)S(1)}, bf16[128,128]{1,0:T(8,128)(2,1)}, u32[]{:S(2)}) copy-start(bf16[128,128]{1,0:T(8,128)(2,1)} %get-tuple-element.27.scaled_ref) | copy-start | bytes 98308
  5.2 26.8 %collective-permute-start = (bf16[128,4224]{1,0:T(8,128)(2,1)}, bf16[128,4224]{1,0:T(8,128)(2,1)S(1)}, u32[]{:S(2)}, u32[]{:S(2)}) collective-permute-start(bf16[128,4224]{1,0:T(8,128)(2,1)} %get-tuple-element.25), channel_id=1, source_target_pairs={{0,1},{1,0},{2,3},{3,2},{4,5},{5,4},{6,7},{7,6},{8,9},{9,8},{10,11... | collective-permute-start | bytes 3244040 | tf_op jit(solution)/shard_map/ppermute | solution.py:232
  7.2 24.8 %all-to-all-start = ((bf16[8,128,128]{2,1,0:T(8,128)(2,1)}), bf16[8,128,128]{2,1,0:T(8,128)(2,1)S(1)}, u32[]{:S(2)}, u32[]{:S(2)}) async-start(bf16[8,128,128]{2,1,0:T(8,128)(2,1)} %get-tuple-element.26), calls=%async_computation | async-start | bytes 524288 | tf_op jit(solution)/shard_map/all_to_all | solution.py:39
  33.2 0.8 copy-start.9
  34.0 18.2 %copy-start.8 = (bf16[2,8,128,128]{3,2,1,0:T(8,128)(2,1)}, bf16[2,8,128,128]{3,2,1,0:T(8,128)(2,1)S(1)}, u32[]{:S(2)}) copy-start(bf16[2,8,128,128]{3,2,1,0:T(8,128)(2,1)S(1)} %get-tuple-element.30) | copy-start | bytes 1572868
  34.0 28.6 %all-to-all-start.1 = ((bf16[16,8,1024]{2,1,0:T(8,128)(2,1)}), bf16[16,8,1024]{2,1,0:T(8,128)(2,1)}, u32[]{:S(2)}, u32[]{:S(2)}) async-start(bf16[16,8,1024]{2,1,0:T(8,128)(2,1)} %convert_bitcast_fusion), calls=%async_computation.1 | async-start | bytes 524288 | tf_op jit(solution)/shard_map/all_to_all | solution.py:39
  52.2 20.0 %collective-permute-start.1 = (bf16[2,8,128,128]{3,2,1,0:T(8,128)(2,1)}, bf16[2,8,128,128]{3,2,1,0:T(8,128)(2,1)S(1)}, u32[]{:S(2)}, u32[]{:S(2)}) collective-permute-start(bf16[2,8,128,128]{3,2,1,0:T(8,128)(2,1)} %get-tuple-element.28), channel_id=1, source_target_pairs={{0,8},{2,10},{4,12},{6,14},{32,40},{34,42},{36,44},{38,46},{8,0},{... | collective-permute-start | bytes 1572872 | tf_op jit(solution)/shard_map/ppermute | solution.py:242
  55.4 21.2 %collective-permute-start.2 = (bf16[2,8,128,128]{3,2,1,0:T(8,128)(2,1)}, bf16[2,8,128,128]{3,2,1,0:T(8,128)(2,1)S(1)}, u32[]{:S(2)}, u32[]{:S(2)}) collective-permute-start(bf16[2,8,128,128]{3,2,1,0:T(8,128)(2,1)} %copy-done.9), channel_id=1, source_target_pairs={{0,16},{2,18},{4,20},{6,22},{32,48},{34,50},{36,52},{38,54},{8,24}... | collective-permute-start | bytes 1572872 | tf_op jit(solution)/shard_map/ppermute | solution.py:242
  58.3 25.6 %collective-permute-start.3 = (bf16[2,8,128,128]{3,2,1,0:T(8,128)(2,1)}, bf16[2,8,128,128]{3,2,1,0:T(8,128)(2,1)}, u32[]{:S(2)}, u32[]{:S(2)}) collective-permute-start(bf16[2,8,128,128]{3,2,1,0:T(8,128)(2,1)} %copy-done.8), channel_id=1, source_target_pairs={{0,24},{2,26},{4,28},{6,30},{32,56},{34,58},{36,60},{38,62},{8,16}... | collective-permute-start | bytes 1572872 | tf_op jit(solution)/shard_map/ppermute | solution.py:242
  64.3 25.9 %all-to-all-start.2 = ((bf16[16,8,1024]{2,1,0:T(8,128)(2,1)}), bf16[16,8,1024]{2,1,0:T(8,128)(2,1)}, u32[]{:S(2)}, u32[]{:S(2)}) async-start(bf16[16,8,1024]{2,1,0:T(8,128)(2,1)} %broadcast_in_dim.20), calls=%async_computation.2 | async-start | bytes 524288 | tf_op jit(solution)/shard_map/all_to_all | solution.py:39
  72.2 15.9 %copy-start.12 = (f32[2,1]{0,1:T(1,128)S(1)}, f32[2,1]{0,1:T(1,128)}, u32[]{:S(2)}) copy-start(f32[2,1]{0,1:T(1,128)} %constant.14.clone) | copy-start | bytes 28
  86.2 7.6 %collective-permute-start.4 = (f32[128,128]{1,0:T(8,128)}, f32[128,128]{1,0:T(8,128)}, u32[]{:S(2)}, u32[]{:S(2)}) collective-permute-start(f32[128,128]{1,0:T(8,128)} %get-tuple-element.32), channel_id=1, source_target_pairs={{0,1},{1,0},{2,3},{3,2},{4,5},{5,4},{6,7},{7,6},{8,9},{9,8},{10,11... | collective-permute-start | bytes 196616 | tf_op jit(solution)/shard_map/ppermute | solution.py:258
  90.2 5.1 %copy-start.11 = (f32[128,1024]{1,0:T(8,128)S(1)}, f32[128,1024]{1,0:T(8,128)}, u32[]{:S(2)}) copy-start(f32[128,1024]{1,0:T(8,128)} %param.23) | copy-start | bytes 1572868
  90.2 18.1 %all-to-all-start.3 = ((bf16[8,128,128]{2,1,0:T(8,128)(2,1)}), bf16[8,128,128]{2,1,0:T(8,128)(2,1)S(1)}, u32[]{:S(2)}, u32[]{:S(2)}) async-start(bf16[8,128,128]{2,1,0:T(8,128)(2,1)} %shard_map.167), calls=%async_computation.3 | async-start | bytes 524288 | tf_op jit(solution)/shard_map/all_to_all | solution.py:39
  95.3 13.1 %copy-start.1 = (bf16[1,128,128]{2,1,0:T(8,128)(2,1)S(1)}, bf16[1,128,128]{2,1,0:T(8,128)(2,1)}, u32[]{:S(2)}) copy-start(bf16[1,128,128]{2,1,0:T(8,128)(2,1)} %param.15) | copy-start | bytes 98308
  95.3 13.1 %copy-start.2 = (f32[1,128,128]{2,1,0:T(8,128)S(1)}, f32[1,128,128]{2,1,0:T(8,128)}, u32[]{:S(2)}) copy-start(f32[1,128,128]{2,1,0:T(8,128)} %param.18) | copy-start | bytes 196612
  95.3 13.1 %copy-start.3 = (f32[1,128,128]{2,1,0:T(8,128)S(1)}, f32[1,128,128]{2,1,0:T(8,128)}, u32[]{:S(2)}) copy-start(f32[1,128,128]{2,1,0:T(8,128)} %param.19) | copy-start | bytes 196612
  95.3 13.1 %copy-start.5 = (bf16[1,128]{1,0:T(2,128)(2,1)S(1)}, bf16[1,128]{1,0:T(2,128)(2,1)}, u32[]{:S(2)}) copy-start(bf16[1,128]{1,0:T(2,128)(2,1)} %gain_ref.3) | copy-start | bytes 772
  95.3 13.1 %copy-start.6 = (f32[1,128]{1,0:T(1,128)S(1)}, f32[1,128]{1,0:T(1,128)}, u32[]{:S(2)}) copy-start(f32[1,128]{1,0:T(1,128)} %m_gain_ref.1) | copy-start | bytes 1540
  95.3 13.1 %copy-start.7 = (f32[1,128]{1,0:T(1,128)S(1)}, f32[1,128]{1,0:T(1,128)}, u32[]{:S(2)}) copy-start(f32[1,128]{1,0:T(1,128)} %v_gain_ref.1) | copy-start | bytes 1540

commit v4 on v3

--- a/solution.py
+++ b/solution.py
@@ -22,6 +22,11 @@
     return chip_of(core, four, eight) * 2 + core
 
 
+SIXTEEN_GROUPS = [
+    [device_of(core, 2 * high + low, eight) for high in range(2) for eight in range(EIGHT)]
+    for core in range(2)
+    for low in range(2)
+]
 EIGHT_GROUPS = [[device_of(core, four, eight) for eight in range(EIGHT)] for core in range(2) for four in range(FOUR)]
 SWAP_CORES = [(device, device ^ 1) for device in range(2 * FOUR * EIGHT)]
 
@@ -50,6 +55,13 @@
         **specs,
         compiler_params=pltpu.CompilerParams(vmem_limit_bytes=mebibytes * 1024 * 1024),
     )
+
+
+def place():
+    device = lax.axis_index("fsdp")
+    chip = lax.div(device, 2)
+    row, column = lax.div(chip, FOUR), lax.rem(chip, FOUR)
+    return lax.rem(device, 2), (lax.rem(row, FOUR), column)
 
 
 def lanes_of(block):
@@ -87,8 +99,8 @@
     copies[0].wait()
     gains = jnp.broadcast_to(gain_ref[...].astype(jnp.float32), (LANES, LANES)).T
     scaled_weight = (weight_ref[...].astype(jnp.float32) * gains).astype(jnp.bfloat16)
-    for eight in range(EIGHT):
-        spread_ref[eight] = scaled_weight
+    for block in range(spread_ref.shape[0]):
+        spread_ref[block] = scaled_weight
 
     total = jnp.zeros((rows, LANES), jnp.float32)
     for index in range(pieces):
@@ -103,11 +115,7 @@
     scaled_ref[...] = scaled
     send_ref[:, lanes_of(FOUR * EIGHT)] = scaled
 
-    device = lax.axis_index("fsdp")
-    core = lax.rem(device, 2)
-    chip = lax.div(device, 2)
-    row, column = lax.div(chip, FOUR), lax.rem(chip, FOUR)
-    fours = (lax.rem(row, FOUR), column)
+    core, fours = place()
     for step in range(FOUR):
         for eight in range(EIGHT):
             chips = [chip_of(kind, fours[kind] ^ step, eight) for kind in range(2)]
@@ -124,13 +132,12 @@
     return lax.dot_general(cotangents, both, (((0,), (0,)), ((), ())), preferred_element_type=jnp.float32)
 
 
-def outgoing_kernel(keep_ref, arrived_ref, scaled_ref, weight_ref, again_ref, *out_refs):
+def outgoing_kernel(keep_ref, arrived_ref, scaled_ref, again_ref, *out_refs):
     again_ref[...] = scaled_ref[...]
     for step, out_ref in enumerate(out_refs, 1):
         term = gradient_term(keep_ref, arrived_ref, scaled_ref, step)
         for eight in range(EIGHT):
-            out_ref[0, eight] = weight_ref[eight]
-            out_ref[1, eight] = term[:, lanes_of(eight)].astype(jnp.bfloat16)
+            out_ref[eight] = term[:, lanes_of(eight)].astype(jnp.bfloat16)
 
 
 def add_kernel(keep_ref, arrived_ref, scaled_ref, first_ref, second_ref, third_ref, out_ref):
@@ -138,19 +145,22 @@
     for eight in range(EIGHT):
         total = own[:, lanes_of(eight)]
         for ref in (first_ref, second_ref, third_ref):
-            total += ref[1, eight].astype(jnp.float32)
+            total += ref[eight].astype(jnp.float32)
         out_ref[eight] = total.astype(out_ref.dtype)
 
 
-def values_kernel(keep_ref, arrived_ref, weight_ref, first_ref, second_ref, third_ref, own_ref, other_ref):
+def values_kernel(keep_ref, arrived_ref, own_weight_ref, partner_weight_ref, own_ref, other_ref):
+    core, fours = place()
+    high = jnp.where(core == 0, fours[0], fours[1]) // 2
     columns = EIGHT * LANES
     rows, head = own_ref.shape
     total = jnp.zeros((2 * rows, head), jnp.float32)
-    weights = [weight_ref[...]] + [ref[0] for ref in (first_ref, second_ref, third_ref)]
-    for step, weight in enumerate(weights):
+    for step in range(FOUR):
         part = slice(step * columns, (step + 1) * columns)
         both = jnp.concatenate([keep_ref[:, part], arrived_ref[:, part]], axis=0)
-        total += jnp.dot(both, weight.reshape(columns, head), preferred_element_type=jnp.float32)
+        blocks = pl.ds((high ^ (step // 2)) * EIGHT, EIGHT)
+        weight = (partner_weight_ref if step % 2 else own_weight_ref)[blocks].reshape(columns, head)
+        total += jnp.dot(both, weight, preferred_element_type=jnp.float32)
     own_ref[...] = total[:rows]
     other_ref[...] = total[rows:]
 
@@ -219,7 +229,7 @@
         jax.ShapeDtypeStruct((rows, half + LANES), jnp.bfloat16),
         jax.ShapeDtypeStruct((rows, head), jnp.bfloat16),
         jax.ShapeDtypeStruct((rows, LANES), jnp.float32),
-        jax.ShapeDtypeStruct((EIGHT, LANES, head), jnp.bfloat16),
+        jax.ShapeDtypeStruct((2 * EIGHT, LANES, head), jnp.bfloat16),
         mebibytes=60,
         in_specs=[hbm, hbm, hbm, pl.BlockSpec(memory_space=pltpu.VMEM)],
         scratch_shapes=[
@@ -230,31 +240,31 @@
         ],
     )(tokens_in[0], value_cotangent[0], value_weight[0], norm_gain)
     arrived = lax.ppermute(send, "fsdp", SWAP_CORES)
-    weight = exchange(spread_weight, "fsdp", EIGHT_GROUPS)
+    weight = exchange(spread_weight, "fsdp", SIXTEEN_GROUPS)
 
     scaled, *outgoing = call(
         outgoing_kernel,
         jax.ShapeDtypeStruct(scaled.shape, scaled.dtype),
-        *[jax.ShapeDtypeStruct((2, EIGHT, head, LANES), jnp.bfloat16)] * (FOUR - 1),
-    )(keep, arrived, scaled, weight)
+        *[jax.ShapeDtypeStruct((EIGHT, head, LANES), jnp.bfloat16)] * (FOUR - 1),
+    )(keep, arrived, scaled)
+    incoming = [lax.ppermute(blocks, "fsdp", four_pairs(step)) for step, blocks in enumerate(outgoing, 1)]
     frag = frag_local[0].astype(jnp.bfloat16).reshape(replicas, -1, frag_shape[1])
-    scaled, frag = lax.optimization_barrier((scaled, frag))
-    incoming = [lax.ppermute(blocks, "fsdp", four_pairs(step)) for step, blocks in enumerate(outgoing, 1)]
+    *incoming, frag = lax.optimization_barrier((*incoming, frag))
+    partner_weight = lax.ppermute(weight, "fsdp", four_pairs(1))
     frag_terms = exchange(frag, "rep")
     frag_sum = jnp.sum(frag_terms.astype(jnp.float32), axis=0).astype(jnp.bfloat16)
-    scaled, frag_sum = lax.optimization_barrier((scaled, frag_sum))
     local_sum = spread(frag_sum, replicas, "rep")
 
     (summed,) = call(add_kernel, jax.ShapeDtypeStruct((EIGHT, head, LANES), jnp.bfloat16))(
         keep, arrived, scaled, *incoming
     )
-    summed, local_sum = lax.optimization_barrier((summed, local_sum))
+    summed, keep, arrived = lax.optimization_barrier((summed, keep, arrived))
     scattered = exchange(summed, "fsdp", EIGHT_GROUPS)
     local_mean = local_sum.reshape(frag_shape).astype(jnp.float32) / replicas
     new_global, new_moment = outer_update(frag_global, frag_moment, local_mean)
 
     partial = jax.ShapeDtypeStruct((rows, head), jnp.float32)
-    own_part, other_part = call(values_kernel, partial, partial)(keep, arrived, weight, *incoming)
+    own_part, other_part = call(values_kernel, partial, partial)(keep, arrived, weight, partner_weight)
     arrived_part = lax.ppermute(other_part, "fsdp", SWAP_CORES)
     values = ((own_part + arrived_part) * inverse_rms).astype(jnp.bfloat16)
 

time: 110 us -> 117 us (1.064)
  the two profiles are of different devices: /device:TPU:18 before, /device:TPU:16 now
where the time goes in v4:
time: 117 us; the launch traced here: 116 us
  starting transfers between devices  58.1 us (50%)
  waiting for transfers between devices  39.3 us (34%)
  Pallas kernels  7.42 us (6%)
  local copies, waits for them, and re-layouts  4.92 us (4%)
  other arithmetic  4.81 us (4%)
  between operations  1.54 us (1%)
    all_to_all x4, starting transfers between devices, exchange(): lax.all_to_all(blocks, axis, 0, 0, axis_index_groups=groups, tiled=True)  38.8 us
    all_to_all x4, waiting for transfers between devices, exchange(): lax.all_to_all(blocks, axis, 0, 0, axis_index_groups=groups, tiled=True)  23.7 us
    ppermute x3, waiting for transfers between devices, local(): lax.ppermute(blocks, 'fsdp', four_pairs(step))  14.4 us
    ppermute x3, starting transfers between devices, local(): lax.ppermute(blocks, 'fsdp', four_pairs(step))  13.4 us
    pallas_call x1, Pallas kernels, local(): call(split_kernel, jax.ShapeDtypeStruct((rows, half), jnp.bfloat16), jax....  4.54 us
    unnamed x30, local copies, waits for them, and re-layouts  4.13 us
    sub x1, other arithmetic, outer_update(): return (global_params - 0.7 * (delta + 0.9 * moment_new), moment_new)  2.43 us
  transfers between devices with their start and end apart: 10, of which 7 were waited for; matrix products, arithmetic and copies ran while one was open for 3% of the time, Pallas kernels for 2%

profile of v4, /device:TPU:16, one launch (start us, length us, event | category | flops | bytes accessed | tf_op | source)
XLA Modules:
  0.0 116.1 jit_solution(7763380896966429993)
XLA Ops:
  0.6 4.5 %shard_map.164 = (bf16[128,4096]{1,0:T(8,128)(2,1)}, bf16[128,4224]{1,0:T(8,128)(2,1)}, bf16[128,128]{1,0:T(8,128)(2,1)}, f32[128,128]{1,0:T(8,128)}, bf16[16,128,128]{2,1,0:T(8,128)(2,1)}) custom-call(bf16[128,8192]{1,0:T(8,128)(2,1)} %bitcast.23, bf16[128,128]{1,0:T(8,128)(2,1)} %bitcast.24, bf16[128,128]{1,0:T(8,128)(2,1)} %bitcast.19, ...), custom_call_target="tpu_custom_call" | custom-call | tf_op jit(solution)/shard_map/pallas_call | solution.py:226
  5.2 2.1 %collective-permute-start = (bf16[128,4224]{1,0:T(8,128)(2,1)}, bf16[128,4224]{1,0:T(8,128)(2,1)S(1)}, u32[]{:S(2)}, u32[]{:S(2)}) collective-permute-start(bf16[128,4224]{1,0:T(8,128)(2,1)} %get-tuple-element.26), channel_id=1, source_target_pairs={{0,1},{1,0},{2,3},{3,2},{4,5},{5,4},{6,7},{7,6},{8,9},{9,8},{10,11... | collective-permute-start | bytes 3244040 | tf_op jit(solution)/shard_map/ppermute | solution.py:242
  7.3 11.7 %all-to-all-start = ((bf16[16,128,128]{2,1,0:T(8,128)(2,1)}), bf16[16,128,128]{2,1,0:T(8,128)(2,1)S(1)}, u32[]{:S(2)}, u32[]{:S(2)}) async-start(bf16[16,128,128]{2,1,0:T(8,128)(2,1)} %get-tuple-element.37), calls=%async_computation | async-start | bytes 1048576 | tf_op jit(solution)/shard_map/all_to_all | solution.py:44
  19.0 0.0 collective-permute-done.arrived_ref
  19.0 0.0 copy-start.8
  19.0 0.7 copy-done.8
  19.7 0.4 shard_map.165
  20.1 6.8 %collective-permute-start.1 = (bf16[8,128,128]{2,1,0:T(8,128)(2,1)S(1)}, bf16[8,128,128]{2,1,0:T(8,128)(2,1)S(1)}, u32[]{:S(2)}, u32[]{:S(2)}) collective-permute-start(bf16[8,128,128]{2,1,0:T(8,128)(2,1)S(1)} %get-tuple-element.29), channel_id=1, source_target_pairs={{0,8},{2,10},{4,12},{6,14},{32,40},{34,42},{36,44},{38,46},{8,0},{... | collective-permute-start | bytes 786440 | tf_op jit(solution)/shard_map/ppermute | solution.py:250
  27.0 4.7 %collective-permute-start.2 = (bf16[8,128,128]{2,1,0:T(8,128)(2,1)S(1)}, bf16[8,128,128]{2,1,0:T(8,128)(2,1)S(1)}, u32[]{:S(2)}, u32[]{:S(2)}) collective-permute-start(bf16[8,128,128]{2,1,0:T(8,128)(2,1)S(1)} %get-tuple-element.30), channel_id=1, source_target_pairs={{0,16},{2,18},{4,20},{6,22},{32,48},{34,50},{36,52},{38,54},{8,24}... | collective-permute-start | bytes 786440 | tf_op jit(solution)/shard_map/ppermute | solution.py:250
  31.6 1.9 %collective-permute-start.3 = (bf16[8,128,128]{2,1,0:T(8,128)(2,1)S(1)}, bf16[8,128,128]{2,1,0:T(8,128)(2,1)S(1)}, u32[]{:S(2)}, u32[]{:S(2)}) collective-permute-start(bf16[8,128,128]{2,1,0:T(8,128)(2,1)S(1)} %get-tuple-element.31), channel_id=1, source_target_pairs={{0,24},{2,26},{4,28},{6,30},{32,56},{34,58},{36,60},{38,62},{8,16}... | collective-permute-start | bytes 786440 | tf_op jit(solution)/shard_map/ppermute | solution.py:250
  33.6 0.0 copy-done.12
  33.6 0.7 convert_bitcast_fusion
  34.3 5.7 %collective-permute-done.1.first_ref = bf16[8,128,128]{2,1,0:T(8,128)(2,1)S(1)} collective-permute-done((bf16[8,128,128]{2,1,0:T(8,128)(2,1)S(1)}, bf16[8,128,128]{2,1,0:T(8,128)(2,1)S(1)}, u32[]{:S(2)}, u32[]{:S(2)}) %collective-permute-start.1) | collective-permute-done | bytes 262176 | tf_op jit(solution)/shard_map/ppermute | solution.py:250
  40.0 5.6 %collective-permute-done.2.second_ref = bf16[8,128,128]{2,1,0:T(8,128)(2,1)S(1)} collective-permute-done((bf16[8,128,128]{2,1,0:T(8,128)(2,1)S(1)}, bf16[8,128,128]{2,1,0:T(8,128)(2,1)S(1)}, u32[]{:S(2)}, u32[]{:S(2)}) %collective-permute-start.2) | collective-permute-done | bytes 262176 | tf_op jit(solution)/shard_map/ppermute | solution.py:250
  45.6 0.7 copy-done.1
  46.3 3.1 %collective-permute-done.3.third_ref = bf16[8,128,128]{2,1,0:T(8,128)(2,1)S(1)} collective-permute-done((bf16[8,128,128]{2,1,0:T(8,128)(2,1)S(1)}, bf16[8,128,128]{2,1,0:T(8,128)(2,1)S(1)}, u32[]{:S(2)}, u32[]{:S(2)}) %collective-permute-start.3) | collective-permute-done | bytes 262176 | tf_op jit(solution)/shard_map/ppermute | solution.py:250
  49.4 0.7 copy-done.3
  50.1 0.0 all-to-all-done.own_weight_ref
  50.1 14.3 %all-to-all-start.2 = ((bf16[16,8,1024]{2,1,0:T(8,128)(2,1)}), bf16[16,8,1024]{2,1,0:T(8,128)(2,1)}, u32[]{:S(2)}, u32[]{:S(2)}) async-start(bf16[16,8,1024]{2,1,0:T(8,128)(2,1)} %convert_bitcast_fusion), calls=%async_computation.2 | async-start | bytes 524288 | tf_op jit(solution)/shard_map/all_to_all | solution.py:44
  64.4 1.9 %collective-permute-start.4 = (bf16[16,128,128]{2,1,0:T(8,128)(2,1)S(1)}, bf16[16,128,128]{2,1,0:T(8,128)(2,1)S(1)}, u32[]{:S(2)}, u32[]{:S(2)}) collective-permute-start(bf16[16,128,128]{2,1,0:T(8,128)(2,1)S(1)} %all-to-all-done.own_weight_ref), channel_id=1, source_target_pairs={{0,8},{2,10},{4,12},{6,14},{32,40},{34,42},{36,44},{38,46},{8,0},{... | collective-permute-start | bytes 1572872 | tf_op jit(solution)/shard_map/ppermute | solution.py:253
  66.3 0.0 copy-start.2
  66.3 0.9 copy-done.2
  67.3 0.9 copy-done.4
  68.2 1.0 shard_map.166
  69.2 7.1 %all-to-all-done.2 = bf16[16,8,1024]{2,1,0:T(8,128)(2,1)} async-done(((bf16[16,8,1024]{2,1,0:T(8,128)(2,1)}), bf16[16,8,1024]{2,1,0:T(8,128)(2,1)}, u32[]{:S(2)}, u32[]{:S(2)}) %all-to-all-start.2) | async-done | bytes 262176 | tf_op jit(solution)/shard_map/all_to_all | solution.py:44
  76.3 7.9 %all-to-all-start.1 = ((bf16[8,128,128]{2,1,0:T(8,128)(2,1)}), bf16[8,128,128]{2,1,0:T(8,128)(2,1)S(1)}, u32[]{:S(2)}, u32[]{:S(2)}) async-start(bf16[8,128,128]{2,1,0:T(8,128)(2,1)} %shard_map.166), calls=%async_computation.1 | async-start | bytes 524288 | tf_op jit(solution)/shard_map/all_to_all | solution.py:44
  84.3 1.0 reduce_sum.12
  85.3 12.5 %all-to-all-done.1.terms_ref = bf16[8,128,128]{2,1,0:T(8,128)(2,1)S(1)} async-done(((bf16[8,128,128]{2,1,0:T(8,128)(2,1)}), bf16[8,128,128]{2,1,0:T(8,128)(2,1)S(1)}, u32[]{:S(2)}, u32[]{:S(2)}) %all-to-all-start.1) | async-done | bytes 262176 | tf_op jit(solution)/shard_map/all_to_all | solution.py:44
  97.8 0.7 broadcast_in_dim.23
  98.5 4.9 %all-to-all-start.3 = ((bf16[16,8,1024]{2,1,0:T(8,128)(2,1)}), bf16[16,8,1024]{2,1,0:T(8,128)(2,1)}, u32[]{:S(2)}, u32[]{:S(2)}) async-start(bf16[16,8,1024]{2,1,0:T(8,128)(2,1)} %broadcast_in_dim.23), calls=%async_computation.3 | async-start | bytes 524288 | tf_op jit(solution)/shard_map/all_to_all | solution.py:44
  104.0 0.0 copy-start.14
  104.1 0.0 copy-start.13
  104.1 0.0 copy-start.5
  104.1 0.0 copy-start.6
  104.1 0.0 copy-start.7
  104.1 0.0 copy-start.9
  104.1 0.0 copy-start.10
  104.1 0.0 copy-start.11
  104.1 0.0 collective-permute-done.4.partner_weight_ref
  104.2 0.7 shard_map.167
  104.9 1.9 %collective-permute-start.5 = (f32[128,128]{1,0:T(8,128)S(1)}, f32[128,128]{1,0:T(8,128)S(1)}, u32[]{:S(2)}, u32[]{:S(2)}) collective-permute-start(f32[128,128]{1,0:T(8,128)S(1)} %get-tuple-element.39), channel_id=1, source_target_pairs={{0,1},{1,0},{2,3},{3,2},{4,5},{5,4},{6,7},{7,6},{8,9},{9,8},{10,11... | collective-permute-start | bytes 196616 | tf_op jit(solution)/shard_map/ppermute | solution.py:268
  106.8 0.0 copy-done.14
  106.8 1.2 %collective-permute-done.5 = f32[128,128]{1,0:T(8,128)S(1)} collective-permute-done((f32[128,128]{1,0:T(8,128)S(1)}, f32[128,128]{1,0:T(8,128)S(1)}, u32[]{:S(2)}, u32[]{:S(2)}) %collective-permute-start.5) | collective-permute-done | bytes 65568 | tf_op jit(solution)/shard_map/ppermute | solution.py:268
  108.0 0.6 fusion
  108.7 0.1 broadcast_in_dim.21.fixes_ref
  108.8 0.8 shard_map.168
  109.5 4.1 %all-to-all-done.3 = bf16[16,8,1024]{2,1,0:T(8,128)(2,1)} async-done(((bf16[16,8,1024]{2,1,0:T(8,128)(2,1)}), bf16[16,8,1024]{2,1,0:T(8,128)(2,1)}, u32[]{:S(2)}, u32[]{:S(2)}) %all-to-all-start.3) | async-done | bytes 262176 | tf_op jit(solution)/shard_map/all_to_all | solution.py:44
  113.7 2.4 %multiply_subtract_fusion = (f32[128,1024]{1,0:T(8,128)}, f32[128,1024]{1,0:T(8,128)}) fusion(f32[128,1024]{1,0:T(8,128)} %param.23, bf16[16,8,1024]{2,1,0:T(8,128)(2,1)} %all-to-all-done.3, f32[128,1024]{1,0:T(8,128)} %param.24), kind=kLoop, calls=%fused_computation.1 | loop fusion | flops 1179648 | bytes 2359296 | tf_op jit(solution)/shard_map/sub | solution.py:201
  (14 shorter events, 0.0 us)
Async XLA Ops:
  5.2 13.8 %copy-start = (bf16[128,4096]{1,0:T(8,128)(2,1)S(1)}, bf16[128,4096]{1,0:T(8,128)(2,1)}, u32[]{:S(2)}) copy-start(bf16[128,4096]{1,0:T(8,128)(2,1)} %get-tuple-element.35.keep_ref) | copy-start | bytes 3145732
  5.2 13.8 %collective-permute-start = (bf16[128,4224]{1,0:T(8,128)(2,1)}, bf16[128,4224]{1,0:T(8,128)(2,1)S(1)}, u32[]{:S(2)}, u32[]{:S(2)}) collective-permute-start(bf16[128,4224]{1,0:T(8,128)(2,1)} %get-tuple-element.26), channel_id=1, source_target_pairs={{0,1},{1,0},{2,3},{3,2},{4,5},{5,4},{6,7},{7,6},{8,9},{9,8},{10,11... | collective-permute-start | bytes 3244040 | tf_op jit(solution)/shard_map/ppermute | solution.py:242
  7.3 42.9 %all-to-all-start = ((bf16[16,128,128]{2,1,0:T(8,128)(2,1)}), bf16[16,128,128]{2,1,0:T(8,128)(2,1)S(1)}, u32[]{:S(2)}, u32[]{:S(2)}) async-start(bf16[16,128,128]{2,1,0:T(8,128)(2,1)} %get-tuple-element.37), calls=%async_computation | async-start | bytes 1048576 | tf_op jit(solution)/shard_map/all_to_all | solution.py:44
  19.0 0.8 copy-start.8
  19.7 13.8 %copy-start.12 = (f32[1,128,1024]{2,1,0:T(8,128)S(1)}, f32[1,128,1024]{2,1,0:T(8,128)}, u32[]{:S(2)}) copy-start(f32[1,128,1024]{2,1,0:T(8,128)} %param.22) | copy-start | bytes 1572868
  20.1 19.9 %collective-permute-start.1 = (bf16[8,128,128]{2,1,0:T(8,128)(2,1)S(1)}, bf16[8,128,128]{2,1,0:T(8,128)(2,1)S(1)}, u32[]{:S(2)}, u32[]{:S(2)}) collective-permute-start(bf16[8,128,128]{2,1,0:T(8,128)(2,1)S(1)} %get-tuple-element.29), channel_id=1, source_target_pairs={{0,8},{2,10},{4,12},{6,14},{32,40},{34,42},{36,44},{38,46},{8,0},{... | collective-permute-start | bytes 786440 | tf_op jit(solution)/shard_map/ppermute | solution.py:250
  27.0 18.6 %collective-permute-start.2 = (bf16[8,128,128]{2,1,0:T(8,128)(2,1)S(1)}, bf16[8,128,128]{2,1,0:T(8,128)(2,1)S(1)}, u32[]{:S(2)}, u32[]{:S(2)}) collective-permute-start(bf16[8,128,128]{2,1,0:T(8,128)(2,1)S(1)} %get-tuple-element.30), channel_id=1, source_target_pairs={{0,16},{2,18},{4,20},{6,22},{32,48},{34,50},{36,52},{38,54},{8,24}... | collective-permute-start | bytes 786440 | tf_op jit(solution)/shard_map/ppermute | solution.py:250
  31.6 17.8 %collective-permute-start.3 = (bf16[8,128,128]{2,1,0:T(8,128)(2,1)S(1)}, bf16[8,128,128]{2,1,0:T(8,128)(2,1)S(1)}, u32[]{:S(2)}, u32[]{:S(2)}) collective-permute-start(bf16[8,128,128]{2,1,0:T(8,128)(2,1)S(1)} %get-tuple-element.31), channel_id=1, source_target_pairs={{0,24},{2,26},{4,28},{6,30},{32,56},{34,58},{36,60},{38,62},{8,16}... | collective-permute-start | bytes 786440 | tf_op jit(solution)/shard_map/ppermute | solution.py:250
  45.6 0.7 copy-start.1
  49.4 0.7 copy-start.3
  50.1 26.2 %all-to-all-start.2 = ((bf16[16,8,1024]{2,1,0:T(8,128)(2,1)}), bf16[16,8,1024]{2,1,0:T(8,128)(2,1)}, u32[]{:S(2)}, u32[]{:S(2)}) async-start(bf16[16,8,1024]{2,1,0:T(8,128)(2,1)} %convert_bitcast_fusion), calls=%async_computation.2 | async-start | bytes 524288 | tf_op jit(solution)/shard_map/all_to_all | solution.py:44
  64.4 39.7 %collective-permute-start.4 = (bf16[16,128,128]{2,1,0:T(8,128)(2,1)S(1)}, bf16[16,128,128]{2,1,0:T(8,128)(2,1)S(1)}, u32[]{:S(2)}, u32[]{:S(2)}) collective-permute-start(bf16[16,128,128]{2,1,0:T(8,128)(2,1)S(1)} %all-to-all-done.own_weight_ref), channel_id=1, source_target_pairs={{0,8},{2,10},{4,12},{6,14},{32,40},{34,42},{36,44},{38,46},{8,0},{... | collective-permute-start | bytes 1572872 | tf_op jit(solution)/shard_map/ppermute | solution.py:253
  66.3 1.0 copy-start.2
  67.3 0.9 copy-start.4
  76.3 21.4 %all-to-all-start.1 = ((bf16[8,128,128]{2,1,0:T(8,128)(2,1)}), bf16[8,128,128]{2,1,0:T(8,128)(2,1)S(1)}, u32[]{:S(2)}, u32[]{:S(2)}) async-start(bf16[8,128,128]{2,1,0:T(8,128)(2,1)} %shard_map.166), calls=%async_computation.1 | async-start | bytes 524288 | tf_op jit(solution)/shard_map/all_to_all | solution.py:44
  98.5 15.2 %all-to-all-start.3 = ((bf16[16,8,1024]{2,1,0:T(8,128)(2,1)}), bf16[16,8,1024]{2,1,0:T(8,128)(2,1)}, u32[]{:S(2)}, u32[]{:S(2)}) async-start(bf16[16,8,1024]{2,1,0:T(8,128)(2,1)} %broadcast_in_dim.23), calls=%async_computation.3 | async-start | bytes 524288 | tf_op jit(solution)/shard_map/all_to_all | solution.py:44
  104.0 2.8 %copy-start.14 = (f32[2,1]{0,1:T(1,128)S(1)}, f32[2,1]{0,1:T(1,128)}, u32[]{:S(2)}) copy-start(f32[2,1]{0,1:T(1,128)} %constant.14.clone) | copy-start | bytes 28
  104.1 4.0 %copy-start.13 = (f32[128,128]{1,0:T(8,128)S(1)}, f32[128,128]{1,0:T(8,128)}, u32[]{:S(2)}) copy-start(f32[128,128]{1,0:T(8,128)} %get-tuple-element.40) | copy-start | bytes 196612
  104.1 4.7 %copy-start.5 = (bf16[1,128,128]{2,1,0:T(8,128)(2,1)S(1)}, bf16[1,128,128]{2,1,0:T(8,128)(2,1)}, u32[]{:S(2)}) copy-start(bf16[1,128,128]{2,1,0:T(8,128)(2,1)} %param.15) | copy-start | bytes 98308
  104.1 4.6 %copy-start.6 = (f32[1,128,128]{2,1,0:T(8,128)S(1)}, f32[1,128,128]{2,1,0:T(8,128)}, u32[]{:S(2)}) copy-start(f32[1,128,128]{2,1,0:T(8,128)} %param.18) | copy-start | bytes 196612
  104.1 4.6 %copy-start.7 = (f32[1,128,128]{2,1,0:T(8,128)S(1)}, f32[1,128,128]{2,1,0:T(8,128)}, u32[]{:S(2)}) copy-start(f32[1,128,128]{2,1,0:T(8,128)} %param.19) | copy-start | bytes 196612
  104.1 4.6 %copy-start.9 = (bf16[1,128]{1,0:T(2,128)(2,1)S(1)}, bf16[1,128]{1,0:T(2,128)(2,1)}, u32[]{:S(2)}) copy-start(bf16[1,128]{1,0:T(2,128)(2,1)} %gain_ref.3) | copy-start | bytes 772
  104.1 4.6 %copy-start.10 = (f32[1,128]{1,0:T(1,128)S(1)}, f32[1,128]{1,0:T(1,128)}, u32[]{:S(2)}) copy-start(f32[1,128]{1,0:T(1,128)} %m_gain_ref.1) | copy-start | bytes 1540
  104.1 4.6 %copy-start.11 = (f32[1,128]{1,0:T(1,128)S(1)}, f32[1,128]{1,0:T(1,128)}, u32[]{:S(2)}) copy-start(f32[1,128]{1,0:T(1,128)} %v_gain_ref.1) | copy-start | bytes 1540
  104.9 3.1 %collective-permute-start.5 = (f32[128,128]{1,0:T(8,128)S(1)}, f32[128,128]{1,0:T(8,128)S(1)}, u32[]{:S(2)}, u32[]{:S(2)}) collective-permute-start(f32[128,128]{1,0:T(8,128)S(1)} %get-tuple-element.39), channel_id=1, source_target_pairs={{0,1},{1,0},{2,3},{3,2},{4,5},{5,4},{6,7},{7,6},{8,9},{9,8},{10,11... | collective-permute-start | bytes 196616 | tf_op jit(solution)/shard_map/ppermute | solution.py:268

commit v5 on v3

--- a/solution.py
+++ b/solution.py
@@ -13,9 +13,9 @@
 
 
 def chip_of(core, four, eight):
-    if core:
-        return eight * FOUR + four
-    return (eight // FOUR * FOUR + four) * FOUR + eight % FOUR
+    row = (2 * (eight // 2) + (four >> 1) + core) & 7
+    column = (2 * (eight % 2) + (four & 1) + core) & 3
+    return row * 4 + column
 
 
 def device_of(core, four, eight):
@@ -52,6 +52,10 @@
     )
 
 
+def part_of(index, head):
+    return pl.BlockSpec((1, EIGHT, head, LANES), lambda i: (index, 0, 0, 0))
+
+
 def lanes_of(block):
     return slice(block * LANES, (block + 1) * LANES)
 
@@ -61,26 +65,29 @@
     cotangent_hbm,
     weight_hbm,
     gain_ref,
-    keep_ref,
-    send_ref,
+    keep_hbm,
+    send_hbm,
     scaled_ref,
     inverse_ref,
     spread_ref,
     tokens_ref,
     cotangent_ref,
     weight_ref,
-    semaphores,
+    keep_ref,
+    send_ref,
+    in_semaphores,
+    out_semaphores,
 ):
     rows, width = tokens_ref.shape
     pieces = 4
     piece = width // pieces
     copies = [
-        pltpu.make_async_copy(weight_hbm, weight_ref, semaphores.at[pieces]),
-        pltpu.make_async_copy(cotangent_hbm, cotangent_ref, semaphores.at[pieces + 1]),
+        pltpu.make_async_copy(weight_hbm, weight_ref, in_semaphores.at[pieces]),
+        pltpu.make_async_copy(cotangent_hbm, cotangent_ref, in_semaphores.at[pieces + 1]),
     ]
     for index in range(pieces):
         part = slice(index * piece, (index + 1) * piece)
-        copies.append(pltpu.make_async_copy(tokens_hbm.at[:, part], tokens_ref.at[:, part], semaphores.at[index]))
+        copies.append(pltpu.make_async_copy(tokens_hbm.at[:, part], tokens_ref.at[:, part], in_semaphores.at[index]))
     for copy in copies:
         copy.start()
 
@@ -90,31 +97,47 @@
     for eight in range(EIGHT):
         spread_ref[eight] = scaled_weight
 
-    total = jnp.zeros((rows, LANES), jnp.float32)
-    for index in range(pieces):
-        copies[2 + index].wait()
+    def squares(index):
+        total = jnp.zeros((rows, LANES), jnp.float32)
         for block in range(index * piece // LANES, (index + 1) * piece // LANES):
             floats = tokens_ref[:, lanes_of(block)].astype(jnp.float32)
             total += floats * floats
+        return total
+
+    total = jnp.zeros((rows, LANES), jnp.float32)
+    for index in range(pieces - 1):
+        copies[2 + index].wait()
+        total += squares(index)
+    copies[1 + pieces].wait()
+
+    device = lax.axis_index("fsdp")
+    core, row, column = device & 1, device >> 3, (device >> 1) & 3
+    out_copies = []
+    for step in range(FOUR):
+        part = slice(step * EIGHT * LANES, (step + 1) * EIGHT * LANES)
+        for target, target_hbm, kind in ((keep_ref, keep_hbm, core), (send_ref, send_hbm, 1 - core)):
+            four = (((row + kind) & 1) * 2 + ((column + kind) & 1)) ^ step
+            for eight in range(EIGHT):
+                start = pl.multiple_of(device_of(kind, four, eight) * LANES, LANES)
+                target[:, lanes_of(step * EIGHT + eight)] = tokens_ref[:, pl.ds(start, LANES)]
+            semaphore = out_semaphores.at[len(out_copies)]
+            out_copies.append(pltpu.make_async_copy(target.at[:, part], target_hbm.at[:, part], semaphore))
+            out_copies[-1].start()
+
+    total += squares(pieces - 1)
     inverse = lax.rsqrt(jnp.sum(total, axis=1, keepdims=True) / width + 1e-05)
     inverse_ref[...] = jnp.broadcast_to(inverse, (rows, LANES))
     copies[1].wait()
     scaled = (cotangent_ref[...].astype(jnp.float32) * inverse).astype(jnp.bfloat16)
     scaled_ref[...] = scaled
-    send_ref[:, lanes_of(FOUR * EIGHT)] = scaled
-
-    device = lax.axis_index("fsdp")
-    core = lax.rem(device, 2)
-    chip = lax.div(device, 2)
-    row, column = lax.div(chip, FOUR), lax.rem(chip, FOUR)
-    fours = (lax.rem(row, FOUR), column)
-    for step in range(FOUR):
-        for eight in range(EIGHT):
-            chips = [chip_of(kind, fours[kind] ^ step, eight) for kind in range(2)]
-            for target, kind in ((keep_ref, core), (send_ref, 1 - core)):
-                source = jnp.where(kind == 0, chips[0], chips[1]) * 2 + kind
-                start = pl.multiple_of(source * LANES, LANES)
-                target[:, lanes_of(step * EIGHT + eight)] = tokens_ref[:, pl.ds(start, LANES)]
+    last = lanes_of(FOUR * EIGHT)
+    send_ref[:, last] = scaled
+    out_copies.append(
+        pltpu.make_async_copy(send_ref.at[:, last], send_hbm.at[:, last], out_semaphores.at[len(out_copies)])
+    )
+    out_copies[-1].start()
+    for copy in out_copies:
+        copy.wait()
 
 
 def gradient_term(keep_ref, arrived_ref, scaled_ref, step):
@@ -138,7 +161,7 @@
     for eight in range(EIGHT):
         total = own[:, lanes_of(eight)]
         for ref in (first_ref, second_ref, third_ref):
-            total += ref[1, eight].astype(jnp.float32)
+            total += ref[0, eight].astype(jnp.float32)
         out_ref[eight] = total.astype(out_ref.dtype)
 
 
@@ -222,11 +245,15 @@
         jax.ShapeDtypeStruct((EIGHT, LANES, head), jnp.bfloat16),
         mebibytes=60,
         in_specs=[hbm, hbm, hbm, pl.BlockSpec(memory_space=pltpu.VMEM)],
+        out_specs=[hbm, hbm] + [pl.BlockSpec(memory_space=pltpu.VMEM)] * 3,
         scratch_shapes=[
             pltpu.VMEM((rows, width), jnp.bfloat16),
             pltpu.VMEM((rows, head), jnp.bfloat16),
             pltpu.VMEM((LANES, head), jnp.bfloat16),
+            pltpu.VMEM((rows, half), jnp.bfloat16),
+            pltpu.VMEM((rows, half + LANES), jnp.bfloat16),
             pltpu.SemaphoreType.DMA((6,)),
+            pltpu.SemaphoreType.DMA((2 * FOUR + 1,)),
         ],
     )(tokens_in[0], value_cotangent[0], value_weight[0], norm_gain)
     arrived = lax.ppermute(send, "fsdp", SWAP_CORES)
@@ -245,16 +272,22 @@
     scaled, frag_sum = lax.optimization_barrier((scaled, frag_sum))
     local_sum = spread(frag_sum, replicas, "rep")
 
-    (summed,) = call(add_kernel, jax.ShapeDtypeStruct((EIGHT, head, LANES), jnp.bfloat16))(
-        keep, arrived, scaled, *incoming
-    )
+    whole = pl.BlockSpec(memory_space=pltpu.VMEM)
+    (summed,) = call(
+        add_kernel,
+        jax.ShapeDtypeStruct((EIGHT, head, LANES), jnp.bfloat16),
+        grid=(1,),
+        in_specs=[whole] * 3 + [part_of(1, head)] * (FOUR - 1),
+    )(keep, arrived, scaled, *incoming)
     summed, local_sum = lax.optimization_barrier((summed, local_sum))
     scattered = exchange(summed, "fsdp", EIGHT_GROUPS)
     local_mean = local_sum.reshape(frag_shape).astype(jnp.float32) / replicas
     new_global, new_moment = outer_update(frag_global, frag_moment, local_mean)
 
     partial = jax.ShapeDtypeStruct((rows, head), jnp.float32)
-    own_part, other_part = call(values_kernel, partial, partial)(keep, arrived, weight, *incoming)
+    own_part, other_part = call(
+        values_kernel, partial, partial, grid=(1,), in_specs=[whole] * 3 + [part_of(0, head)] * (FOUR - 1)
+    )(keep, arrived, weight, *incoming)
     arrived_part = lax.ppermute(other_part, "fsdp", SWAP_CORES)
     values = ((own_part + arrived_part) * inverse_rms).astype(jnp.bfloat16)
 

time: 110 us -> 112 us (1.018)
  the two profiles are of different devices: /device:TPU:18 before, /device:TPU:8 now
where the time goes in v5:
time: 112 us; the launch traced here: 111 us
  starting transfers between devices  64.8 us (58%)
  waiting for transfers between devices  27 us (24%)
  Pallas kernels  10.8 us (10%)
  other arithmetic  5.58 us (5%)
  local copies, waits for them, and re-layouts  1.66 us (1%)
  between operations  1.48 us (1%)
    all_to_all x4, starting transfers between devices, exchange(): lax.all_to_all(blocks, axis, 0, 0, axis_index_groups=groups, tiled=True)  48.8 us
    all_to_all x4, waiting for transfers between devices, exchange(): lax.all_to_all(blocks, axis, 0, 0, axis_index_groups=groups, tiled=True)  18.3 us
    ppermute x3, starting transfers between devices, local(): lax.ppermute(blocks, 'fsdp', four_pairs(step))  10.1 us
    ppermute x3, waiting for transfers between devices, local(): lax.ppermute(blocks, 'fsdp', four_pairs(step))  8.68 us
    pallas_call x1, Pallas kernels, local(): call(split_kernel, jax.ShapeDtypeStruct((rows, half), jnp.bfloat16), jax....  4.65 us
    ppermute x1, starting transfers between devices, local(): arrived_part = lax.ppermute(other_part, 'fsdp', SWAP_CORES)  3.84 us
    sub x1, other arithmetic, outer_update(): return (global_params - 0.7 * (delta + 0.9 * moment_new), moment_new)  2.33 us
    pallas_call x1, Pallas kernels, local(): call(values_kernel, partial, partial, grid=(1,), in_specs=[whole] * 3 + [...  2.28 us
  transfers between devices with their start and end apart: 9, of which 4 were waited for; matrix products, arithmetic and copies ran while one was open for 6% of the time, Pallas kernels for 4%

profile of v5, /device:TPU:8, one launch (start us, length us, event | category | flops | bytes accessed | tf_op | source)
XLA Modules:
  0.0 111.3 jit_solution(16105525210652245097)
XLA Ops:
  0.6 0.0 copy-start.10
  0.6 4.6 %shard_map.164 = (bf16[128,4096]{1,0:T(8,128)(2,1)}, bf16[128,4224]{1,0:T(8,128)(2,1)}, bf16[128,128]{1,0:T(8,128)(2,1)}, f32[128,128]{1,0:T(8,128)}, bf16[8,128,128]{2,1,0:T(8,128)(2,1)}) custom-call(bf16[128,8192]{1,0:T(8,128)(2,1)} %bitcast.23, bf16[128,128]{1,0:T(8,128)(2,1)} %bitcast.24, bf16[128,128]{1,0:T(8,128)(2,1)} %bitcast.19, bf16[1,128]{1,0:T(2,128)(2,1)} %gain_ref.3), custom_call_target="tpu_custom_call" | custom-call | tf_op jit(solution)/shard_map/pallas_call | solution.py:239
  5.3 0.0 copy-start
  5.3 0.0 copy-start.4
  5.3 2.1 %collective-permute-start = (bf16[128,4224]{1,0:T(8,128)(2,1)}, bf16[128,4224]{1,0:T(8,128)(2,1)S(1)}, u32[]{:S(2)}, u32[]{:S(2)}) collective-permute-start(bf16[128,4224]{1,0:T(8,128)(2,1)} %get-tuple-element.25), channel_id=1, source_target_pairs={{0,1},{1,0},{2,3},{3,2},{4,5},{5,4},{6,7},{7,6},{8,9},{9,8},{10,11... | collective-permute-start | bytes 3244040 | tf_op jit(solution)/shard_map/ppermute | solution.py:259
  7.4 16.4 %all-to-all-start = ((bf16[8,128,128]{2,1,0:T(8,128)(2,1)}), bf16[8,128,128]{2,1,0:T(8,128)(2,1)S(1)}, u32[]{:S(2)}, u32[]{:S(2)}) async-start(bf16[8,128,128]{2,1,0:T(8,128)(2,1)} %get-tuple-element.26), calls=%async_computation | async-start | bytes 524288 | tf_op jit(solution)/shard_map/all_to_all | solution.py:39
  23.8 0.0 copy-done.10
  23.8 0.7 convert_bitcast_fusion
  24.6 8.4 %all-to-all-done.weight_ref = bf16[8,128,128]{2,1,0:T(8,128)(2,1)S(1)} async-done(((bf16[8,128,128]{2,1,0:T(8,128)(2,1)}), bf16[8,128,128]{2,1,0:T(8,128)(2,1)S(1)}, u32[]{:S(2)}, u32[]{:S(2)}) %all-to-all-start) | async-done | bytes 262176 | tf_op jit(solution)/shard_map/all_to_all | solution.py:39
  33.0 0.0 collective-permute-done.arrived_ref
  33.0 0.0 copy-done
  33.0 0.0 copy-done.4
  33.0 1.2 %shard_map.165 = (bf16[128,128]{1,0:T(8,128)(2,1)S(1)}, bf16[2,8,128,128]{3,2,1,0:T(8,128)(2,1)}, bf16[2,8,128,128]{3,2,1,0:T(8,128)(2,1)S(1)}, bf16[2,8,128,128]{3,2,1,0:T(8,128)(2,1)S(1)}) custom-call(bf16[128,4096]{1,0:T(8,128)(2,1)S(1)} %copy-done, bf16[128,4224]{1,0:T(8,128)(2,1)S(1)} %collective-permute-done.arrived_ref, ...), custom_call_target="tpu_custom_call" | custom-call | tf_op jit(solution)/shard_map/pallas_call | solution.py:262
  34.2 0.8 copy-done.9
  35.0 14.9 %all-to-all-start.1 = ((bf16[16,8,1024]{2,1,0:T(8,128)(2,1)}), bf16[16,8,1024]{2,1,0:T(8,128)(2,1)}, u32[]{:S(2)}, u32[]{:S(2)}) async-start(bf16[16,8,1024]{2,1,0:T(8,128)(2,1)} %convert_bitcast_fusion), calls=%async_computation.1 | async-start | bytes 524288 | tf_op jit(solution)/shard_map/all_to_all | solution.py:39
  49.9 0.0 copy-done.8
  49.9 2.5 %collective-permute-start.1 = (bf16[2,8,128,128]{3,2,1,0:T(8,128)(2,1)}, bf16[2,8,128,128]{3,2,1,0:T(8,128)(2,1)S(1)}, u32[]{:S(2)}, u32[]{:S(2)}) collective-permute-start(bf16[2,8,128,128]{3,2,1,0:T(8,128)(2,1)} %get-tuple-element.28), channel_id=1, source_target_pairs={{0,2},{4,6},{16,18},{20,22},{32,34},{36,38},{48,50},{52,54},{2,0},... | collective-permute-start | bytes 1572872 | tf_op jit(solution)/shard_map/ppermute | solution.py:269
  52.4 3.9 %collective-permute-start.2 = (bf16[2,8,128,128]{3,2,1,0:T(8,128)(2,1)}, bf16[2,8,128,128]{3,2,1,0:T(8,128)(2,1)S(1)}, u32[]{:S(2)}, u32[]{:S(2)}) collective-permute-start(bf16[2,8,128,128]{3,2,1,0:T(8,128)(2,1)} %copy-done.9), channel_id=1, source_target_pairs={{0,8},{4,12},{16,24},{20,28},{32,40},{36,44},{48,56},{52,60},{2,10... | collective-permute-start | bytes 1572872 | tf_op jit(solution)/shard_map/ppermute | solution.py:269
  56.3 3.7 %collective-permute-start.3 = (bf16[2,8,128,128]{3,2,1,0:T(8,128)(2,1)}, bf16[2,8,128,128]{3,2,1,0:T(8,128)(2,1)}, u32[]{:S(2)}, u32[]{:S(2)}) collective-permute-start(bf16[2,8,128,128]{3,2,1,0:T(8,128)(2,1)} %copy-done.8), channel_id=1, source_target_pairs={{0,10},{4,14},{16,26},{20,30},{32,42},{36,46},{48,58},{52,62},{2,8... | collective-permute-start | bytes 1572872 | tf_op jit(solution)/shard_map/ppermute | solution.py:269
  60.0 1.5 %all-to-all-done.1 = bf16[16,8,1024]{2,1,0:T(8,128)(2,1)} async-done(((bf16[16,8,1024]{2,1,0:T(8,128)(2,1)}), bf16[16,8,1024]{2,1,0:T(8,128)(2,1)}, u32[]{:S(2)}, u32[]{:S(2)}) %all-to-all-start.1) | async-done | bytes 262176 | tf_op jit(solution)/shard_map/all_to_all | solution.py:39
  61.5 1.0 reduce_sum.12
  62.5 0.7 broadcast_in_dim.20
  63.2 6.7 %all-to-all-start.2 = ((bf16[16,8,1024]{2,1,0:T(8,128)(2,1)}), bf16[16,8,1024]{2,1,0:T(8,128)(2,1)}, u32[]{:S(2)}, u32[]{:S(2)}) async-start(bf16[16,8,1024]{2,1,0:T(8,128)(2,1)} %broadcast_in_dim.20), calls=%async_computation.2 | async-start | bytes 524288 | tf_op jit(solution)/shard_map/all_to_all | solution.py:39
  70.5 0.0 copy-start.12
  70.6 0.0 collective-permute-done.1.first_ref
  70.6 0.0 collective-permute-done.2.second_ref
  70.6 8.7 %collective-permute-done.3.third_ref = bf16[2,8,128,128]{3,2,1,0:T(8,128)(2,1)} collective-permute-done((bf16[2,8,128,128]{3,2,1,0:T(8,128)(2,1)}, bf16[2,8,128,128]{3,2,1,0:T(8,128)(2,1)}, u32[]{:S(2)}, u32[]{:S(2)}) %collective-permute-start.3) | collective-permute-done | bytes 524320 | tf_op jit(solution)/shard_map/ppermute | solution.py:269
  79.2 2.3 %shard_map.166 = (f32[128,128]{1,0:T(8,128)S(1)}, f32[128,128]{1,0:T(8,128)}) custom-call(bf16[128,4096]{1,0:T(8,128)(2,1)S(1)} %copy-done, bf16[128,4224]{1,0:T(8,128)(2,1)S(1)} %collective-permute-done.arrived_ref, bf16[8,128,128]{2,1,0:T(8,128)(2,1)S(1)} %all-to-all-done.weight_ref, bf16[2,8,128,128]{3,2,1,0:T(8,128)(2,1)S(1)} %collective-permute-done.1.first_ref, ...), custom_call_target="tpu_custom_call" | custom-call | tf_op jit(solution)/shard_map/pallas_call | solution.py:288
  81.5 3.8 %collective-permute-start.4 = (f32[128,128]{1,0:T(8,128)}, f32[128,128]{1,0:T(8,128)}, u32[]{:S(2)}, u32[]{:S(2)}) collective-permute-start(f32[128,128]{1,0:T(8,128)} %get-tuple-element.32), channel_id=1, source_target_pairs={{0,1},{1,0},{2,3},{3,2},{4,5},{5,4},{6,7},{7,6},{8,9},{9,8},{10,11... | collective-permute-start | bytes 196616 | tf_op jit(solution)/shard_map/ppermute | solution.py:291
  85.4 0.0 copy-done.12
  85.4 2.0 %shard_map.167 = bf16[8,128,128]{2,1,0:T(8,128)(2,1)} custom-call(bf16[128,4096]{1,0:T(8,128)(2,1)S(1)} %copy-done, bf16[128,4224]{1,0:T(8,128)(2,1)S(1)} %collective-permute-done.arrived_ref, bf16[128,128]{1,0:T(8,128)(2,1)S(1)} %get-tuple-element.37.scaled_ref, bf16[2,8,128,128]{3,2,1,0:T(8,128)(2,1)S(1)} %collective-permute-done.1.first_ref, ...), custom_call_target="tpu_custom_call" | custom-call | tf_op jit(solution)/shard_map/pallas_call | solution.py:276
  87.4 0.0 all-to-all-done.2
  87.4 10.8 %all-to-all-start.3 = ((bf16[8,128,128]{2,1,0:T(8,128)(2,1)}), bf16[8,128,128]{2,1,0:T(8,128)(2,1)S(1)}, u32[]{:S(2)}, u32[]{:S(2)}) async-start(bf16[8,128,128]{2,1,0:T(8,128)(2,1)} %shard_map.167), calls=%async_computation.3 | async-start | bytes 524288 | tf_op jit(solution)/shard_map/all_to_all | solution.py:39
  98.1 0.0 collective-permute-done.4
  98.2 1.5 %fusion = bf16[1,128,128]{2,1,0:T(8,128)(2,1)} fusion(f32[128,128]{1,0:T(8,128)} %get-tuple-element.33, f32[128,128]{1,0:T(8,128)S(1)} %get-tuple-element.31, f32[128,128]{1,0:T(8,128)} %collective-permute-done.4), kind=kLoop, calls=%fused_computation.5 | loop fusion | flops 49152 | bytes 229376 | tf_op jit(solution)/shard_map/broadcast_in_dim | solution.py:310
  99.7 0.0 copy-done.11
  99.7 0.0 copy-start.5
  99.7 0.0 copy-start.6
  99.7 0.0 copy-start.7
  99.7 2.3 %multiply_subtract_fusion = (f32[128,1024]{1,0:T(8,128)}, f32[128,1024]{1,0:T(8,128)}) fusion(f32[128,1024]{1,0:T(8,128)S(1)} %copy-done.11, bf16[16,8,1024]{2,1,0:T(8,128)(2,1)} %all-to-all-done.2, f32[128,1024]{1,0:T(8,128)} %param.24), kind=kLoop, calls=%fused_computation.1 | loop fusion | flops 1179648 | bytes 2359296 | tf_op jit(solution)/shard_map/sub | solution.py:214
  102.0 8.4 %all-to-all-done.3.terms_ref = bf16[8,128,128]{2,1,0:T(8,128)(2,1)S(1)} async-done(((bf16[8,128,128]{2,1,0:T(8,128)(2,1)}), bf16[8,128,128]{2,1,0:T(8,128)(2,1)S(1)}, u32[]{:S(2)}, u32[]{:S(2)}) %all-to-all-start.3) | async-done | bytes 262176 | tf_op jit(solution)/shard_map/all_to_all | solution.py:39
  110.4 0.1 broadcast_in_dim.22.fixes_ref
  110.5 0.0 copy-done.1
  110.5 0.0 copy-done.2
  110.5 0.0 copy-done.3
  110.5 0.0 copy-done.5
  110.5 0.0 copy-done.6
  110.5 0.8 shard_map.168
  (8 shorter events, 0.0 us)
Async XLA Ops:
  0.6 23.2 %copy-start.10 = (f32[1,128,1024]{2,1,0:T(8,128)S(1)}, f32[1,128,1024]{2,1,0:T(8,128)}, u32[]{:S(2)}) copy-start(f32[1,128,1024]{2,1,0:T(8,128)} %param.22) | copy-start | bytes 1572868
  5.3 27.7 %copy-start = (bf16[128,4096]{1,0:T(8,128)(2,1)S(1)}, bf16[128,4096]{1,0:T(8,128)(2,1)}, u32[]{:S(2)}) copy-start(bf16[128,4096]{1,0:T(8,128)(2,1)} %get-tuple-element.24.keep_ref) | copy-start | bytes 3145732
  5.3 27.7 %copy-start.4 = (bf16[128,128]{1,0:T(8,128)(2,1)S(1)}, bf16[128,128]{1,0:T(8,128)(2,1)}, u32[]{:S(2)}) copy-start(bf16[128,128]{1,0:T(8,128)(2,1)} %get-tuple-element.27.scaled_ref) | copy-start | bytes 98308
  5.3 27.6 %collective-permute-start = (bf16[128,4224]{1,0:T(8,128)(2,1)}, bf16[128,4224]{1,0:T(8,128)(2,1)S(1)}, u32[]{:S(2)}, u32[]{:S(2)}) collective-permute-start(bf16[128,4224]{1,0:T(8,128)(2,1)} %get-tuple-element.25), channel_id=1, source_target_pairs={{0,1},{1,0},{2,3},{3,2},{4,5},{5,4},{6,7},{7,6},{8,9},{9,8},{10,11... | collective-permute-start | bytes 3244040 | tf_op jit(solution)/shard_map/ppermute | solution.py:259
  7.4 25.6 %all-to-all-start = ((bf16[8,128,128]{2,1,0:T(8,128)(2,1)}), bf16[8,128,128]{2,1,0:T(8,128)(2,1)S(1)}, u32[]{:S(2)}, u32[]{:S(2)}) async-start(bf16[8,128,128]{2,1,0:T(8,128)(2,1)} %get-tuple-element.26), calls=%async_computation | async-start | bytes 524288 | tf_op jit(solution)/shard_map/all_to_all | solution.py:39
  34.2 0.8 copy-start.9
  35.0 14.9 %copy-start.8 = (bf16[2,8,128,128]{3,2,1,0:T(8,128)(2,1)}, bf16[2,8,128,128]{3,2,1,0:T(8,128)(2,1)S(1)}, u32[]{:S(2)}) copy-start(bf16[2,8,128,128]{3,2,1,0:T(8,128)(2,1)S(1)} %get-tuple-element.30) | copy-start | bytes 1572868
  35.0 26.5 %all-to-all-start.1 = ((bf16[16,8,1024]{2,1,0:T(8,128)(2,1)}), bf16[16,8,1024]{2,1,0:T(8,128)(2,1)}, u32[]{:S(2)}, u32[]{:S(2)}) async-start(bf16[16,8,1024]{2,1,0:T(8,128)(2,1)} %convert_bitcast_fusion), calls=%async_computation.1 | async-start | bytes 524288 | tf_op jit(solution)/shard_map/all_to_all | solution.py:39
  49.9 20.7 %collective-permute-start.1 = (bf16[2,8,128,128]{3,2,1,0:T(8,128)(2,1)}, bf16[2,8,128,128]{3,2,1,0:T(8,128)(2,1)S(1)}, u32[]{:S(2)}, u32[]{:S(2)}) collective-permute-start(bf16[2,8,128,128]{3,2,1,0:T(8,128)(2,1)} %get-tuple-element.28), channel_id=1, source_target_pairs={{0,2},{4,6},{16,18},{20,22},{32,34},{36,38},{48,50},{52,54},{2,0},... | collective-permute-start | bytes 1572872 | tf_op jit(solution)/shard_map/ppermute | solution.py:269
  52.4 18.2 %collective-permute-start.2 = (bf16[2,8,128,128]{3,2,1,0:T(8,128)(2,1)}, bf16[2,8,128,128]{3,2,1,0:T(8,128)(2,1)S(1)}, u32[]{:S(2)}, u32[]{:S(2)}) collective-permute-start(bf16[2,8,128,128]{3,2,1,0:T(8,128)(2,1)} %copy-done.9), channel_id=1, source_target_pairs={{0,8},{4,12},{16,24},{20,28},{32,40},{36,44},{48,56},{52,60},{2,10... | collective-permute-start | bytes 1572872 | tf_op jit(solution)/shard_map/ppermute | solution.py:269
  56.3 22.9 %collective-permute-start.3 = (bf16[2,8,128,128]{3,2,1,0:T(8,128)(2,1)}, bf16[2,8,128,128]{3,2,1,0:T(8,128)(2,1)}, u32[]{:S(2)}, u32[]{:S(2)}) collective-permute-start(bf16[2,8,128,128]{3,2,1,0:T(8,128)(2,1)} %copy-done.8), channel_id=1, source_target_pairs={{0,10},{4,14},{16,26},{20,30},{32,42},{36,46},{48,58},{52,62},{2,8... | collective-permute-start | bytes 1572872 | tf_op jit(solution)/shard_map/ppermute | solution.py:269
  63.2 24.1 %all-to-all-start.2 = ((bf16[16,8,1024]{2,1,0:T(8,128)(2,1)}), bf16[16,8,1024]{2,1,0:T(8,128)(2,1)}, u32[]{:S(2)}, u32[]{:S(2)}) async-start(bf16[16,8,1024]{2,1,0:T(8,128)(2,1)} %broadcast_in_dim.20), calls=%async_computation.2 | async-start | bytes 524288 | tf_op jit(solution)/shard_map/all_to_all | solution.py:39
  70.5 14.8 %copy-start.12 = (f32[2,1]{0,1:T(1,128)S(1)}, f32[2,1]{0,1:T(1,128)}, u32[]{:S(2)}) copy-start(f32[2,1]{0,1:T(1,128)} %constant.14.clone) | copy-start | bytes 28
  81.5 16.6 %collective-permute-start.4 = (f32[128,128]{1,0:T(8,128)}, f32[128,128]{1,0:T(8,128)}, u32[]{:S(2)}, u32[]{:S(2)}) collective-permute-start(f32[128,128]{1,0:T(8,128)} %get-tuple-element.32), channel_id=1, source_target_pairs={{0,1},{1,0},{2,3},{3,2},{4,5},{5,4},{6,7},{7,6},{8,9},{9,8},{10,11... | collective-permute-start | bytes 196616 | tf_op jit(solution)/shard_map/ppermute | solution.py:291
  87.4 12.3 %copy-start.11 = (f32[128,1024]{1,0:T(8,128)S(1)}, f32[128,1024]{1,0:T(8,128)}, u32[]{:S(2)}) copy-start(f32[128,1024]{1,0:T(8,128)} %param.23) | copy-start | bytes 1572868
  87.4 23.1 %all-to-all-start.3 = ((bf16[8,128,128]{2,1,0:T(8,128)(2,1)}), bf16[8,128,128]{2,1,0:T(8,128)(2,1)S(1)}, u32[]{:S(2)}, u32[]{:S(2)}) async-start(bf16[8,128,128]{2,1,0:T(8,128)(2,1)} %shard_map.167), calls=%async_computation.3 | async-start | bytes 524288 | tf_op jit(solution)/shard_map/all_to_all | solution.py:39
  99.7 10.9 %copy-start.1 = (bf16[1,128,128]{2,1,0:T(8,128)(2,1)S(1)}, bf16[1,128,128]{2,1,0:T(8,128)(2,1)}, u32[]{:S(2)}) copy-start(bf16[1,128,128]{2,1,0:T(8,128)(2,1)} %param.15) | copy-start | bytes 98308
  99.7 10.9 %copy-start.2 = (f32[1,128,128]{2,1,0:T(8,128)S(1)}, f32[1,128,128]{2,1,0:T(8,128)}, u32[]{:S(2)}) copy-start(f32[1,128,128]{2,1,0:T(8,128)} %param.18) | copy-start | bytes 196612
  99.7 10.9 %copy-start.3 = (f32[1,128,128]{2,1,0:T(8,128)S(1)}, f32[1,128,128]{2,1,0:T(8,128)}, u32[]{:S(2)}) copy-start(f32[1,128,128]{2,1,0:T(8,128)} %param.19) | copy-start | bytes 196612
  99.7 10.9 %copy-start.5 = (bf16[1,128]{1,0:T(2,128)(2,1)S(1)}, bf16[1,128]{1,0:T(2,128)(2,1)}, u32[]{:S(2)}) copy-start(bf16[1,128]{1,0:T(2,128)(2,1)} %gain_ref.3) | copy-start | bytes 772
  99.7 10.8 %copy-start.6 = (f32[1,128]{1,0:T(1,128)S(1)}, f32[1,128]{1,0:T(1,128)}, u32[]{:S(2)}) copy-start(f32[1,128]{1,0:T(1,128)} %m_gain_ref.1) | copy-start | bytes 1540
  99.7 10.8 %copy-start.7 = (f32[1,128]{1,0:T(1,128)S(1)}, f32[1,128]{1,0:T(1,128)}, u32[]{:S(2)}) copy-start(f32[1,128]{1,0:T(1,128)} %v_gain_ref.1) | copy-start | bytes 1540

commit v6 on v5

--- a/solution.py
+++ b/solution.py
@@ -9,6 +9,7 @@
 
 EIGHT = 8
 FOUR = 4
+ALONG_X, ALONG_Y = 1, 2
 LANES = 128
 
 
@@ -50,10 +51,6 @@
         **specs,
         compiler_params=pltpu.CompilerParams(vmem_limit_bytes=mebibytes * 1024 * 1024),
     )
-
-
-def part_of(index, head):
-    return pl.BlockSpec((1, EIGHT, head, LANES), lambda i: (index, 0, 0, 0))
 
 
 def lanes_of(block):
@@ -147,33 +144,37 @@
     return lax.dot_general(cotangents, both, (((0,), (0,)), ((), ())), preferred_element_type=jnp.float32)
 
 
-def outgoing_kernel(keep_ref, arrived_ref, scaled_ref, weight_ref, again_ref, *out_refs):
-    again_ref[...] = scaled_ref[...]
-    for step, out_ref in enumerate(out_refs, 1):
-        term = gradient_term(keep_ref, arrived_ref, scaled_ref, step)
+def first_kernel(keep_ref, arrived_ref, scaled_ref, out_ref):
+    for index in range(2):
+        term = gradient_term(keep_ref, arrived_ref, scaled_ref, ALONG_Y + index)
         for eight in range(EIGHT):
-            out_ref[0, eight] = weight_ref[eight]
-            out_ref[1, eight] = term[:, lanes_of(eight)].astype(jnp.bfloat16)
-
-
-def add_kernel(keep_ref, arrived_ref, scaled_ref, first_ref, second_ref, third_ref, out_ref):
-    own = gradient_term(keep_ref, arrived_ref, scaled_ref, 0)
+            out_ref[index, eight] = term[:, lanes_of(eight)].astype(jnp.bfloat16)
+
+
+def second_kernel(keep_ref, arrived_ref, scaled_ref, first_ref, weight_ref, x_weight_ref, out_ref, weights_ref):
+    term = gradient_term(keep_ref, arrived_ref, scaled_ref, ALONG_X)
     for eight in range(EIGHT):
-        total = own[:, lanes_of(eight)]
-        for ref in (first_ref, second_ref, third_ref):
-            total += ref[0, eight].astype(jnp.float32)
-        out_ref[eight] = total.astype(out_ref.dtype)
-
-
-def values_kernel(keep_ref, arrived_ref, weight_ref, first_ref, second_ref, third_ref, own_ref, other_ref):
+        out_ref[eight] = (term[:, lanes_of(eight)] + first_ref[1, eight].astype(jnp.float32)).astype(jnp.bfloat16)
+        weights_ref[0, eight] = weight_ref[eight]
+        weights_ref[1, eight] = x_weight_ref[eight]
+
+
+def third_kernel(keep_ref, arrived_ref, scaled_ref, first_ref, second_ref, out_ref):
+    term = gradient_term(keep_ref, arrived_ref, scaled_ref, 0)
+    for eight in range(EIGHT):
+        total = term[:, lanes_of(eight)] + first_ref[0, eight].astype(jnp.float32)
+        out_ref[eight] = (total + second_ref[eight].astype(jnp.float32)).astype(jnp.bfloat16)
+
+
+def values_kernel(keep_ref, arrived_ref, weights_ref, y_weights_ref, own_ref, other_ref):
     columns = EIGHT * LANES
     rows, head = own_ref.shape
     total = jnp.zeros((2 * rows, head), jnp.float32)
-    weights = [weight_ref[...]] + [ref[0] for ref in (first_ref, second_ref, third_ref)]
-    for step, weight in enumerate(weights):
+    for step in range(FOUR):
         part = slice(step * columns, (step + 1) * columns)
         both = jnp.concatenate([keep_ref[:, part], arrived_ref[:, part]], axis=0)
-        total += jnp.dot(both, weight.reshape(columns, head), preferred_element_type=jnp.float32)
+        weight = (weights_ref, y_weights_ref)[step // 2][step % 2].reshape(columns, head)
+        total += jnp.dot(both, weight, preferred_element_type=jnp.float32)
     own_ref[...] = total[:rows]
     other_ref[...] = total[rows:]
 
@@ -259,35 +260,32 @@
     arrived = lax.ppermute(send, "fsdp", SWAP_CORES)
     weight = exchange(spread_weight, "fsdp", EIGHT_GROUPS)
 
-    scaled, *outgoing = call(
-        outgoing_kernel,
-        jax.ShapeDtypeStruct(scaled.shape, scaled.dtype),
-        *[jax.ShapeDtypeStruct((2, EIGHT, head, LANES), jnp.bfloat16)] * (FOUR - 1),
-    )(keep, arrived, scaled, weight)
+    blocks = jax.ShapeDtypeStruct((EIGHT, head, LANES), jnp.bfloat16)
+    two_blocks = jax.ShapeDtypeStruct((2, EIGHT, head, LANES), jnp.bfloat16)
+    (first,) = call(first_kernel, two_blocks)(keep, arrived, scaled)
+    first, weight = lax.optimization_barrier((first, weight))
+    first = lax.ppermute(first, "fsdp", four_pairs(ALONG_Y))
+    x_weight = lax.ppermute(weight, "fsdp", four_pairs(ALONG_X))
+
     frag = frag_local[0].astype(jnp.bfloat16).reshape(replicas, -1, frag_shape[1])
-    scaled, frag = lax.optimization_barrier((scaled, frag))
-    incoming = [lax.ppermute(blocks, "fsdp", four_pairs(step)) for step, blocks in enumerate(outgoing, 1)]
+    first, frag = lax.optimization_barrier((first, frag))
     frag_terms = exchange(frag, "rep")
     frag_sum = jnp.sum(frag_terms.astype(jnp.float32), axis=0).astype(jnp.bfloat16)
-    scaled, frag_sum = lax.optimization_barrier((scaled, frag_sum))
+
+    second, weights = call(second_kernel, blocks, two_blocks)(keep, arrived, scaled, first, weight, x_weight)
+    second = lax.ppermute(second, "fsdp", four_pairs(ALONG_X))
+    y_weights = lax.ppermute(weights, "fsdp", four_pairs(ALONG_Y))
+
     local_sum = spread(frag_sum, replicas, "rep")
-
-    whole = pl.BlockSpec(memory_space=pltpu.VMEM)
-    (summed,) = call(
-        add_kernel,
-        jax.ShapeDtypeStruct((EIGHT, head, LANES), jnp.bfloat16),
-        grid=(1,),
-        in_specs=[whole] * 3 + [part_of(1, head)] * (FOUR - 1),
-    )(keep, arrived, scaled, *incoming)
+    (summed,) = call(third_kernel, blocks)(keep, arrived, scaled, first, second)
     summed, local_sum = lax.optimization_barrier((summed, local_sum))
     scattered = exchange(summed, "fsdp", EIGHT_GROUPS)
     local_mean = local_sum.reshape(frag_shape).astype(jnp.float32) / replicas
     new_global, new_moment = outer_update(frag_global, frag_moment, local_mean)
+    new_global, keep = lax.optimization_barrier((new_global, keep))
 
     partial = jax.ShapeDtypeStruct((rows, head), jnp.float32)
-    own_part, other_part = call(
-        values_kernel, partial, partial, grid=(1,), in_specs=[whole] * 3 + [part_of(0, head)] * (FOUR - 1)
-    )(keep, arrived, weight, *incoming)
+    own_part, other_part = call(values_kernel, partial, partial)(keep, arrived, weights, y_weights)
     arrived_part = lax.ppermute(other_part, "fsdp", SWAP_CORES)
     values = ((own_part + arrived_part) * inverse_rms).astype(jnp.bfloat16)
 

time: 112 us -> 115 us (1.027)
  the two profiles are of different devices: /device:TPU:8 before, /device:TPU:2 now
where the time goes in v6:
time: 115 us; the launch traced here: 114 us
  starting transfers between devices  53.2 us (46%)
  waiting for transfers between devices  40.3 us (35%)
  Pallas kernels  9.56 us (8%)
  other arithmetic  4.9 us (4%)
  local copies, waits for them, and re-layouts  4.47 us (4%)
  between operations  1.48 us (1%)
    all_to_all x4, starting transfers between devices, exchange(): lax.all_to_all(blocks, axis, 0, 0, axis_index_groups=groups, tiled=True)  39.6 us
    all_to_all x4, waiting for transfers between devices, exchange(): lax.all_to_all(blocks, axis, 0, 0, axis_index_groups=groups, tiled=True)  27.4 us
    ppermute x1, waiting for transfers between devices, local(): first = lax.ppermute(first, 'fsdp', four_pairs(ALONG_Y))  7.36 us
    pallas_call x1, Pallas kernels, local(): call(split_kernel, jax.ShapeDtypeStruct((rows, half), jnp.bfloat16), jax....  4.68 us
    ppermute x1, waiting for transfers between devices, local(): second = lax.ppermute(second, 'fsdp', four_pairs(ALONG_X))  4.59 us
    unnamed x28, local copies, waits for them, and re-layouts  3.67 us
    ppermute x1, starting transfers between devices, local(): second = lax.ppermute(second, 'fsdp', four_pairs(ALONG_X))  3 us
    ppermute x1, starting transfers between devices, local(): y_weights = lax.ppermute(weights, 'fsdp', four_pairs(ALONG_Y))  2.63 us
  transfers between devices with their start and end apart: 10, of which 6 were waited for; matrix products, arithmetic and copies ran while one was open for 5% of the time, Pallas kernels for 4%

profile of v6, /device:TPU:2, one launch (start us, length us, event | category | flops | bytes accessed | tf_op | source)
XLA Modules:
  0.0 114.0 jit_solution(13547702243065404427)
XLA Ops:
  0.6 4.7 %shard_map.164 = (bf16[128,4096]{1,0:T(8,128)(2,1)}, bf16[128,4224]{1,0:T(8,128)(2,1)}, bf16[128,128]{1,0:T(8,128)(2,1)}, f32[128,128]{1,0:T(8,128)}, bf16[8,128,128]{2,1,0:T(8,128)(2,1)}) custom-call(bf16[128,8192]{1,0:T(8,128)(2,1)} %bitcast.23, bf16[128,128]{1,0:T(8,128)(2,1)} %bitcast.24, bf16[128,128]{1,0:T(8,128)(2,1)} %bitcast.19, bf16[1,128]{1,0:T(2,128)(2,1)} %gain_ref.3), custom_call_target="tpu_custom_call" | custom-call | tf_op jit(solution)/shard_map/pallas_call | solution.py:240
  5.3 1.9 %collective-permute-start = (bf16[128,4224]{1,0:T(8,128)(2,1)}, bf16[128,4224]{1,0:T(8,128)(2,1)S(1)}, u32[]{:S(2)}, u32[]{:S(2)}) collective-permute-start(bf16[128,4224]{1,0:T(8,128)(2,1)} %get-tuple-element.25), channel_id=1, source_target_pairs={{0,1},{1,0},{2,3},{3,2},{4,5},{5,4},{6,7},{7,6},{8,9},{9,8},{10,11... | collective-permute-start | bytes 3244040 | tf_op jit(solution)/shard_map/ppermute | solution.py:260
  7.2 11.6 %all-to-all-start = ((bf16[8,128,128]{2,1,0:T(8,128)(2,1)}), bf16[8,128,128]{2,1,0:T(8,128)(2,1)S(1)}, u32[]{:S(2)}, u32[]{:S(2)}) async-start(bf16[8,128,128]{2,1,0:T(8,128)(2,1)} %get-tuple-element.27), calls=%async_computation | async-start | bytes 524288 | tf_op jit(solution)/shard_map/all_to_all | solution.py:40
  18.8 0.0 collective-permute-done.arrived_ref
  18.8 0.0 copy-start
  18.8 1.2 %copy-done = bf16[128,4096]{1,0:T(8,128)(2,1)S(1)} copy-done((bf16[128,4096]{1,0:T(8,128)(2,1)S(1)}, bf16[128,4096]{1,0:T(8,128)(2,1)}, u32[]{:S(2)}) %copy-start) | copy-done | bytes 1048600
  20.1 0.8 copy-done.2
  20.8 0.3 shard_map.165
  21.2 0.0 copy-start.1
  21.2 0.0 copy-start.3
  21.2 13.2 %all-to-all-done.weight_ref = bf16[8,128,128]{2,1,0:T(8,128)(2,1)S(1)} async-done(((bf16[8,128,128]{2,1,0:T(8,128)(2,1)}), bf16[8,128,128]{2,1,0:T(8,128)(2,1)S(1)}, u32[]{:S(2)}, u32[]{:S(2)}) %all-to-all-start) | async-done | bytes 262176 | tf_op jit(solution)/shard_map/all_to_all | solution.py:40
  34.4 1.9 %collective-permute-start.1 = (bf16[2,8,128,128]{3,2,1,0:T(8,128)(2,1)S(1)}, bf16[2,8,128,128]{3,2,1,0:T(8,128)(2,1)S(1)}, u32[]{:S(2)}, u32[]{:S(2)}) collective-permute-start(bf16[2,8,128,128]{3,2,1,0:T(8,128)(2,1)S(1)} %shard_map.165), channel_id=1, source_target_pairs={{0,8},{4,12},{16,24},{20,28},{32,40},{36,44},{48,56},{52,60},{2,10... | collective-permute-start | bytes 1572872 | tf_op jit(solution)/shard_map/ppermute | solution.py:267
  36.3 1.8 %convert_bitcast_fusion = bf16[16,8,1024]{2,1,0:T(8,128)(2,1)} fusion(f32[1,128,1024]{2,1,0:T(8,128)} %param.22), kind=kLoop, calls=%fused_computation.3 | loop fusion | flops 131072 | bytes 786432 | tf_op jit(solution)/shard_map/convert_element_type | solution.py:270
  38.1 7.4 %collective-permute-done.1.first_ref = bf16[2,8,128,128]{3,2,1,0:T(8,128)(2,1)S(1)} collective-permute-done((bf16[2,8,128,128]{3,2,1,0:T(8,128)(2,1)S(1)}, bf16[2,8,128,128]{3,2,1,0:T(8,128)(2,1)S(1)}, u32[]{:S(2)}, u32[]{:S(2)}) %collective-permute-start.1) | collective-permute-done | bytes 524320 | tf_op jit(solution)/shard_map/ppermute | solution.py:267
  45.5 18.2 %all-to-all-start.1 = ((bf16[16,8,1024]{2,1,0:T(8,128)(2,1)}), bf16[16,8,1024]{2,1,0:T(8,128)(2,1)S(1)}, u32[]{:S(2)}, u32[]{:S(2)}) async-start(bf16[16,8,1024]{2,1,0:T(8,128)(2,1)} %convert_bitcast_fusion), calls=%async_computation.1 | async-start | bytes 524288 | tf_op jit(solution)/shard_map/all_to_all | solution.py:40
  63.6 2.0 %collective-permute-start.2 = (bf16[8,128,128]{2,1,0:T(8,128)(2,1)S(1)}, bf16[8,128,128]{2,1,0:T(8,128)(2,1)S(1)}, u32[]{:S(2)}, u32[]{:S(2)}) collective-permute-start(bf16[8,128,128]{2,1,0:T(8,128)(2,1)S(1)} %all-to-all-done.weight_ref), channel_id=1, source_target_pairs={{0,2},{4,6},{16,18},{20,22},{32,34},{36,38},{48,50},{52,54},{2,0},... | collective-permute-start | bytes 786440 | tf_op jit(solution)/shard_map/ppermute | solution.py:268
  65.7 7.4 %all-to-all-done.1 = bf16[16,8,1024]{2,1,0:T(8,128)(2,1)S(1)} async-done(((bf16[16,8,1024]{2,1,0:T(8,128)(2,1)}), bf16[16,8,1024]{2,1,0:T(8,128)(2,1)S(1)}, u32[]{:S(2)}, u32[]{:S(2)}) %all-to-all-start.1) | async-done | bytes 262176 | tf_op jit(solution)/shard_map/all_to_all | solution.py:40
  73.1 0.7 broadcast_in_dim.19
  73.9 4.7 %all-to-all-start.2 = ((bf16[16,8,1024]{2,1,0:T(8,128)(2,1)}), bf16[16,8,1024]{2,1,0:T(8,128)(2,1)}, u32[]{:S(2)}, u32[]{:S(2)}) async-start(bf16[16,8,1024]{2,1,0:T(8,128)(2,1)} %broadcast_in_dim.19), calls=%async_computation.2 | async-start | bytes 524288 | tf_op jit(solution)/shard_map/all_to_all | solution.py:40
  78.6 0.0 collective-permute-done.2.x_weight_ref
  78.6 0.0 copy-start.4
  78.6 0.7 copy-done.4
  79.3 0.0 copy-done.1
  79.3 0.9 copy-done.5
  80.3 1.0 shard_map.166
  81.3 3.0 %collective-permute-start.3 = (bf16[8,128,128]{2,1,0:T(8,128)(2,1)}, bf16[8,128,128]{2,1,0:T(8,128)(2,1)S(1)}, u32[]{:S(2)}, u32[]{:S(2)}) collective-permute-start(bf16[8,128,128]{2,1,0:T(8,128)(2,1)} %get-tuple-element.31), channel_id=1, source_target_pairs={{0,2},{4,6},{16,18},{20,22},{32,34},{36,38},{48,50},{52,54},{2,0},... | collective-permute-start | bytes 786440 | tf_op jit(solution)/shard_map/ppermute | solution.py:276
  84.3 2.6 %collective-permute-start.4 = (bf16[2,8,128,128]{3,2,1,0:T(8,128)(2,1)S(1)}, bf16[2,8,128,128]{3,2,1,0:T(8,128)(2,1)}, u32[]{:S(2)}, u32[]{:S(2)}) collective-permute-start(bf16[2,8,128,128]{3,2,1,0:T(8,128)(2,1)S(1)} %get-tuple-element.35.weights_ref), channel_id=1, source_target_pairs={{0,8},{4,12},{16,24},{20,28},{32,40},{36,44},{48,56},{52,60},{2,10... | collective-permute-start | bytes 1572872 | tf_op jit(solution)/shard_map/ppermute | solution.py:277
  87.6 4.6 %collective-permute-done.3.second_ref = bf16[8,128,128]{2,1,0:T(8,128)(2,1)S(1)} collective-permute-done((bf16[8,128,128]{2,1,0:T(8,128)(2,1)}, bf16[8,128,128]{2,1,0:T(8,128)(2,1)S(1)}, u32[]{:S(2)}, u32[]{:S(2)}) %collective-permute-start.3) | collective-permute-done | bytes 262176 | tf_op jit(solution)/shard_map/ppermute | solution.py:276
  92.1 1.0 shard_map.167
  93.1 0.0 all-to-all-done.2
  93.1 5.1 %all-to-all-start.3 = ((bf16[8,128,128]{2,1,0:T(8,128)(2,1)}), bf16[8,128,128]{2,1,0:T(8,128)(2,1)S(1)}, u32[]{:S(2)}, u32[]{:S(2)}) async-start(bf16[8,128,128]{2,1,0:T(8,128)(2,1)} %shard_map.167), calls=%async_computation.3 | async-start | bytes 524288 | tf_op jit(solution)/shard_map/all_to_all | solution.py:40
  98.2 2.4 %multiply_subtract_fusion = (f32[128,1024]{1,0:T(8,128)}, f32[128,1024]{1,0:T(8,128)}) fusion(f32[128,1024]{1,0:T(8,128)} %param.23, bf16[16,8,1024]{2,1,0:T(8,128)(2,1)} %all-to-all-done.2, f32[128,1024]{1,0:T(8,128)} %param.24), kind=kLoop, calls=%fused_computation.1 | loop fusion | flops 1179648 | bytes 2359296 | tf_op jit(solution)/shard_map/sub | solution.py:215
  100.7 0.0 copy-start.8
  100.7 0.0 copy-start.9
  100.7 0.0 copy-start.10
  100.7 0.0 copy-start.11
  100.7 0.0 collective-permute-done.4.y_weights_ref
  100.7 1.8 %shard_map.168 = (f32[128,128]{1,0:T(8,128)S(1)}, f32[128,128]{1,0:T(8,128)S(1)}) custom-call(bf16[128,4096]{1,0:T(8,128)(2,1)S(1)} %copy-done.1, bf16[128,4224]{1,0:T(8,128)(2,1)S(1)} %collective-permute-done.arrived_ref, bf16[2,8,128,128]{3,2,1,0:T(8,128)(2,1)S(1)} %get-tuple-element.35.weights_ref, ...), custom_call_target="tpu_custom_call" | custom-call | tf_op jit(solution)/shard_map/pallas_call | solution.py:288
  102.6 2.1 %collective-permute-start.5 = (f32[128,128]{1,0:T(8,128)S(1)}, f32[128,128]{1,0:T(8,128)S(1)}, u32[]{:S(2)}, u32[]{:S(2)}) collective-permute-start(f32[128,128]{1,0:T(8,128)S(1)} %get-tuple-element.37), channel_id=1, source_target_pairs={{0,1},{1,0},{2,3},{3,2},{4,5},{5,4},{6,7},{7,6},{8,9},{9,8},{10,11... | collective-permute-start | bytes 196616 | tf_op jit(solution)/shard_map/ppermute | solution.py:289
  104.7 1.0 collective-permute-done.5
  105.7 0.6 fusion
  106.4 6.7 %all-to-all-done.3.terms_ref = bf16[8,128,128]{2,1,0:T(8,128)(2,1)S(1)} async-done(((bf16[8,128,128]{2,1,0:T(8,128)(2,1)}), bf16[8,128,128]{2,1,0:T(8,128)(2,1)S(1)}, u32[]{:S(2)}, u32[]{:S(2)}) %all-to-all-start.3) | async-done | bytes 262176 | tf_op jit(solution)/shard_map/all_to_all | solution.py:40
  113.1 0.1 broadcast_in_dim.22.fixes_ref
  113.1 0.0 copy-done.6
  113.2 0.0 copy-done.8
  113.2 0.0 copy-done.10
  113.2 0.0 copy-done.11
  113.2 0.8 shard_map.169
  (13 shorter events, 0.1 us)
Async XLA Ops:
  5.3 13.5 %collective-permute-start = (bf16[128,4224]{1,0:T(8,128)(2,1)}, bf16[128,4224]{1,0:T(8,128)(2,1)S(1)}, u32[]{:S(2)}, u32[]{:S(2)}) collective-permute-start(bf16[128,4224]{1,0:T(8,128)(2,1)} %get-tuple-element.25), channel_id=1, source_target_pairs={{0,1},{1,0},{2,3},{3,2},{4,5},{5,4},{6,7},{7,6},{8,9},{9,8},{10,11... | collective-permute-start | bytes 3244040 | tf_op jit(solution)/shard_map/ppermute | solution.py:260
  7.2 27.2 %all-to-all-start = ((bf16[8,128,128]{2,1,0:T(8,128)(2,1)}), bf16[8,128,128]{2,1,0:T(8,128)(2,1)S(1)}, u32[]{:S(2)}, u32[]{:S(2)}) async-start(bf16[8,128,128]{2,1,0:T(8,128)(2,1)} %get-tuple-element.27), calls=%async_computation | async-start | bytes 524288 | tf_op jit(solution)/shard_map/all_to_all | solution.py:40
  18.8 1.2 %copy-start = (bf16[128,4096]{1,0:T(8,128)(2,1)S(1)}, bf16[128,4096]{1,0:T(8,128)(2,1)}, u32[]{:S(2)}) copy-start(bf16[128,4096]{1,0:T(8,128)(2,1)} %get-tuple-element.34.keep_ref) | copy-start | bytes 3145732
  20.1 0.8 copy-start.2
  21.2 58.2 %copy-start.1 = (bf16[128,4096]{1,0:T(8,128)(2,1)S(1)}, bf16[128,4096]{1,0:T(8,128)(2,1)}, u32[]{:S(2)}) copy-start(bf16[128,4096]{1,0:T(8,128)(2,1)} %get-tuple-element.34.keep_ref) | copy-start | bytes 3145732
  21.2 58.2 %copy-start.3 = (bf16[128,128]{1,0:T(8,128)(2,1)S(1)}, bf16[128,128]{1,0:T(8,128)(2,1)}, u32[]{:S(2)}) copy-start(bf16[128,128]{1,0:T(8,128)(2,1)} %get-tuple-element.26.scaled_ref) | copy-start | bytes 98308
  34.4 11.1 %collective-permute-start.1 = (bf16[2,8,128,128]{3,2,1,0:T(8,128)(2,1)S(1)}, bf16[2,8,128,128]{3,2,1,0:T(8,128)(2,1)S(1)}, u32[]{:S(2)}, u32[]{:S(2)}) collective-permute-start(bf16[2,8,128,128]{3,2,1,0:T(8,128)(2,1)S(1)} %shard_map.165), channel_id=1, source_target_pairs={{0,8},{4,12},{16,24},{20,28},{32,40},{36,44},{48,56},{52,60},{2,10... | collective-permute-start | bytes 1572872 | tf_op jit(solution)/shard_map/ppermute | solution.py:267
  45.5 27.6 %all-to-all-start.1 = ((bf16[16,8,1024]{2,1,0:T(8,128)(2,1)}), bf16[16,8,1024]{2,1,0:T(8,128)(2,1)S(1)}, u32[]{:S(2)}, u32[]{:S(2)}) async-start(bf16[16,8,1024]{2,1,0:T(8,128)(2,1)} %convert_bitcast_fusion), calls=%async_computation.1 | async-start | bytes 524288 | tf_op jit(solution)/shard_map/all_to_all | solution.py:40
  63.6 15.0 %collective-permute-start.2 = (bf16[8,128,128]{2,1,0:T(8,128)(2,1)S(1)}, bf16[8,128,128]{2,1,0:T(8,128)(2,1)S(1)}, u32[]{:S(2)}, u32[]{:S(2)}) collective-permute-start(bf16[8,128,128]{2,1,0:T(8,128)(2,1)S(1)} %all-to-all-done.weight_ref), channel_id=1, source_target_pairs={{0,2},{4,6},{16,18},{20,22},{32,34},{36,38},{48,50},{52,54},{2,0},... | collective-permute-start | bytes 786440 | tf_op jit(solution)/shard_map/ppermute | solution.py:268
  73.9 19.3 %all-to-all-start.2 = ((bf16[16,8,1024]{2,1,0:T(8,128)(2,1)}), bf16[16,8,1024]{2,1,0:T(8,128)(2,1)}, u32[]{:S(2)}, u32[]{:S(2)}) async-start(bf16[16,8,1024]{2,1,0:T(8,128)(2,1)} %broadcast_in_dim.19), calls=%async_computation.2 | async-start | bytes 524288 | tf_op jit(solution)/shard_map/all_to_all | solution.py:40
  78.6 0.7 copy-start.4
  79.3 1.0 copy-start.5
  81.3 10.9 %collective-permute-start.3 = (bf16[8,128,128]{2,1,0:T(8,128)(2,1)}, bf16[8,128,128]{2,1,0:T(8,128)(2,1)S(1)}, u32[]{:S(2)}, u32[]{:S(2)}) collective-permute-start(bf16[8,128,128]{2,1,0:T(8,128)(2,1)} %get-tuple-element.31), channel_id=1, source_target_pairs={{0,2},{4,6},{16,18},{20,22},{32,34},{36,38},{48,50},{52,54},{2,0},... | collective-permute-start | bytes 786440 | tf_op jit(solution)/shard_map/ppermute | solution.py:276
  84.3 16.5 %collective-permute-start.4 = (bf16[2,8,128,128]{3,2,1,0:T(8,128)(2,1)S(1)}, bf16[2,8,128,128]{3,2,1,0:T(8,128)(2,1)}, u32[]{:S(2)}, u32[]{:S(2)}) collective-permute-start(bf16[2,8,128,128]{3,2,1,0:T(8,128)(2,1)S(1)} %get-tuple-element.35.weights_ref), channel_id=1, source_target_pairs={{0,8},{4,12},{16,24},{20,28},{32,40},{36,44},{48,56},{52,60},{2,10... | collective-permute-start | bytes 1572872 | tf_op jit(solution)/shard_map/ppermute | solution.py:277
  93.1 19.9 %all-to-all-start.3 = ((bf16[8,128,128]{2,1,0:T(8,128)(2,1)}), bf16[8,128,128]{2,1,0:T(8,128)(2,1)S(1)}, u32[]{:S(2)}, u32[]{:S(2)}) async-start(bf16[8,128,128]{2,1,0:T(8,128)(2,1)} %shard_map.167), calls=%async_computation.3 | async-start | bytes 524288 | tf_op jit(solution)/shard_map/all_to_all | solution.py:40
  100.7 4.0 %copy-start.13 = (f32[2,1]{0,1:T(1,128)S(1)}, f32[2,1]{0,1:T(1,128)}, u32[]{:S(2)}) copy-start(f32[2,1]{0,1:T(1,128)} %constant.14.clone) | copy-start | bytes 28
  100.7 5.1 %copy-start.12 = (f32[128,128]{1,0:T(8,128)S(1)}, f32[128,128]{1,0:T(8,128)}, u32[]{:S(2)}) copy-start(f32[128,128]{1,0:T(8,128)} %get-tuple-element.38) | copy-start | bytes 196612
  100.7 12.5 %copy-start.6 = (bf16[1,128,128]{2,1,0:T(8,128)(2,1)S(1)}, bf16[1,128,128]{2,1,0:T(8,128)(2,1)}, u32[]{:S(2)}) copy-start(bf16[1,128,128]{2,1,0:T(8,128)(2,1)} %param.15) | copy-start | bytes 98308
  100.7 12.5 %copy-start.7 = (f32[1,128,128]{2,1,0:T(8,128)S(1)}, f32[1,128,128]{2,1,0:T(8,128)}, u32[]{:S(2)}) copy-start(f32[1,128,128]{2,1,0:T(8,128)} %param.18) | copy-start | bytes 196612
  100.7 12.5 %copy-start.8 = (f32[1,128,128]{2,1,0:T(8,128)S(1)}, f32[1,128,128]{2,1,0:T(8,128)}, u32[]{:S(2)}) copy-start(f32[1,128,128]{2,1,0:T(8,128)} %param.19) | copy-start | bytes 196612
  100.7 12.5 %copy-start.9 = (bf16[1,128]{1,0:T(2,128)(2,1)S(1)}, bf16[1,128]{1,0:T(2,128)(2,1)}, u32[]{:S(2)}) copy-start(bf16[1,128]{1,0:T(2,128)(2,1)} %gain_ref.3) | copy-start | bytes 772
  100.7 12.5 %copy-start.10 = (f32[1,128]{1,0:T(1,128)S(1)}, f32[1,128]{1,0:T(1,128)}, u32[]{:S(2)}) copy-start(f32[1,128]{1,0:T(1,128)} %m_gain_ref.1) | copy-start | bytes 1540
  100.7 12.5 %copy-start.11 = (f32[1,128]{1,0:T(1,128)S(1)}, f32[1,128]{1,0:T(1,128)}, u32[]{:S(2)}) copy-start(f32[1,128]{1,0:T(1,128)} %v_gain_ref.1) | copy-start | bytes 1540
  102.6 3.1 %collective-permute-start.5 = (f32[128,128]{1,0:T(8,128)S(1)}, f32[128,128]{1,0:T(8,128)S(1)}, u32[]{:S(2)}, u32[]{:S(2)}) collective-permute-start(f32[128,128]{1,0:T(8,128)S(1)} %get-tuple-element.37), channel_id=1, source_target_pairs={{0,1},{1,0},{2,3},{3,2},{4,5},{5,4},{6,7},{7,6},{8,9},{9,8},{10,11... | collective-permute-start | bytes 196616 | tf_op jit(solution)/shard_map/ppermute | solution.py:289

commit v7 on v6

--- a/solution.py
+++ b/solution.py
@@ -151,12 +151,15 @@
             out_ref[index, eight] = term[:, lanes_of(eight)].astype(jnp.bfloat16)
 
 
-def second_kernel(keep_ref, arrived_ref, scaled_ref, first_ref, weight_ref, x_weight_ref, out_ref, weights_ref):
+def second_kernel(keep_ref, arrived_ref, scaled_ref, first_ref, out_ref):
     term = gradient_term(keep_ref, arrived_ref, scaled_ref, ALONG_X)
     for eight in range(EIGHT):
         out_ref[eight] = (term[:, lanes_of(eight)] + first_ref[1, eight].astype(jnp.float32)).astype(jnp.bfloat16)
-        weights_ref[0, eight] = weight_ref[eight]
-        weights_ref[1, eight] = x_weight_ref[eight]
+
+
+def join_kernel(weight_ref, x_weight_ref, out_ref):
+    out_ref[0] = weight_ref[...]
+    out_ref[1] = x_weight_ref[...]
 
 
 def third_kernel(keep_ref, arrived_ref, scaled_ref, first_ref, second_ref, out_ref):
@@ -258,25 +261,23 @@
         ],
     )(tokens_in[0], value_cotangent[0], value_weight[0], norm_gain)
     arrived = lax.ppermute(send, "fsdp", SWAP_CORES)
-    weight = exchange(spread_weight, "fsdp", EIGHT_GROUPS)
+    frag = frag_local[0].astype(jnp.bfloat16).reshape(replicas, -1, frag_shape[1])
+    frag_terms = exchange(frag, "rep")
 
     blocks = jax.ShapeDtypeStruct((EIGHT, head, LANES), jnp.bfloat16)
     two_blocks = jax.ShapeDtypeStruct((2, EIGHT, head, LANES), jnp.bfloat16)
-    (first,) = call(first_kernel, two_blocks)(keep, arrived, scaled)
-    first, weight = lax.optimization_barrier((first, weight))
+    (first,) = call(first_kernel, two_blocks, mebibytes=16)(keep, arrived, scaled)
     first = lax.ppermute(first, "fsdp", four_pairs(ALONG_Y))
+    frag_terms, spread_weight = lax.optimization_barrier((frag_terms, spread_weight))
+    weight = exchange(spread_weight, "fsdp", EIGHT_GROUPS)
+    (second,) = call(second_kernel, blocks)(keep, arrived, scaled, first)
+    second = lax.ppermute(second, "fsdp", four_pairs(ALONG_X))
     x_weight = lax.ppermute(weight, "fsdp", four_pairs(ALONG_X))
-
-    frag = frag_local[0].astype(jnp.bfloat16).reshape(replicas, -1, frag_shape[1])
-    first, frag = lax.optimization_barrier((first, frag))
-    frag_terms = exchange(frag, "rep")
+    (weights,) = call(join_kernel, two_blocks)(weight, x_weight)
+    y_weights = lax.ppermute(weights, "fsdp", four_pairs(ALONG_Y))
     frag_sum = jnp.sum(frag_terms.astype(jnp.float32), axis=0).astype(jnp.bfloat16)
-
-    second, weights = call(second_kernel, blocks, two_blocks)(keep, arrived, scaled, first, weight, x_weight)
-    second = lax.ppermute(second, "fsdp", four_pairs(ALONG_X))
-    y_weights = lax.ppermute(weights, "fsdp", four_pairs(ALONG_Y))
-
     local_sum = spread(frag_sum, replicas, "rep")
+
     (summed,) = call(third_kernel, blocks)(keep, arrived, scaled, first, second)
     summed, local_sum = lax.optimization_barrier((summed, local_sum))
     scattered = exchange(summed, "fsdp", EIGHT_GROUPS)

time: 115 us -> 106 us (0.922)
  the two profiles are of different devices: /device:TPU:2 before, /device:TPU:6 now
where the time goes in v7:
time: 106 us; the launch traced here: 105 us
  starting transfers between devices  34 us (32%)
  blocking collectives  29.1 us (27%)
  waiting for transfers between devices  23.8 us (22%)
  Pallas kernels  11.4 us (11%)
  other arithmetic  4.11 us (4%)
  between operations  1.52 us (1%)
    all_to_all x1, blocking collectives, exchange(): lax.all_to_all(blocks, axis, 0, 0, axis_index_groups=groups, tiled=True)  29.1 us
    all_to_all x3, starting transfers between devices, exchange(): lax.all_to_all(blocks, axis, 0, 0, axis_index_groups=groups, tiled=True)  17.6 us
    all_to_all x3, waiting for transfers between devices, exchange(): lax.all_to_all(blocks, axis, 0, 0, axis_index_groups=groups, tiled=True)  16.8 us
    ppermute x1, waiting for transfers between devices, local(): second = lax.ppermute(second, 'fsdp', four_pairs(ALONG_X))  5.8 us
    ppermute x1, starting transfers between devices, local(): x_weight = lax.ppermute(weight, 'fsdp', four_pairs(ALONG_X))  4.91 us
    pallas_call x1, Pallas kernels, local(): call(split_kernel, jax.ShapeDtypeStruct((rows, half), jnp.bfloat16), jax....  4.65 us
    ppermute x1, starting transfers between devices, local(): y_weights = lax.ppermute(weights, 'fsdp', four_pairs(ALONG_Y))  2.87 us
    ppermute x1, starting transfers between devices, local(): first = lax.ppermute(first, 'fsdp', four_pairs(ALONG_Y))  2.69 us
  transfers between devices with their start and end apart: 9, of which 4 were waited for; matrix products, arithmetic and copies ran while one was open for 5% of the time, Pallas kernels for 6%

profile of v7, /device:TPU:6, one launch (start us, length us, event | category | flops | bytes accessed | tf_op | source)
XLA Modules:
  0.0 104.8 jit_solution(16258937031639603998)
XLA Ops:
  0.6 0.0 copy-start.8
  0.6 4.7 %shard_map.164 = (bf16[128,4096]{1,0:T(8,128)(2,1)}, bf16[128,4224]{1,0:T(8,128)(2,1)}, bf16[128,128]{1,0:T(8,128)(2,1)}, f32[128,128]{1,0:T(8,128)}, bf16[8,128,128]{2,1,0:T(8,128)(2,1)}) custom-call(bf16[128,8192]{1,0:T(8,128)(2,1)} %bitcast.23, bf16[128,128]{1,0:T(8,128)(2,1)} %bitcast.24, bf16[128,128]{1,0:T(8,128)(2,1)} %bitcast.19, bf16[1,128]{1,0:T(2,128)(2,1)} %gain_ref.3), custom_call_target="tpu_custom_call" | custom-call | tf_op jit(solution)/shard_map/pallas_call | solution.py:243
  5.3 0.0 copy-start
  5.3 0.0 copy-start.1
  5.3 2.1 %collective-permute-start = (bf16[128,4224]{1,0:T(8,128)(2,1)}, bf16[128,4224]{1,0:T(8,128)(2,1)S(1)}, u32[]{:S(2)}, u32[]{:S(2)}) collective-permute-start(bf16[128,4224]{1,0:T(8,128)(2,1)} %get-tuple-element.21), channel_id=1, source_target_pairs={{0,1},{1,0},{2,3},{3,2},{4,5},{5,4},{6,7},{7,6},{8,9},{9,8},{10,11... | collective-permute-start | bytes 3244040 | tf_op jit(solution)/shard_map/ppermute | solution.py:263
  7.4 0.0 copy-done.8
  7.4 29.1 %all_to_all.20 = bf16[16,8,1024]{2,1,0:T(8,128)(2,1)} all-to-all(bf16[16,8,1024]{2,1,0:T(8,128)(2,1)S(1)} %convert_bitcast_fusion), channel_id=1, replica_groups=mesh['rep'=16,'fsdp'=64] {'rep'}, dimensions={0} | all-to-all | bytes 524288 | tf_op jit(solution)/shard_map/all_to_all | solution.py:40
  36.6 9.8 %all-to-all-start.2 = ((bf16[8,128,128]{2,1,0:T(8,128)(2,1)}), bf16[8,128,128]{2,1,0:T(8,128)(2,1)S(1)}, u32[]{:S(2)}, u32[]{:S(2)}) async-start(bf16[8,128,128]{2,1,0:T(8,128)(2,1)} %get-tuple-element.27), calls=%async_computation.2 | async-start | bytes 524288 | tf_op jit(solution)/shard_map/all_to_all | solution.py:40
  46.3 0.0 collective-permute-done.arrived_ref
  46.3 0.0 copy-done
  46.4 0.0 copy-done.1
  46.4 0.3 shard_map.165
  46.7 2.7 %collective-permute-start.1 = (bf16[2,8,128,128]{3,2,1,0:T(8,128)(2,1)S(1)}, bf16[2,8,128,128]{3,2,1,0:T(8,128)(2,1)S(1)}, u32[]{:S(2)}, u32[]{:S(2)}) collective-permute-start(bf16[2,8,128,128]{3,2,1,0:T(8,128)(2,1)S(1)} %shard_map.165), channel_id=1, source_target_pairs={{0,8},{4,12},{16,24},{20,28},{32,40},{36,44},{48,56},{52,60},{2,10... | collective-permute-start | bytes 1572872 | tf_op jit(solution)/shard_map/ppermute | solution.py:270
  49.4 11.4 %all-to-all-done.2.weight_ref = bf16[8,128,128]{2,1,0:T(8,128)(2,1)S(1)} async-done(((bf16[8,128,128]{2,1,0:T(8,128)(2,1)}), bf16[8,128,128]{2,1,0:T(8,128)(2,1)S(1)}, u32[]{:S(2)}, u32[]{:S(2)}) %all-to-all-start.2) | async-done | bytes 262176 | tf_op jit(solution)/shard_map/all_to_all | solution.py:40
  60.8 4.9 %collective-permute-start.3 = (bf16[8,128,128]{2,1,0:T(8,128)(2,1)S(1)}, bf16[8,128,128]{2,1,0:T(8,128)(2,1)}, u32[]{:S(2)}, u32[]{:S(2)}) collective-permute-start(bf16[8,128,128]{2,1,0:T(8,128)(2,1)S(1)} %all-to-all-done.2.weight_ref), channel_id=1, source_target_pairs={{0,2},{4,6},{16,18},{20,22},{32,34},{36,38},{48,50},{52,54},{2,0},... | collective-permute-start | bytes 786440 | tf_op jit(solution)/shard_map/ppermute | solution.py:275
  65.8 1.0 reduce_sum.12
  66.8 0.7 broadcast_in_dim.19
  67.5 4.4 %all-to-all-start.1 = ((bf16[16,8,1024]{2,1,0:T(8,128)(2,1)}), bf16[16,8,1024]{2,1,0:T(8,128)(2,1)}, u32[]{:S(2)}, u32[]{:S(2)}) async-start(bf16[16,8,1024]{2,1,0:T(8,128)(2,1)} %broadcast_in_dim.19), calls=%async_computation.1 | async-start | bytes 524288 | tf_op jit(solution)/shard_map/all_to_all | solution.py:40
  71.9 0.0 collective-permute-done.1.first_ref
  71.9 1.0 shard_map.166
  72.9 1.9 %collective-permute-start.2 = (bf16[8,128,128]{2,1,0:T(8,128)(2,1)}, bf16[8,128,128]{2,1,0:T(8,128)(2,1)}, u32[]{:S(2)}, u32[]{:S(2)}) collective-permute-start(bf16[8,128,128]{2,1,0:T(8,128)(2,1)} %shard_map.166), channel_id=1, source_target_pairs={{0,2},{4,6},{16,18},{20,22},{32,34},{36,38},{48,50},{52,54},{2,0},... | collective-permute-start | bytes 786440 | tf_op jit(solution)/shard_map/ppermute | solution.py:274
  74.8 0.0 collective-permute-done.3.x_weight_ref
  74.8 1.0 shard_map.168.weights_ref
  75.8 2.9 %collective-permute-start.4 = (bf16[2,8,128,128]{3,2,1,0:T(8,128)(2,1)S(1)}, bf16[2,8,128,128]{3,2,1,0:T(8,128)(2,1)}, u32[]{:S(2)}, u32[]{:S(2)}) collective-permute-start(bf16[2,8,128,128]{3,2,1,0:T(8,128)(2,1)S(1)} %shard_map.168.weights_ref), channel_id=1, source_target_pairs={{0,8},{4,12},{16,24},{20,28},{32,40},{36,44},{48,56},{52,60},{2,10... | collective-permute-start | bytes 1572872 | tf_op jit(solution)/shard_map/ppermute | solution.py:277
  79.3 5.8 %collective-permute-done.2.second_ref = bf16[8,128,128]{2,1,0:T(8,128)(2,1)} collective-permute-done((bf16[8,128,128]{2,1,0:T(8,128)(2,1)}, bf16[8,128,128]{2,1,0:T(8,128)(2,1)}, u32[]{:S(2)}, u32[]{:S(2)}) %collective-permute-start.2) | collective-permute-done | bytes 262176 | tf_op jit(solution)/shard_map/ppermute | solution.py:274
  85.1 1.9 %shard_map.167 = bf16[8,128,128]{2,1,0:T(8,128)(2,1)} custom-call(bf16[128,4096]{1,0:T(8,128)(2,1)S(1)} %copy-done, bf16[128,4224]{1,0:T(8,128)(2,1)S(1)} %collective-permute-done.arrived_ref, bf16[128,128]{1,0:T(8,128)(2,1)S(1)} %copy-done.1, bf16[2,8,128,128]{3,2,1,0:T(8,128)(2,1)S(1)} %collective-permute-done.1.first_ref, ...), custom_call_target="tpu_custom_call" | custom-call | tf_op jit(solution)/shard_map/pallas_call | solution.py:281
  87.1 0.0 all-to-all-done.1
  87.1 3.4 %all-to-all-start.3 = ((bf16[8,128,128]{2,1,0:T(8,128)(2,1)}), bf16[8,128,128]{2,1,0:T(8,128)(2,1)S(1)}, u32[]{:S(2)}, u32[]{:S(2)}) async-start(bf16[8,128,128]{2,1,0:T(8,128)(2,1)} %shard_map.167), calls=%async_computation.3 | async-start | bytes 524288 | tf_op jit(solution)/shard_map/all_to_all | solution.py:40
  90.5 2.4 %multiply_subtract_fusion = (f32[128,1024]{1,0:T(8,128)}, f32[128,1024]{1,0:T(8,128)}) fusion(f32[128,1024]{1,0:T(8,128)} %param.23, bf16[16,8,1024]{2,1,0:T(8,128)(2,1)} %all-to-all-done.1, f32[128,1024]{1,0:T(8,128)} %param.24), kind=kLoop, calls=%fused_computation.1 | loop fusion | flops 1179648 | bytes 2359296 | tf_op jit(solution)/shard_map/sub | solution.py:218
  92.9 0.0 copy-start.4
  92.9 0.0 copy-start.5
  92.9 0.0 copy-start.6
  93.0 0.0 copy-start.7
  93.0 0.0 collective-permute-done.4.y_weights_ref
  93.0 1.8 %shard_map.169 = (f32[128,128]{1,0:T(8,128)S(1)}, f32[128,128]{1,0:T(8,128)S(1)}) custom-call(bf16[128,4096]{1,0:T(8,128)(2,1)S(1)} %copy-done, bf16[128,4224]{1,0:T(8,128)(2,1)S(1)} %collective-permute-done.arrived_ref, bf16[2,8,128,128]{3,2,1,0:T(8,128)(2,1)S(1)} %shard_map.168.weights_ref, bf16[2,8,128,128]{3,2,1,0:T(8,128)(2,1)} %collective-permute-done.4.y_weights_ref), custom_call_target="tpu_custom_call" | custom-call | tf_op jit(solution)/shard_map/pallas_call | solution.py:289
  94.8 1.9 %collective-permute-start.5 = (f32[128,128]{1,0:T(8,128)S(1)}, f32[128,128]{1,0:T(8,128)S(1)}, u32[]{:S(2)}, u32[]{:S(2)}) collective-permute-start(f32[128,128]{1,0:T(8,128)S(1)} %get-tuple-element.29), channel_id=1, source_target_pairs={{0,1},{1,0},{2,3},{3,2},{4,5},{5,4},{6,7},{7,6},{8,9},{9,8},{10,11... | collective-permute-start | bytes 196616 | tf_op jit(solution)/shard_map/ppermute | solution.py:290
  96.7 0.0 copy-done.10
  96.8 1.2 %collective-permute-done.5 = f32[128,128]{1,0:T(8,128)S(1)} collective-permute-done((f32[128,128]{1,0:T(8,128)S(1)}, f32[128,128]{1,0:T(8,128)S(1)}, u32[]{:S(2)}, u32[]{:S(2)}) %collective-permute-start.5) | collective-permute-done | bytes 65568 | tf_op jit(solution)/shard_map/ppermute | solution.py:290
  98.0 0.0 copy-done.9
  98.0 0.6 fusion
  98.6 5.3 %all-to-all-done.3.terms_ref = bf16[8,128,128]{2,1,0:T(8,128)(2,1)S(1)} async-done(((bf16[8,128,128]{2,1,0:T(8,128)(2,1)}), bf16[8,128,128]{2,1,0:T(8,128)(2,1)S(1)}, u32[]{:S(2)}, u32[]{:S(2)}) %all-to-all-start.3) | async-done | bytes 262176 | tf_op jit(solution)/shard_map/all_to_all | solution.py:40
  103.9 0.1 broadcast_in_dim.22.fixes_ref
  104.0 0.0 copy-done.2
  104.0 0.0 copy-done.3
  104.0 0.0 copy-done.4
  104.0 0.0 copy-done.6
  104.0 0.0 copy-done.7
  104.0 0.8 shard_map.170
  (7 shorter events, 0.1 us)
Async XLA Ops:
  0.6 6.8 %copy-start.8 = (f32[1,128,1024]{2,1,0:T(8,128)S(1)}, f32[1,128,1024]{2,1,0:T(8,128)}, u32[]{:S(2)}) copy-start(f32[1,128,1024]{2,1,0:T(8,128)} %param.22) | copy-start | bytes 1572868
  5.3 41.0 %copy-start = (bf16[128,4096]{1,0:T(8,128)(2,1)S(1)}, bf16[128,4096]{1,0:T(8,128)(2,1)}, u32[]{:S(2)}) copy-start(bf16[128,4096]{1,0:T(8,128)(2,1)} %get-tuple-element.26.keep_ref) | copy-start | bytes 3145732
  5.3 41.0 %copy-start.1 = (bf16[128,128]{1,0:T(8,128)(2,1)S(1)}, bf16[128,128]{1,0:T(8,128)(2,1)}, u32[]{:S(2)}) copy-start(bf16[128,128]{1,0:T(8,128)(2,1)} %get-tuple-element.22.scaled_ref) | copy-start | bytes 98308
  5.3 41.0 %collective-permute-start = (bf16[128,4224]{1,0:T(8,128)(2,1)}, bf16[128,4224]{1,0:T(8,128)(2,1)S(1)}, u32[]{:S(2)}, u32[]{:S(2)}) collective-permute-start(bf16[128,4224]{1,0:T(8,128)(2,1)} %get-tuple-element.21), channel_id=1, source_target_pairs={{0,1},{1,0},{2,3},{3,2},{4,5},{5,4},{6,7},{7,6},{8,9},{9,8},{10,11... | collective-permute-start | bytes 3244040 | tf_op jit(solution)/shard_map/ppermute | solution.py:263
  36.6 24.3 %all-to-all-start.2 = ((bf16[8,128,128]{2,1,0:T(8,128)(2,1)}), bf16[8,128,128]{2,1,0:T(8,128)(2,1)S(1)}, u32[]{:S(2)}, u32[]{:S(2)}) async-start(bf16[8,128,128]{2,1,0:T(8,128)(2,1)} %get-tuple-element.27), calls=%async_computation.2 | async-start | bytes 524288 | tf_op jit(solution)/shard_map/all_to_all | solution.py:40
  46.7 25.2 %collective-permute-start.1 = (bf16[2,8,128,128]{3,2,1,0:T(8,128)(2,1)S(1)}, bf16[2,8,128,128]{3,2,1,0:T(8,128)(2,1)S(1)}, u32[]{:S(2)}, u32[]{:S(2)}) collective-permute-start(bf16[2,8,128,128]{3,2,1,0:T(8,128)(2,1)S(1)} %shard_map.165), channel_id=1, source_target_pairs={{0,8},{4,12},{16,24},{20,28},{32,40},{36,44},{48,56},{52,60},{2,10... | collective-permute-start | bytes 1572872 | tf_op jit(solution)/shard_map/ppermute | solution.py:270
  60.8 14.0 %collective-permute-start.3 = (bf16[8,128,128]{2,1,0:T(8,128)(2,1)S(1)}, bf16[8,128,128]{2,1,0:T(8,128)(2,1)}, u32[]{:S(2)}, u32[]{:S(2)}) collective-permute-start(bf16[8,128,128]{2,1,0:T(8,128)(2,1)S(1)} %all-to-all-done.2.weight_ref), channel_id=1, source_target_pairs={{0,2},{4,6},{16,18},{20,22},{32,34},{36,38},{48,50},{52,54},{2,0},... | collective-permute-start | bytes 786440 | tf_op jit(solution)/shard_map/ppermute | solution.py:275
  67.5 19.6 %all-to-all-start.1 = ((bf16[16,8,1024]{2,1,0:T(8,128)(2,1)}), bf16[16,8,1024]{2,1,0:T(8,128)(2,1)}, u32[]{:S(2)}, u32[]{:S(2)}) async-start(bf16[16,8,1024]{2,1,0:T(8,128)(2,1)} %broadcast_in_dim.19), calls=%async_computation.1 | async-start | bytes 524288 | tf_op jit(solution)/shard_map/all_to_all | solution.py:40
  72.9 12.2 %collective-permute-start.2 = (bf16[8,128,128]{2,1,0:T(8,128)(2,1)}, bf16[8,128,128]{2,1,0:T(8,128)(2,1)}, u32[]{:S(2)}, u32[]{:S(2)}) collective-permute-start(bf16[8,128,128]{2,1,0:T(8,128)(2,1)} %shard_map.166), channel_id=1, source_target_pairs={{0,2},{4,6},{16,18},{20,22},{32,34},{36,38},{48,50},{52,54},{2,0},... | collective-permute-start | bytes 786440 | tf_op jit(solution)/shard_map/ppermute | solution.py:274
  75.8 17.2 %collective-permute-start.4 = (bf16[2,8,128,128]{3,2,1,0:T(8,128)(2,1)S(1)}, bf16[2,8,128,128]{3,2,1,0:T(8,128)(2,1)}, u32[]{:S(2)}, u32[]{:S(2)}) collective-permute-start(bf16[2,8,128,128]{3,2,1,0:T(8,128)(2,1)S(1)} %shard_map.168.weights_ref), channel_id=1, source_target_pairs={{0,8},{4,12},{16,24},{20,28},{32,40},{36,44},{48,56},{52,60},{2,10... | collective-permute-start | bytes 1572872 | tf_op jit(solution)/shard_map/ppermute | solution.py:277
  87.1 16.9 %all-to-all-start.3 = ((bf16[8,128,128]{2,1,0:T(8,128)(2,1)}), bf16[8,128,128]{2,1,0:T(8,128)(2,1)S(1)}, u32[]{:S(2)}, u32[]{:S(2)}) async-start(bf16[8,128,128]{2,1,0:T(8,128)(2,1)} %shard_map.167), calls=%async_computation.3 | async-start | bytes 524288 | tf_op jit(solution)/shard_map/all_to_all | solution.py:40
  92.9 3.8 %copy-start.10 = (f32[2,1]{0,1:T(1,128)S(1)}, f32[2,1]{0,1:T(1,128)}, u32[]{:S(2)}) copy-start(f32[2,1]{0,1:T(1,128)} %constant.14.clone) | copy-start | bytes 28
  92.9 5.1 %copy-start.9 = (f32[128,128]{1,0:T(8,128)S(1)}, f32[128,128]{1,0:T(8,128)}, u32[]{:S(2)}) copy-start(f32[128,128]{1,0:T(8,128)} %get-tuple-element.30) | copy-start | bytes 196612
  92.9 11.1 %copy-start.2 = (bf16[1,128,128]{2,1,0:T(8,128)(2,1)S(1)}, bf16[1,128,128]{2,1,0:T(8,128)(2,1)}, u32[]{:S(2)}) copy-start(bf16[1,128,128]{2,1,0:T(8,128)(2,1)} %param.15) | copy-start | bytes 98308
  92.9 11.1 %copy-start.3 = (f32[1,128,128]{2,1,0:T(8,128)S(1)}, f32[1,128,128]{2,1,0:T(8,128)}, u32[]{:S(2)}) copy-start(f32[1,128,128]{2,1,0:T(8,128)} %param.18) | copy-start | bytes 196612
  92.9 11.1 %copy-start.4 = (f32[1,128,128]{2,1,0:T(8,128)S(1)}, f32[1,128,128]{2,1,0:T(8,128)}, u32[]{:S(2)}) copy-start(f32[1,128,128]{2,1,0:T(8,128)} %param.19) | copy-start | bytes 196612
  92.9 11.1 %copy-start.5 = (bf16[1,128]{1,0:T(2,128)(2,1)S(1)}, bf16[1,128]{1,0:T(2,128)(2,1)}, u32[]{:S(2)}) copy-start(bf16[1,128]{1,0:T(2,128)(2,1)} %gain_ref.3) | copy-start | bytes 772
  92.9 11.1 %copy-start.6 = (f32[1,128]{1,0:T(1,128)S(1)}, f32[1,128]{1,0:T(1,128)}, u32[]{:S(2)}) copy-start(f32[1,128]{1,0:T(1,128)} %m_gain_ref.1) | copy-start | bytes 1540
  93.0 11.1 %copy-start.7 = (f32[1,128]{1,0:T(1,128)S(1)}, f32[1,128]{1,0:T(1,128)}, u32[]{:S(2)}) copy-start(f32[1,128]{1,0:T(1,128)} %v_gain_ref.1) | copy-start | bytes 1540
  94.8 3.1 %collective-permute-start.5 = (f32[128,128]{1,0:T(8,128)S(1)}, f32[128,128]{1,0:T(8,128)S(1)}, u32[]{:S(2)}, u32[]{:S(2)}) collective-permute-start(f32[128,128]{1,0:T(8,128)S(1)} %get-tuple-element.29), channel_id=1, source_target_pairs={{0,1},{1,0},{2,3},{3,2},{4,5},{5,4},{6,7},{7,6},{8,9},{9,8},{10,11... | collective-permute-start | bytes 196616 | tf_op jit(solution)/shard_map/ppermute | solution.py:290

commit v8 on v7

--- a/solution.py
+++ b/solution.py
@@ -276,6 +276,7 @@
     (weights,) = call(join_kernel, two_blocks)(weight, x_weight)
     y_weights = lax.ppermute(weights, "fsdp", four_pairs(ALONG_Y))
     frag_sum = jnp.sum(frag_terms.astype(jnp.float32), axis=0).astype(jnp.bfloat16)
+    second, frag_sum = lax.optimization_barrier((second, frag_sum))
     local_sum = spread(frag_sum, replicas, "rep")
 
     (summed,) = call(third_kernel, blocks)(keep, arrived, scaled, first, second)

time: 106 us -> 107 us (level)
  the two profiles are of different devices: /device:TPU:6 before, /device:TPU:2 now
where the time goes in v8:
time: 107 us; the launch traced here: 106 us
  starting transfers between devices  56.9 us (53%)
  waiting for transfers between devices  30.6 us (29%)
  Pallas kernels  9.83 us (9%)
  other arithmetic  4.81 us (4%)
  local copies, waits for them, and re-layouts  2.56 us (2%)
  between operations  1.53 us (1%)
    all_to_all x4, starting transfers between devices, exchange(): lax.all_to_all(blocks, axis, 0, 0, axis_index_groups=groups, tiled=True)  40.5 us
    all_to_all x4, waiting for transfers between devices, exchange(): lax.all_to_all(blocks, axis, 0, 0, axis_index_groups=groups, tiled=True)  29.5 us
    pallas_call x1, Pallas kernels, local(): call(split_kernel, jax.ShapeDtypeStruct((rows, half), jnp.bfloat16), jax....  4.67 us
    ppermute x1, starting transfers between devices, local(): first = lax.ppermute(first, 'fsdp', four_pairs(ALONG_Y))  3.6 us
    ppermute x1, starting transfers between devices, local(): y_weights = lax.ppermute(weights, 'fsdp', four_pairs(ALONG_Y))  3.06 us
    ppermute x1, starting transfers between devices, local(): arrived_part = lax.ppermute(other_part, 'fsdp', SWAP_CORES)  2.74 us
    ppermute x1, starting transfers between devices, local(): second = lax.ppermute(second, 'fsdp', four_pairs(ALONG_X))  2.53 us
    sub x1, other arithmetic, outer_update(): return (global_params - 0.7 * (delta + 0.9 * moment_new), moment_new)  2.42 us
  transfers between devices with their start and end apart: 10, of which 6 were waited for; matrix products, arithmetic and copies ran while one was open for 5% of the time, Pallas kernels for 4%

profile of v8, /device:TPU:2, one launch (start us, length us, event | category | flops | bytes accessed | tf_op | source)
XLA Modules:
  0.0 106.2 jit_solution(7757336302881998409)
XLA Ops:
  0.6 4.7 %shard_map.164 = (bf16[128,4096]{1,0:T(8,128)(2,1)}, bf16[128,4224]{1,0:T(8,128)(2,1)}, bf16[128,128]{1,0:T(8,128)(2,1)}, f32[128,128]{1,0:T(8,128)}, bf16[8,128,128]{2,1,0:T(8,128)(2,1)}) custom-call(bf16[128,8192]{1,0:T(8,128)(2,1)} %bitcast.23, bf16[128,128]{1,0:T(8,128)(2,1)} %bitcast.24, bf16[128,128]{1,0:T(8,128)(2,1)} %bitcast.19, bf16[1,128]{1,0:T(2,128)(2,1)} %gain_ref.3), custom_call_target="tpu_custom_call" | custom-call | tf_op jit(solution)/shard_map/pallas_call | solution.py:243
  5.3 0.0 copy-start.1
  5.3 2.1 %collective-permute-start = (bf16[128,4224]{1,0:T(8,128)(2,1)}, bf16[128,4224]{1,0:T(8,128)(2,1)S(1)}, u32[]{:S(2)}, u32[]{:S(2)}) collective-permute-start(bf16[128,4224]{1,0:T(8,128)(2,1)} %get-tuple-element.23), channel_id=1, source_target_pairs={{0,1},{1,0},{2,3},{3,2},{4,5},{5,4},{6,7},{7,6},{8,9},{9,8},{10,11... | collective-permute-start | bytes 3244040 | tf_op jit(solution)/shard_map/ppermute | solution.py:263
  7.4 0.7 convert_bitcast_fusion
  8.2 18.2 %all-to-all-start = ((bf16[16,8,1024]{2,1,0:T(8,128)(2,1)}), bf16[16,8,1024]{2,1,0:T(8,128)(2,1)S(1)}, u32[]{:S(2)}, u32[]{:S(2)}) async-start(bf16[16,8,1024]{2,1,0:T(8,128)(2,1)} %convert_bitcast_fusion), calls=%async_computation | async-start | bytes 524288 | tf_op jit(solution)/shard_map/all_to_all | solution.py:40
  26.3 0.0 collective-permute-done.arrived_ref
  26.3 0.0 copy-done
  26.3 0.0 copy-done.1
  26.3 0.3 shard_map.165
  26.7 3.6 %collective-permute-start.1 = (bf16[2,8,128,128]{3,2,1,0:T(8,128)(2,1)S(1)}, bf16[2,8,128,128]{3,2,1,0:T(8,128)(2,1)S(1)}, u32[]{:S(2)}, u32[]{:S(2)}) collective-permute-start(bf16[2,8,128,128]{3,2,1,0:T(8,128)(2,1)S(1)} %shard_map.165), channel_id=1, source_target_pairs={{0,8},{4,12},{16,24},{20,28},{32,40},{36,44},{48,56},{52,60},{2,10... | collective-permute-start | bytes 1572872 | tf_op jit(solution)/shard_map/ppermute | solution.py:270
  30.3 7.1 %all-to-all-done = bf16[16,8,1024]{2,1,0:T(8,128)(2,1)S(1)} async-done(((bf16[16,8,1024]{2,1,0:T(8,128)(2,1)}), bf16[16,8,1024]{2,1,0:T(8,128)(2,1)S(1)}, u32[]{:S(2)}, u32[]{:S(2)}) %all-to-all-start) | async-done | bytes 262176 | tf_op jit(solution)/shard_map/all_to_all | solution.py:40
  37.4 0.7 copy-done.10
  38.1 11.6 %all-to-all-start.2 = ((bf16[8,128,128]{2,1,0:T(8,128)(2,1)}), bf16[8,128,128]{2,1,0:T(8,128)(2,1)S(1)}, u32[]{:S(2)}, u32[]{:S(2)}) async-start(bf16[8,128,128]{2,1,0:T(8,128)(2,1)} %get-tuple-element.31), calls=%async_computation.2 | async-start | bytes 524288 | tf_op jit(solution)/shard_map/all_to_all | solution.py:40
  49.7 0.0 collective-permute-done.1.first_ref
  49.7 0.3 shard_map.166
  49.9 2.5 %collective-permute-start.2 = (bf16[8,128,128]{2,1,0:T(8,128)(2,1)S(1)}, bf16[8,128,128]{2,1,0:T(8,128)(2,1)S(1)}, u32[]{:S(2)}, u32[]{:S(2)}) collective-permute-start(bf16[8,128,128]{2,1,0:T(8,128)(2,1)S(1)} %shard_map.166), channel_id=1, source_target_pairs={{0,2},{4,6},{16,18},{20,22},{32,34},{36,38},{48,50},{52,54},{2,0},... | collective-permute-start | bytes 786440 | tf_op jit(solution)/shard_map/ppermute | solution.py:274
  52.5 13.0 %all-to-all-done.2.weight_ref = bf16[8,128,128]{2,1,0:T(8,128)(2,1)S(1)} async-done(((bf16[8,128,128]{2,1,0:T(8,128)(2,1)}), bf16[8,128,128]{2,1,0:T(8,128)(2,1)S(1)}, u32[]{:S(2)}, u32[]{:S(2)}) %all-to-all-start.2) | async-done | bytes 262176 | tf_op jit(solution)/shard_map/all_to_all | solution.py:40
  65.5 2.4 %collective-permute-start.3 = (bf16[8,128,128]{2,1,0:T(8,128)(2,1)S(1)}, bf16[8,128,128]{2,1,0:T(8,128)(2,1)}, u32[]{:S(2)}, u32[]{:S(2)}) collective-permute-start(bf16[8,128,128]{2,1,0:T(8,128)(2,1)S(1)} %all-to-all-done.2.weight_ref), channel_id=1, source_target_pairs={{0,2},{4,6},{16,18},{20,22},{32,34},{36,38},{48,50},{52,54},{2,0},... | collective-permute-start | bytes 786440 | tf_op jit(solution)/shard_map/ppermute | solution.py:275
  67.9 1.0 reduce_sum.12
  68.8 0.0 collective-permute-done.2.second_ref
  68.9 0.0 copy-start.2
  68.9 0.8 broadcast_in_dim.19
  69.7 4.9 %all-to-all-start.1 = ((bf16[16,8,1024]{2,1,0:T(8,128)(2,1)}), bf16[16,8,1024]{2,1,0:T(8,128)(2,1)}, u32[]{:S(2)}, u32[]{:S(2)}) async-start(bf16[16,8,1024]{2,1,0:T(8,128)(2,1)} %broadcast_in_dim.19), calls=%async_computation.1 | async-start | bytes 524288 | tf_op jit(solution)/shard_map/all_to_all | solution.py:40
  74.6 0.0 copy-done.2
  74.6 0.2 collective-permute-done.3.x_weight_ref
  74.8 1.0 shard_map.168.weights_ref
  75.8 3.1 %collective-permute-start.4 = (bf16[2,8,128,128]{3,2,1,0:T(8,128)(2,1)S(1)}, bf16[2,8,128,128]{3,2,1,0:T(8,128)(2,1)}, u32[]{:S(2)}, u32[]{:S(2)}) collective-permute-start(bf16[2,8,128,128]{3,2,1,0:T(8,128)(2,1)S(1)} %shard_map.168.weights_ref), channel_id=1, source_target_pairs={{0,8},{4,12},{16,24},{20,28},{32,40},{36,44},{48,56},{52,60},{2,10... | collective-permute-start | bytes 1572872 | tf_op jit(solution)/shard_map/ppermute | solution.py:277
  79.5 0.0 copy-start.3
  79.5 0.9 copy-done.3
  80.5 1.0 shard_map.167
  81.5 2.6 %all-to-all-done.1 = bf16[16,8,1024]{2,1,0:T(8,128)(2,1)} async-done(((bf16[16,8,1024]{2,1,0:T(8,128)(2,1)}), bf16[16,8,1024]{2,1,0:T(8,128)(2,1)}, u32[]{:S(2)}, u32[]{:S(2)}) %all-to-all-start.1) | async-done | bytes 262176 | tf_op jit(solution)/shard_map/all_to_all | solution.py:40
  84.1 5.8 %all-to-all-start.3 = ((bf16[8,128,128]{2,1,0:T(8,128)(2,1)}), bf16[8,128,128]{2,1,0:T(8,128)(2,1)S(1)}, u32[]{:S(2)}, u32[]{:S(2)}) async-start(bf16[8,128,128]{2,1,0:T(8,128)(2,1)} %shard_map.167), calls=%async_computation.3 | async-start | bytes 524288 | tf_op jit(solution)/shard_map/all_to_all | solution.py:40
  89.9 2.4 %multiply_subtract_fusion = (f32[128,1024]{1,0:T(8,128)}, f32[128,1024]{1,0:T(8,128)}) fusion(f32[128,1024]{1,0:T(8,128)} %param.23, bf16[16,8,1024]{2,1,0:T(8,128)(2,1)} %all-to-all-done.1, f32[128,1024]{1,0:T(8,128)} %param.24), kind=kLoop, calls=%fused_computation.1 | loop fusion | flops 1179648 | bytes 2359296 | tf_op jit(solution)/shard_map/sub | solution.py:218
  92.4 0.0 copy-start.6
  92.4 0.0 copy-start.7
  92.4 0.0 copy-start.8
  92.4 0.0 copy-start.9
  92.4 0.0 collective-permute-done.4.y_weights_ref
  92.4 1.8 %shard_map.169 = (f32[128,128]{1,0:T(8,128)S(1)}, f32[128,128]{1,0:T(8,128)S(1)}) custom-call(bf16[128,4096]{1,0:T(8,128)(2,1)S(1)} %copy-done, bf16[128,4224]{1,0:T(8,128)(2,1)S(1)} %collective-permute-done.arrived_ref, bf16[2,8,128,128]{3,2,1,0:T(8,128)(2,1)S(1)} %shard_map.168.weights_ref, bf16[2,8,128,128]{3,2,1,0:T(8,128)(2,1)} %collective-permute-done.4.y_weights_ref), custom_call_target="tpu_custom_call" | custom-call | tf_op jit(solution)/shard_map/pallas_call | solution.py:290
  94.3 2.7 %collective-permute-start.5 = (f32[128,128]{1,0:T(8,128)S(1)}, f32[128,128]{1,0:T(8,128)S(1)}, u32[]{:S(2)}, u32[]{:S(2)}) collective-permute-start(f32[128,128]{1,0:T(8,128)S(1)} %get-tuple-element.33), channel_id=1, source_target_pairs={{0,1},{1,0},{2,3},{3,2},{4,5},{5,4},{6,7},{7,6},{8,9},{9,8},{10,11... | collective-permute-start | bytes 196616 | tf_op jit(solution)/shard_map/ppermute | solution.py:291
  97.0 0.8 collective-permute-done.5
  97.9 0.0 copy-done.12
  97.9 0.6 fusion
  98.5 6.8 %all-to-all-done.3.terms_ref = bf16[8,128,128]{2,1,0:T(8,128)(2,1)S(1)} async-done(((bf16[8,128,128]{2,1,0:T(8,128)(2,1)}), bf16[8,128,128]{2,1,0:T(8,128)(2,1)S(1)}, u32[]{:S(2)}, u32[]{:S(2)}) %all-to-all-start.3) | async-done | bytes 262176 | tf_op jit(solution)/shard_map/all_to_all | solution.py:40
  105.3 0.1 broadcast_in_dim.22.fixes_ref
  105.4 0.0 copy-done.4
  105.4 0.0 copy-done.6
  105.4 0.8 shard_map.170
  (14 shorter events, 0.0 us)
Async XLA Ops:
  0.6 6.8 %copy-start.11 = (f32[1,128,1024]{2,1,0:T(8,128)S(1)}, f32[1,128,1024]{2,1,0:T(8,128)}, u32[]{:S(2)}) copy-start(f32[1,128,1024]{2,1,0:T(8,128)} %param.22) | copy-start | bytes 1572868
  5.3 21.0 %copy-start = (bf16[128,4096]{1,0:T(8,128)(2,1)S(1)}, bf16[128,4096]{1,0:T(8,128)(2,1)}, u32[]{:S(2)}) copy-start(bf16[128,4096]{1,0:T(8,128)(2,1)} %get-tuple-element.30.keep_ref) | copy-start | bytes 3145732
  5.3 21.0 %copy-start.1 = (bf16[128,128]{1,0:T(8,128)(2,1)S(1)}, bf16[128,128]{1,0:T(8,128)(2,1)}, u32[]{:S(2)}) copy-start(bf16[128,128]{1,0:T(8,128)(2,1)} %get-tuple-element.24.scaled_ref) | copy-start | bytes 98308
  5.3 21.0 %collective-permute-start = (bf16[128,4224]{1,0:T(8,128)(2,1)}, bf16[128,4224]{1,0:T(8,128)(2,1)S(1)}, u32[]{:S(2)}, u32[]{:S(2)}) collective-permute-start(bf16[128,4224]{1,0:T(8,128)(2,1)} %get-tuple-element.23), channel_id=1, source_target_pairs={{0,1},{1,0},{2,3},{3,2},{4,5},{5,4},{6,7},{7,6},{8,9},{9,8},{10,11... | collective-permute-start | bytes 3244040 | tf_op jit(solution)/shard_map/ppermute | solution.py:263
  8.2 29.2 %all-to-all-start = ((bf16[16,8,1024]{2,1,0:T(8,128)(2,1)}), bf16[16,8,1024]{2,1,0:T(8,128)(2,1)S(1)}, u32[]{:S(2)}, u32[]{:S(2)}) async-start(bf16[16,8,1024]{2,1,0:T(8,128)(2,1)} %convert_bitcast_fusion), calls=%async_computation | async-start | bytes 524288 | tf_op jit(solution)/shard_map/all_to_all | solution.py:40
  26.7 23.0 %collective-permute-start.1 = (bf16[2,8,128,128]{3,2,1,0:T(8,128)(2,1)S(1)}, bf16[2,8,128,128]{3,2,1,0:T(8,128)(2,1)S(1)}, u32[]{:S(2)}, u32[]{:S(2)}) collective-permute-start(bf16[2,8,128,128]{3,2,1,0:T(8,128)(2,1)S(1)} %shard_map.165), channel_id=1, source_target_pairs={{0,8},{4,12},{16,24},{20,28},{32,40},{36,44},{48,56},{52,60},{2,10... | collective-permute-start | bytes 1572872 | tf_op jit(solution)/shard_map/ppermute | solution.py:270
  37.4 0.7 copy-start.10
  38.1 27.4 %all-to-all-start.2 = ((bf16[8,128,128]{2,1,0:T(8,128)(2,1)}), bf16[8,128,128]{2,1,0:T(8,128)(2,1)S(1)}, u32[]{:S(2)}, u32[]{:S(2)}) async-start(bf16[8,128,128]{2,1,0:T(8,128)(2,1)} %get-tuple-element.31), calls=%async_computation.2 | async-start | bytes 524288 | tf_op jit(solution)/shard_map/all_to_all | solution.py:40
  49.9 18.9 %collective-permute-start.2 = (bf16[8,128,128]{2,1,0:T(8,128)(2,1)S(1)}, bf16[8,128,128]{2,1,0:T(8,128)(2,1)S(1)}, u32[]{:S(2)}, u32[]{:S(2)}) collective-permute-start(bf16[8,128,128]{2,1,0:T(8,128)(2,1)S(1)} %shard_map.166), channel_id=1, source_target_pairs={{0,2},{4,6},{16,18},{20,22},{32,34},{36,38},{48,50},{52,54},{2,0},... | collective-permute-start | bytes 786440 | tf_op jit(solution)/shard_map/ppermute | solution.py:274
  65.5 9.4 %collective-permute-start.3 = (bf16[8,128,128]{2,1,0:T(8,128)(2,1)S(1)}, bf16[8,128,128]{2,1,0:T(8,128)(2,1)}, u32[]{:S(2)}, u32[]{:S(2)}) collective-permute-start(bf16[8,128,128]{2,1,0:T(8,128)(2,1)S(1)} %all-to-all-done.2.weight_ref), channel_id=1, source_target_pairs={{0,2},{4,6},{16,18},{20,22},{32,34},{36,38},{48,50},{52,54},{2,0},... | collective-permute-start | bytes 786440 | tf_op jit(solution)/shard_map/ppermute | solution.py:275
  68.9 5.7 %copy-start.2 = (bf16[8,128,128]{2,1,0:T(8,128)(2,1)}, bf16[8,128,128]{2,1,0:T(8,128)(2,1)S(1)}, u32[]{:S(2)}) copy-start(bf16[8,128,128]{2,1,0:T(8,128)(2,1)S(1)} %collective-permute-done.2.second_ref) | copy-start | bytes 786436
  69.7 14.4 %all-to-all-start.1 = ((bf16[16,8,1024]{2,1,0:T(8,128)(2,1)}), bf16[16,8,1024]{2,1,0:T(8,128)(2,1)}, u32[]{:S(2)}, u32[]{:S(2)}) async-start(bf16[16,8,1024]{2,1,0:T(8,128)(2,1)} %broadcast_in_dim.19), calls=%async_computation.1 | async-start | bytes 524288 | tf_op jit(solution)/shard_map/all_to_all | solution.py:40
  75.8 16.6 %collective-permute-start.4 = (bf16[2,8,128,128]{3,2,1,0:T(8,128)(2,1)S(1)}, bf16[2,8,128,128]{3,2,1,0:T(8,128)(2,1)}, u32[]{:S(2)}, u32[]{:S(2)}) collective-permute-start(bf16[2,8,128,128]{3,2,1,0:T(8,128)(2,1)S(1)} %shard_map.168.weights_ref), channel_id=1, source_target_pairs={{0,8},{4,12},{16,24},{20,28},{32,40},{36,44},{48,56},{52,60},{2,10... | collective-permute-start | bytes 1572872 | tf_op jit(solution)/shard_map/ppermute | solution.py:277
  79.5 1.0 copy-start.3
  84.1 21.2 %all-to-all-start.3 = ((bf16[8,128,128]{2,1,0:T(8,128)(2,1)}), bf16[8,128,128]{2,1,0:T(8,128)(2,1)S(1)}, u32[]{:S(2)}, u32[]{:S(2)}) async-start(bf16[8,128,128]{2,1,0:T(8,128)(2,1)} %shard_map.167), calls=%async_computation.3 | async-start | bytes 524288 | tf_op jit(solution)/shard_map/all_to_all | solution.py:40
  92.3 4.7 %copy-start.13 = (f32[2,1]{0,1:T(1,128)S(1)}, f32[2,1]{0,1:T(1,128)}, u32[]{:S(2)}) copy-start(f32[2,1]{0,1:T(1,128)} %constant.14.clone) | copy-start | bytes 28
  92.4 5.5 %copy-start.12 = (f32[128,128]{1,0:T(8,128)S(1)}, f32[128,128]{1,0:T(8,128)}, u32[]{:S(2)}) copy-start(f32[128,128]{1,0:T(8,128)} %get-tuple-element.34) | copy-start | bytes 196612
  92.4 13.0 %copy-start.4 = (bf16[1,128,128]{2,1,0:T(8,128)(2,1)S(1)}, bf16[1,128,128]{2,1,0:T(8,128)(2,1)}, u32[]{:S(2)}) copy-start(bf16[1,128,128]{2,1,0:T(8,128)(2,1)} %param.15) | copy-start | bytes 98308
  92.4 13.0 %copy-start.5 = (f32[1,128,128]{2,1,0:T(8,128)S(1)}, f32[1,128,128]{2,1,0:T(8,128)}, u32[]{:S(2)}) copy-start(f32[1,128,128]{2,1,0:T(8,128)} %param.18) | copy-start | bytes 196612
  92.4 13.0 %copy-start.6 = (f32[1,128,128]{2,1,0:T(8,128)S(1)}, f32[1,128,128]{2,1,0:T(8,128)}, u32[]{:S(2)}) copy-start(f32[1,128,128]{2,1,0:T(8,128)} %param.19) | copy-start | bytes 196612
  92.4 13.0 %copy-start.7 = (bf16[1,128]{1,0:T(2,128)(2,1)S(1)}, bf16[1,128]{1,0:T(2,128)(2,1)}, u32[]{:S(2)}) copy-start(bf16[1,128]{1,0:T(2,128)(2,1)} %gain_ref.3) | copy-start | bytes 772
  92.4 13.0 %copy-start.8 = (f32[1,128]{1,0:T(1,128)S(1)}, f32[1,128]{1,0:T(1,128)}, u32[]{:S(2)}) copy-start(f32[1,128]{1,0:T(1,128)} %m_gain_ref.1) | copy-start | bytes 1540
  92.4 13.0 %copy-start.9 = (f32[1,128]{1,0:T(1,128)S(1)}, f32[1,128]{1,0:T(1,128)}, u32[]{:S(2)}) copy-start(f32[1,128]{1,0:T(1,128)} %v_gain_ref.1) | copy-start | bytes 1540
  94.3 3.6 %collective-permute-start.5 = (f32[128,128]{1,0:T(8,128)S(1)}, f32[128,128]{1,0:T(8,128)S(1)}, u32[]{:S(2)}, u32[]{:S(2)}) collective-permute-start(f32[128,128]{1,0:T(8,128)S(1)} %get-tuple-element.33), channel_id=1, source_target_pairs={{0,1},{1,0},{2,3},{3,2},{4,5},{5,4},{6,7},{7,6},{8,9},{9,8},{10,11... | collective-permute-start | bytes 196616 | tf_op jit(solution)/shard_map/ppermute | solution.py:291
